TPU v7x, 256 devices: a whole 4x4x8 slice. The times are simulated.
256 devices in a mesh: gz: 8 (over z_lo, core), gy: 4 (over y), gx: 8 (over z_hi, x).
Axes of the slice: x: 4, y: 4, z: 8 (z_hi: 2, z_lo: 4; z = z_hi * 4 + z_lo), core: 2. Of those that a mesh axis runs over, the one named last changes fastest.
Arguments:
- embedding: bfloat16 [32, 32, 256, 1024], P(None, 'gz', 'gy', 'gx'), may hold values from -18 to 18
- face_slot: int32 [32, 256, 1024], P('gz', 'gy', 'gx'), may hold values from 0 to 511
- face_edge: int32 [32768], P(('gz', 'gy', 'gx')), may hold values from 0 to 16383, as said below
- conv1_w: bfloat16 [3, 3, 3, 64, 32], replicated, may hold values from -0.21875 to 0.21875
- conv1_b: float32 [64], replicated, may hold values from -3 to 3
- conv2_w: bfloat16 [3, 3, 3, 64, 64], replicated, may hold values from -0.15625 to 0.15625
- conv2_b: float32 [64], replicated, may hold values from -3 to 3
Outputs:
- context: bfloat16 [64, 16, 64, 256], P(None, 'gz', 'gy', 'gx')
- edge_emb: float32 [32, 16384], P(None, ('gz', 'gy', 'gx'))
- edge_ctx: float32 [64, 16384], P(None, ('gz', 'gy', 'gx'))
Inputs may be any that keep to these rules, and one draw needn't show every extreme that they name: A voxel whose face_slot is 128 or more lies on no contact face. `face_edge`: edge e belongs to tile e // 64 (tiles in order gz, gy, gx). The faces of a tile name only edges of the tiles in its own gz, gy row, exactly 16 faces for each tile of that row.
All inputs are finite; a program needn't handle non-finite values.
Results may differ from a plain program's by a relative error of at most 0.0046.
Values may be sent and summed in bfloat16 or wider, within the bound.
No kernel may reach another device: no remote copies, remote signals or barrier semaphores. Data moves between devices by JAX's collectives and lax.ppermute only.
A program may use at most 128 MiB of HBM per device.

v0:
```python
import jax
import jax.numpy as jnp
from jax import lax
from jax.sharding import PartitionSpec as P

EDGE_DEV = 64


def with_halo(block, sides, width):
    for axis, dim in sides:
        count = lax.axis_size(axis)
        forward = [(i, i + 1) for i in range(count - 1)]
        backward = [(target, source) for source, target in forward]
        low = lax.ppermute(
            lax.slice_in_dim(block, block.shape[dim] - width, None, axis=dim), axis, forward
        )
        high = lax.ppermute(lax.slice_in_dim(block, 0, width, axis=dim), axis, backward)
        block = jnp.concatenate([low, block, high], axis=dim)
    return block


def convolve(padded, weight, bias, depth, rows, cols):
    total = jnp.zeros((weight.shape[3], depth, rows, cols), jnp.float32)
    for dz in range(3):
        for dy in range(3):
            for dx in range(3):
                window = padded[:, dz : dz + depth, dy : dy + rows, dx : dx + cols]
                total = total + jnp.einsum(
                    "oc,czyx->ozyx", weight[dz, dy, dx], window, preferred_element_type=jnp.float32
                )
    return total + bias[:, None, None, None]


def widen(field):
    return with_halo(field, (("gz", 1), ("gy", 2), ("gx", 3)), 1)


def per_device(embedding, face_slot, face_edge, conv1_w, conv1_b, conv2_w, conv2_b):
    chans, depth, rows, cols = embedding.shape
    zc, yc, xc = (depth // 2, rows // 4, cols // 4)
    shaped = embedding.reshape(chans, zc, 2, yc, 4, xc, 4)
    pooled = jnp.mean(shaped, axis=(2, 4, 6), dtype=jnp.float32).astype(jnp.bfloat16)
    hidden1 = jax.nn.relu(convolve(widen(pooled), conv1_w, conv1_b, zc, yc, xc)).astype(
        jnp.bfloat16
    )
    context = convolve(widen(hidden1), conv2_w, conv2_b, zc, yc, xc).astype(jnp.bfloat16)
    cells = depth * rows * cols
    nfaces = face_edge.shape[0]
    slots = face_slot.reshape(cells)
    member = (slots[None, :] == jnp.arange(nfaces, dtype=jnp.int32)[:, None]).astype(jnp.bfloat16)
    fine_ctx = jnp.repeat(jnp.repeat(jnp.repeat(context, 2, axis=1), 4, axis=2), 4, axis=3).reshape(
        context.shape[0], cells
    )
    dims = (((1,), (1,)), ((), ()))
    face_emb = lax.dot_general(
        embedding.reshape(chans, cells), member, dims, preferred_element_type=jnp.float32
    )
    face_ctx = lax.dot_general(fine_ctx, member, dims, preferred_element_type=jnp.float32)
    face_cnt = jnp.dot(
        member, jnp.ones((cells,), jnp.bfloat16), preferred_element_type=jnp.float32
    )[None, :]
    high = lax.Precision.HIGHEST
    owner_lo = lax.axis_index(("gz", "gy", "gx")) * EDGE_DEV
    own_edges = (owner_lo + jnp.arange(EDGE_DEV, dtype=jnp.int32)).astype(jnp.float32)
    labels = face_edge.astype(jnp.float32)[None, :]
    hits = (
        lax.all_gather(labels, "gx", axis=1, tiled=True)[0][:, None] == own_edges[None, :]
    ).astype(jnp.float32)
    sum_emb = jnp.dot(lax.all_gather(face_emb, "gx", axis=1, tiled=True), hits, precision=high)
    sum_ctx = jnp.dot(lax.all_gather(face_ctx, "gx", axis=1, tiled=True), hits, precision=high)
    sum_cnt = jnp.dot(lax.all_gather(face_cnt, "gx", axis=1, tiled=True), hits, precision=high)
    divisor = jnp.maximum(sum_cnt, 1.0)
    return (context, sum_emb / divisor, sum_ctx / divisor)


def solution(mesh):
    in_specs = (
        P(None, "gz", "gy", "gx"),
        P("gz", "gy", "gx"),
        P(("gz", "gy", "gx")),
        P(),
        P(),
        P(),
        P(),
    )
    out_specs = (
        P(None, "gz", "gy", "gx"),
        P(None, ("gz", "gy", "gx")),
        P(None, ("gz", "gy", "gx")),
    )
    return jax.shard_map(
        per_device, mesh=mesh, in_specs=in_specs, out_specs=out_specs, check_vma=False
    )
```

profile of v0, /device:TPU:70, one launch (start us, length us, event | category | flops | bytes accessed | tf_op | source)
XLA Modules:
  0.0 245.8 jit_solution(15145765117570114957)
XLA Ops:
  0.6 8.2 %copy.12 = bf16[32,4,64,128]{0,3,2,1:T(8,128)(2,1)} copy(bf16[32,4,64,128]{3,2,1,0:T(8,128)(2,1)} %param.7) | data formatting | bytes 4194304 | tf_op args[0]
  8.8 8.6 %convert_reduce_fusion = f32[32,2,16,32]{0,3,2,1:T(8,128)S(1)} fusion(bf16[32,2,2,16,4,32,4]{0,6,5,4,3,2,1:T(4,128)(2,1)} %bitcast.511), kind=kLoop, calls=%fused_computation | loop fusion | flops 2064384 | bytes 2228224 | tf_op jit(solution)/shard_map/reduce_sum | solution.py:42
  17.5 2.1 collective-permute-start
  19.6 3.6 %collective-permute-start.1 = (bf16[32,1,16,32]{0,3,2,1:T(8,128)(2,1)S(1)}, bf16[32,1,16,32]{0,3,2,1:T(8,128)(2,1)S(1)}, u32[]{:S(2)}, u32[]{:S(2)}) collective-permute-start(bf16[32,1,16,32]{0,3,2,1:T(8,128)(2,1)S(1)} %get-tuple-element.18), channel_id=1, source_target_pairs={{32,0},{64,32},{96,64},{128,96},{160,128},{192,160},{224,192},{33,... | collective-permute-start | bytes 98312 | tf_op jit(solution)/shard_map/ppermute | solution.py:17
  23.5 2.6 %fusion.66 = f32[1,1,128]{2,1,0:T(1,128)S(1)} fusion(s32[32768]{0:T(1024)S(1)} %bitcast.519, bf16[32768,1]{0,1:T(2,128)(2,1)S(1)} %fusion.280), kind=kOutput, calls=%fused_computation.92 | convolution fusion | flops 12582912 | bytes 197120 | tf_op jit(solution)/shard_map/dot_general | solution.py:59
  26.1 22.6 %all-gather.3 = f32[8,1,128]{2,1,0:T(1,128)S(1)} all-gather(f32[1,1,128]{2,1,0:T(1,128)S(1)} %fusion.66), channel_id=3, replica_groups=mesh['gz'=8,'gy'=4,'gx'=8] {'gx'}, dimensions={0}, use_global_device_ids=true | all-gather | bytes 4608 | tf_op jit(solution)/shard_map/all_gather | solution.py:71
  48.7 25.2 %all-gather.2 = f32[8,1,128]{2,1,0:T(1,128)S(1)} all-gather(f32[1,1,128]{2,1,0:T(1,128)S(1)} %convert_bitcast_fusion), channel_id=2, replica_groups=mesh['gz'=8,'gy'=4,'gx'=8] {'gx'}, dimensions={0}, use_global_device_ids=true | all-gather | bytes 4608 | tf_op jit(solution)/shard_map/all_gather | solution.py:67
  73.9 3.2 %fusion.63 = f32[32,128]{1,0:T(8,128)S(1)} fusion(bf16[4,8,256,128]{3,2,1,0:T(8,128)(2,1)S(1)} %bitcast.514, s32[32768]{0:T(1024)S(1)} %bitcast.520), kind=kOutput, calls=%fused_computation.90 | convolution fusion | flops 272629760 | bytes 2244608 | tf_op jit(solution)/shard_map/dot_general | solution.py:55
  77.1 43.8 %all_gather.12 = f32[32,1024]{1,0:T(8,128)S(1)} all-gather(f32[32,128]{1,0:T(8,128)S(1)} %fusion.63), channel_id=1, replica_groups=mesh['gz'=8,'gy'=4,'gx'=8] {'gx'}, dimensions={1}, use_global_device_ids=true | all-gather | bytes 147456 | tf_op jit(solution)/shard_map/all_gather | solution.py:69
  120.9 0.4 fusion.67
  121.3 1.0 convolution_divide_fusion.1
  122.4 3.5 %collective-permute-start.2 = (bf16[32,4,1,32]{0,3,2,1:T(8,128)(2,1)S(1)}, bf16[32,4,1,32]{0,3,2,1:T(8,128)(2,1)S(1)}, u32[]{:S(2)}, u32[]{:S(2)}) collective-permute-start(bf16[32,4,1,32]{0,3,2,1:T(8,128)(2,1)S(1)} %get-tuple-element.13), channel_id=1, source_target_pairs={{0,8},{8,16},{16,24},{1,9},{9,17},{17,25},{2,10},{10,18},{18,26},{... | collective-permute-start | bytes 24584 | tf_op jit(solution)/shard_map/ppermute | solution.py:14
  125.9 1.3 collective-permute-start.3
  127.6 4.1 %collective-permute-done.3 = bf16[32,4,1,32]{0,3,2,1:T(8,128)(2,1)S(1)} collective-permute-done((bf16[32,4,1,32]{0,3,2,1:T(8,128)(2,1)S(1)}, bf16[32,4,1,32]{0,3,2,1:T(8,128)(2,1)S(1)}, u32[]{:S(2)}, u32[]{:S(2)}) %collective-permute-start.3) | collective-permute-done | bytes 8224 | tf_op jit(solution)/shard_map/ppermute | solution.py:17
  131.8 8.0 %collective-permute-start.4 = (bf16[32,4,18,1]{0,3,2,1:T(2,128)(2,1)S(1)}, bf16[32,4,18,1]{0,3,2,1:T(2,128)(2,1)S(1)}, u32[]{:S(2)}, u32[]{:S(2)}) collective-permute-start(bf16[32,4,18,1]{0,3,2,1:T(2,128)(2,1)S(1)} %get-tuple-element.9), channel_id=1, source_target_pairs={{0,1},{1,2},{2,3},{3,4},{4,5},{5,6},{6,7},{8,9},{9,10},{10,11},{11... | collective-permute-start | bytes 13832 | tf_op jit(solution)/shard_map/ppermute | solution.py:14
  139.8 1.9 collective-permute-start.5
  142.9 8.7 %collective-permute-done.5 = bf16[32,4,18,1]{0,3,2,1:T(2,128)(2,1)S(1)} collective-permute-done((bf16[32,4,18,1]{0,3,2,1:T(2,128)(2,1)S(1)}, bf16[32,4,18,1]{0,3,2,1:T(2,128)(2,1)S(1)}, u32[]{:S(2)}, u32[]{:S(2)}) %collective-permute-start.5) | collective-permute-done | bytes 4640 | tf_op jit(solution)/shard_map/ppermute | solution.py:17
  151.6 0.4 maximum_maximum_fusion
  155.1 0.5 fusion.21
  155.6 0.2 fusion.25
  155.8 0.4 copy-done.4
  156.2 0.4 fusion.61
  156.6 1.9 collective-permute-start.6
  158.6 3.6 %collective-permute-start.7 = (bf16[64,1,16,32]{0,3,2,1:T(8,128)(2,1)S(1)}, bf16[64,1,16,32]{0,3,2,1:T(8,128)(2,1)S(1)}, u32[]{:S(2)}, u32[]{:S(2)}) collective-permute-start(bf16[64,1,16,32]{0,3,2,1:T(8,128)(2,1)S(1)} %get-tuple-element.16), channel_id=1, source_target_pairs={{32,0},{64,32},{96,64},{128,96},{160,128},{192,160},{224,192},{33,... | collective-permute-start | bytes 196616 | tf_op jit(solution)/shard_map/ppermute | solution.py:17
  162.4 0.5 collective-permute-done.6
  162.9 1.8 collective-permute-done.7
  164.7 3.5 %collective-permute-start.8 = (bf16[64,4,1,32]{0,3,2,1:T(8,128)(2,1)S(1)}, bf16[64,4,1,32]{0,3,2,1:T(8,128)(2,1)S(1)}, u32[]{:S(2)}, u32[]{:S(2)}) collective-permute-start(bf16[64,4,1,32]{0,3,2,1:T(8,128)(2,1)S(1)} %get-tuple-element.11), channel_id=1, source_target_pairs={{0,8},{8,16},{16,24},{1,9},{9,17},{17,25},{2,10},{10,18},{18,26},{... | collective-permute-start | bytes 49160 | tf_op jit(solution)/shard_map/ppermute | solution.py:14
  168.2 1.3 collective-permute-start.9
  169.5 0.2 fusion.78
  169.7 0.2 convolution_bitcast_fusion.1
  170.0 4.0 %collective-permute-done.9 = bf16[64,4,1,32]{0,3,2,1:T(8,128)(2,1)S(1)} collective-permute-done((bf16[64,4,1,32]{0,3,2,1:T(8,128)(2,1)S(1)}, bf16[64,4,1,32]{0,3,2,1:T(8,128)(2,1)S(1)}, u32[]{:S(2)}, u32[]{:S(2)}) %collective-permute-start.9) | collective-permute-done | bytes 16416 | tf_op jit(solution)/shard_map/ppermute | solution.py:17
  174.1 1.9 collective-permute-start.10
  176.0 4.1 %collective-permute-start.11 = (bf16[64,4,18,1]{0,3,2,1:T(2,128)(2,1)S(1)}, bf16[64,4,18,1]{0,3,2,1:T(2,128)(2,1)S(1)}, u32[]{:S(2)}, u32[]{:S(2)}) collective-permute-start(bf16[64,4,18,1]{0,3,2,1:T(2,128)(2,1)S(1)} %get-tuple-element.6), channel_id=1, source_target_pairs={{1,0},{2,1},{3,2},{4,3},{5,4},{6,5},{7,6},{9,8},{10,9},{11,10},{12... | collective-permute-start | bytes 27656 | tf_op jit(solution)/shard_map/ppermute | solution.py:17
  180.2 0.2 fusion.175
  180.4 0.2 fusion.168
  180.6 0.2 fusion.164
  180.9 0.2 fusion.156
  181.1 0.2 convolution_bitcast_fusion.2
  181.3 0.2 convolution_bitcast_fusion
  181.6 6.5 %collective-permute-done.11 = bf16[64,4,18,1]{0,3,2,1:T(2,128)(2,1)S(1)} collective-permute-done((bf16[64,4,18,1]{0,3,2,1:T(2,128)(2,1)S(1)}, bf16[64,4,18,1]{0,3,2,1:T(2,128)(2,1)S(1)}, u32[]{:S(2)}, u32[]{:S(2)}) %collective-permute-start.11) | collective-permute-done | bytes 9248 | tf_op jit(solution)/shard_map/ppermute | solution.py:17
  188.1 0.4 maximum_maximum_fusion.1
  188.5 0.2 fusion.101
  188.7 0.2 fusion.105
  188.9 0.2 fusion.103
  189.4 0.2 fusion.109
  189.6 0.2 fusion.95
  189.8 0.2 fusion.97
  190.3 0.2 convolution_bitcast_fusion.12
  190.5 0.2 fusion.92
  190.7 0.2 convolution_bitcast_fusion.10
  190.9 0.2 convolution_bitcast_fusion.6
  191.2 0.2 convolution_bitcast_fusion.7
  191.4 0.2 convolution_bitcast_fusion.8
  191.6 0.2 convolution_bitcast_fusion.9
  191.8 0.5 fusion.47
  192.3 0.2 fusion.51
  192.6 0.4 copy-done.5
  193.0 0.4 fusion.62
  193.5 0.3 broadcast_in_dim.26
  193.8 0.3 copy-done.1
  194.1 4.0 %broadcast_in_dim.27 = bf16[64,4,64,32,4]{0,4,3,2,1:T(4,128)(2,1)S(1)} broadcast(bf16[64,4,64,32]{0,3,2,1:T(8,128)(2,1)S(1)} %bitcast.512), dimensions={0,1,2,3} | broadcast | bytes 5242880 | tf_op jit(solution)/shard_map/broadcast_in_dim | solution.py:51
  198.1 2.6 %fusion = f32[64,128]{1,0:T(8,128)S(1)} fusion(bf16[64,32768]{0,1:T(8,128)(2,1)S(1)} %bitcast.513, s32[32768]{0:T(1024)S(1)} %bitcast.521), kind=kOutput, calls=%fused_computation.2 | convolution fusion | flops 541065216 | bytes 4358144 | tf_op jit(solution)/shard_map/dot_general | solution.py:58
  200.7 44.1 %all_gather.15 = f32[64,1024]{1,0:T(8,128)S(1)} all-gather(f32[64,128]{1,0:T(8,128)S(1)} %fusion), channel_id=1, replica_groups=mesh['gz'=8,'gy'=4,'gx'=8] {'gx'}, dimensions={1}, use_global_device_ids=true | all-gather | bytes 294912 | tf_op jit(solution)/shard_map/all_gather | solution.py:70
  244.8 1.0 convolution_divide_fusion
  (57 shorter events, 5.9 us)
Async XLA Ops:
  17.4 5.9 %copy-start.3 = (bf16[3,3,3,64,32]{3,4,2,1,0:T(8,128)(2,1)S(1)}, bf16[3,3,3,64,32]{3,4,2,1,0:T(8,128)(2,1)}, u32[]{:S(2)}) copy-start(bf16[3,3,3,64,32]{3,4,2,1,0:T(8,128)(2,1)} %param.10) | copy-start | bytes 331780
  17.4 6.1 %copy-start.6 = (s32[4,64,128]{2,1,0:T(8,128)S(1)}, s32[4,64,128]{2,1,0:T(8,128)}, u32[]{:S(2)}) copy-start(s32[4,64,128]{2,1,0:T(8,128)} %param.8) | copy-start | bytes 393220
  17.5 104.8 %collective-permute-start = (bf16[32,1,16,32]{0,3,2,1:T(8,128)(2,1)S(1)}, bf16[32,1,16,32]{0,3,2,1:T(8,128)(2,1)S(1)}, u32[]{:S(2)}, u32[]{:S(2)}) collective-permute-start(bf16[32,1,16,32]{0,3,2,1:T(8,128)(2,1)S(1)} %get-tuple-element.17), channel_id=1, source_target_pairs={{0,32},{32,64},{64,96},{96,128},{128,160},{160,192},{192,224},{1,3... | collective-permute-start | bytes 98312 | tf_op jit(solution)/shard_map/ppermute | solution.py:14
  19.6 102.8 %collective-permute-start.1 = (bf16[32,1,16,32]{0,3,2,1:T(8,128)(2,1)S(1)}, bf16[32,1,16,32]{0,3,2,1:T(8,128)(2,1)S(1)}, u32[]{:S(2)}, u32[]{:S(2)}) collective-permute-start(bf16[32,1,16,32]{0,3,2,1:T(8,128)(2,1)S(1)} %get-tuple-element.18), channel_id=1, source_target_pairs={{32,0},{64,32},{96,64},{128,96},{160,128},{192,160},{224,192},{33,... | collective-permute-start | bytes 98312 | tf_op jit(solution)/shard_map/ppermute | solution.py:17
  23.5 25.2 %copy-start.7 = (s32[128]{0:T(128)S(1)}, s32[128]{0:T(128)}, u32[]{:S(2)}) copy-start(s32[128]{0:T(128)} %param.9) | copy-start | bytes 1540
  23.5 50.4 %copy-start = (bf16[32,4,64,128]{3,2,1,0:T(8,128)(2,1)S(1)}, bf16[32,4,64,128]{3,2,1,0:T(8,128)(2,1)}, u32[]{:S(2)}) copy-start(bf16[32,4,64,128]{3,2,1,0:T(8,128)(2,1)} %param.7) | copy-start | bytes 6291460
  122.4 5.2 %collective-permute-start.2 = (bf16[32,4,1,32]{0,3,2,1:T(8,128)(2,1)S(1)}, bf16[32,4,1,32]{0,3,2,1:T(8,128)(2,1)S(1)}, u32[]{:S(2)}, u32[]{:S(2)}) collective-permute-start(bf16[32,4,1,32]{0,3,2,1:T(8,128)(2,1)S(1)} %get-tuple-element.13), channel_id=1, source_target_pairs={{0,8},{8,16},{16,24},{1,9},{9,17},{17,25},{2,10},{10,18},{18,26},{... | collective-permute-start | bytes 24584 | tf_op jit(solution)/shard_map/ppermute | solution.py:14
  125.9 5.8 %collective-permute-start.3 = (bf16[32,4,1,32]{0,3,2,1:T(8,128)(2,1)S(1)}, bf16[32,4,1,32]{0,3,2,1:T(8,128)(2,1)S(1)}, u32[]{:S(2)}, u32[]{:S(2)}) collective-permute-start(bf16[32,4,1,32]{0,3,2,1:T(8,128)(2,1)S(1)} %get-tuple-element.14), channel_id=1, source_target_pairs={{8,0},{16,8},{24,16},{9,1},{17,9},{25,17},{10,2},{18,10},{26,18},{... | collective-permute-start | bytes 24584 | tf_op jit(solution)/shard_map/ppermute | solution.py:17
  131.8 11.2 %collective-permute-start.4 = (bf16[32,4,18,1]{0,3,2,1:T(2,128)(2,1)S(1)}, bf16[32,4,18,1]{0,3,2,1:T(2,128)(2,1)S(1)}, u32[]{:S(2)}, u32[]{:S(2)}) collective-permute-start(bf16[32,4,18,1]{0,3,2,1:T(2,128)(2,1)S(1)} %get-tuple-element.9), channel_id=1, source_target_pairs={{0,1},{1,2},{2,3},{3,4},{4,5},{5,6},{6,7},{8,9},{9,10},{10,11},{11... | collective-permute-start | bytes 13832 | tf_op jit(solution)/shard_map/ppermute | solution.py:14
  139.8 11.9 %collective-permute-start.5 = (bf16[32,4,18,1]{0,3,2,1:T(2,128)(2,1)S(1)}, bf16[32,4,18,1]{0,3,2,1:T(2,128)(2,1)S(1)}, u32[]{:S(2)}, u32[]{:S(2)}) collective-permute-start(bf16[32,4,18,1]{0,3,2,1:T(2,128)(2,1)S(1)} %get-tuple-element.10), channel_id=1, source_target_pairs={{1,0},{2,1},{3,2},{4,3},{5,4},{6,5},{7,6},{9,8},{10,9},{11,10},{12... | collective-permute-start | bytes 13832 | tf_op jit(solution)/shard_map/ppermute | solution.py:17
  155.6 0.7 copy-start.4
  156.2 6.0 %copy-start.2 = (bf16[3,3,3,64,64]{4,3,2,1,0:T(8,128)(2,1)S(1)}, bf16[3,3,3,64,64]{4,3,2,1,0:T(8,128)(2,1)}, u32[]{:S(2)}) copy-start(bf16[3,3,3,64,64]{4,3,2,1,0:T(8,128)(2,1)} %param.12) | copy-start | bytes 663556
  156.6 6.3 %collective-permute-start.6 = (bf16[64,1,16,32]{0,3,2,1:T(8,128)(2,1)S(1)}, bf16[64,1,16,32]{0,3,2,1:T(8,128)(2,1)S(1)}, u32[]{:S(2)}, u32[]{:S(2)}) collective-permute-start(bf16[64,1,16,32]{0,3,2,1:T(8,128)(2,1)S(1)} %get-tuple-element.15), channel_id=1, source_target_pairs={{0,32},{32,64},{64,96},{96,128},{128,160},{160,192},{192,224},{1,3... | collective-permute-start | bytes 196616 | tf_op jit(solution)/shard_map/ppermute | solution.py:14
  158.6 6.1 %collective-permute-start.7 = (bf16[64,1,16,32]{0,3,2,1:T(8,128)(2,1)S(1)}, bf16[64,1,16,32]{0,3,2,1:T(8,128)(2,1)S(1)}, u32[]{:S(2)}, u32[]{:S(2)}) collective-permute-start(bf16[64,1,16,32]{0,3,2,1:T(8,128)(2,1)S(1)} %get-tuple-element.16), channel_id=1, source_target_pairs={{32,0},{64,32},{96,64},{128,96},{160,128},{192,160},{224,192},{33,... | collective-permute-start | bytes 196616 | tf_op jit(solution)/shard_map/ppermute | solution.py:17
  164.7 5.3 %collective-permute-start.8 = (bf16[64,4,1,32]{0,3,2,1:T(8,128)(2,1)S(1)}, bf16[64,4,1,32]{0,3,2,1:T(8,128)(2,1)S(1)}, u32[]{:S(2)}, u32[]{:S(2)}) collective-permute-start(bf16[64,4,1,32]{0,3,2,1:T(8,128)(2,1)S(1)} %get-tuple-element.11), channel_id=1, source_target_pairs={{0,8},{8,16},{16,24},{1,9},{9,17},{17,25},{2,10},{10,18},{18,26},{... | collective-permute-start | bytes 49160 | tf_op jit(solution)/shard_map/ppermute | solution.py:14
  168.2 5.8 %collective-permute-start.9 = (bf16[64,4,1,32]{0,3,2,1:T(8,128)(2,1)S(1)}, bf16[64,4,1,32]{0,3,2,1:T(8,128)(2,1)S(1)}, u32[]{:S(2)}, u32[]{:S(2)}) collective-permute-start(bf16[64,4,1,32]{0,3,2,1:T(8,128)(2,1)S(1)} %get-tuple-element.12), channel_id=1, source_target_pairs={{8,0},{16,8},{24,16},{9,1},{17,9},{25,17},{10,2},{18,10},{26,18},{... | collective-permute-start | bytes 49160 | tf_op jit(solution)/shard_map/ppermute | solution.py:17
  174.1 7.4 %collective-permute-start.10 = (bf16[64,4,18,1]{0,3,2,1:T(2,128)(2,1)S(1)}, bf16[64,4,18,1]{0,3,2,1:T(2,128)(2,1)S(1)}, u32[]{:S(2)}, u32[]{:S(2)}) collective-permute-start(bf16[64,4,18,1]{0,3,2,1:T(2,128)(2,1)S(1)} %get-tuple-element.5), channel_id=1, source_target_pairs={{0,1},{1,2},{2,3},{3,4},{4,5},{5,6},{6,7},{8,9},{9,10},{10,11},{11... | collective-permute-start | bytes 27656 | tf_op jit(solution)/shard_map/ppermute | solution.py:14
  176.0 12.0 %collective-permute-start.11 = (bf16[64,4,18,1]{0,3,2,1:T(2,128)(2,1)S(1)}, bf16[64,4,18,1]{0,3,2,1:T(2,128)(2,1)S(1)}, u32[]{:S(2)}, u32[]{:S(2)}) collective-permute-start(bf16[64,4,18,1]{0,3,2,1:T(2,128)(2,1)S(1)} %get-tuple-element.6), channel_id=1, source_target_pairs={{1,0},{2,1},{3,2},{4,3},{5,4},{6,5},{7,6},{9,8},{10,9},{11,10},{12... | collective-permute-start | bytes 27656 | tf_op jit(solution)/shard_map/ppermute | solution.py:17
  192.3 0.7 copy-start.5
  193.4 0.7 copy-start.1
where the time goes:
time: 246 us
  blocking collectives  136 us (55%)
  starting transfers between devices  36.8 us (15%)
  waiting for transfers between devices  25.6 us (10%)
  matrix products  23.1 us (9%)
  local copies, waits for them, and re-layouts  13.8 us (6%)
  other arithmetic  9.57 us (4%)
    all_gather x1, blocking collectives, per_device(): lax.all_gather(face_ctx, 'gx', axis=1, tiled=True)  44.1 us
    all_gather x1, blocking collectives, per_device(): lax.all_gather(face_emb, 'gx', axis=1, tiled=True)  43.8 us
    all_gather x1, blocking collectives, per_device(): lax.all_gather(labels, 'gx', axis=1, tiled=True)[0][:, None]  25.2 us
    ppermute x6, waiting for transfers between devices, with_halo(): lax.ppermute(lax.slice_in_dim(block, 0, width, axis=dim), axis, backward)  25.1 us
    all_gather x1, blocking collectives, per_device(): lax.all_gather(face_cnt, 'gx', axis=1, tiled=True)  22.6 us
    ppermute x6, starting transfers between devices, with_halo(): lax.ppermute(lax.slice_in_dim(block, block.shape[dim] - width, None, axis...  20.9 us
    ppermute x6, starting transfers between devices, with_halo(): lax.ppermute(lax.slice_in_dim(block, 0, width, axis=dim), axis, backward)  15.9 us
    dot_general x54, matrix products, convolve(): jnp.einsum('oc,czyx->ozyx', weight[dz, dy, dx], window, preferred_element...  12.2 us
  transfers between devices with their start and end apart: 12, of which 6 were waited for; matrix products, arithmetic and copies ran while one was open for 5% of the time, Pallas kernels for 0%

commit v1 on v0

v1 whole, which is shorter than its diff:
```python
import jax
import jax.numpy as jnp
from jax import lax
from jax.experimental import pallas as pl
from jax.experimental.pallas import tpu as pltpu
from jax.sharding import PartitionSpec as P

BF = jnp.bfloat16
F32 = jnp.float32
NT = (((1,), (1,)), ((), ()))
NN = (((1,), (0,)), ((), ()))


def dot(a, b, dims=NN):
    return lax.dot_general(a, b, dims, preferred_element_type=F32)


def iota(shape, dim):
    return lax.broadcasted_iota(jnp.int32, shape, dim)


def split3(x):
    hi = x.astype(BF)
    rest = x - hi.astype(F32)
    mid = rest.astype(BF)
    low = (rest - mid.astype(F32)).astype(BF)
    return hi, mid, low


def pool_x_matrix():
    row, col = iota((32, 128), 0), iota((32, 128), 1)
    cell = 4 * (row & 7) + (row >> 3)
    return jnp.where((col >> 2) == cell, 1.0, 0.0).astype(BF)


def pool_kernel(emb_ref, out_ref, sums):
    step = pl.program_id(0)
    row, col = iota((32, 256), 0), iota((32, 256), 1)
    cell = ((col >> 7) << 4) + ((col & 63) >> 2)
    pool_zy = jnp.where(cell == row, 1.0, 0.0).astype(BF)
    per = emb_ref.shape[0]
    for i in range(per):
        sums[step * per + i] = dot(pool_zy, emb_ref[i])

    @pl.when(step == pl.num_programs(0) - 1)
    def _():
        pool_x = pool_x_matrix()
        lane = iota((8, 128), 1)
        for block in range(8):
            rows = jnp.concatenate([sums[:, 4 * block + i, :] for i in range(4)], axis=0)
            cells = sum(dot(pool_x, part, NT) for part in split3(rows)) * (1.0 / 32.0)
            v = [cells[8 * i : 8 * i + 8] for i in range(4)]
            far = lane < 64
            a = [jnp.where(far, v[i], pltpu.roll(v[i + 2], 64, 1)) for i in range(2)]
            b = [jnp.where(far, pltpu.roll(v[i], 64, 1), v[i + 2]) for i in range(2)]
            near = (lane & 32) == 0
            done = []
            for lo, hi in (a, b):
                done.append(jnp.where(near, lo, pltpu.roll(hi, 32, 1)))
                done.append(jnp.where(near, pltpu.roll(lo, 96, 1), hi))
            out_ref[pl.ds(32 * block, 32), :] = jnp.concatenate(done, axis=0).astype(BF)


def pool(emb):
    steps = 4
    return pl.pallas_call(
        pool_kernel,
        grid=(steps,),
        in_specs=[pl.BlockSpec((32 // steps, 256, 128), lambda i: (i, 0, 0))],
        out_specs=pl.BlockSpec((256, 128), lambda i: (0, 0)),
        out_shape=jax.ShapeDtypeStruct((256, 128), BF),
        scratch_shapes=[pltpu.VMEM((32, 32, 128), F32)],
        compiler_params=pltpu.CompilerParams(vmem_limit_bytes=16 << 20),
        cost_estimate=pl.CostEstimate(flops=80_000_000, bytes_accessed=2_200_000, transcendentals=0),
        name="pool",
    )(emb)


def banded(tap, taps):
    zero = jnp.zeros_like(taps(tap, 0))
    w = [taps(tap, k) if 0 <= k < 3 else zero for k in range(-1, 4)]
    return [jnp.concatenate([w[k + 1], w[k]], axis=1) for k in range(4)]


def face_kernel(emb_ref, slot_ref, edge_ref, w1_ref, w2_ref, cnt_ref, face_ref, w1a_ref, w1b_ref, w2a_ref,
                wide, order, cells, total):
    step = pl.program_id(0)
    last = pl.num_programs(0) - 1
    i0, i1 = iota((128, 128), 0), iota((128, 128), 1)

    @pl.when(step == 0)
    def _():
        label = jnp.broadcast_to(edge_ref[...], (128, 128))
        owner = ((label >> 6) & 7).astype(F32)
        local = (label & 63).astype(F32)
        ahead = jnp.where((owner == owner.T) & (i0 < i1), 1.0, 0.0)
        place = owner[0:1, :] * 16.0 + jnp.sum(ahead, axis=0, keepdims=True)
        chosen = place == i0.astype(F32)
        face = jnp.sum(jnp.where(chosen, i1.astype(F32), 0.0), axis=1, keepdims=True)
        edge = jnp.sum(jnp.where(chosen, local, 0.0), axis=1, keepdims=True)
        order[0] = jnp.broadcast_to(face, (128, 128))
        order[1] = jnp.broadcast_to(edge, (128, 128))
        total[...] = jnp.zeros_like(total)

    wide[...] = emb_ref[...].astype(F32)
    faces = order[0].astype(BF)
    pool_x = pool_x_matrix()
    pool_x8 = jnp.concatenate([pool_x] * 8, axis=1)
    sums = jnp.zeros((32, 128), F32)
    count = jnp.zeros((8, 128), F32)
    for yc in range(16):
        voxels, member = [], []
        for q in (64 * zi + 4 * yc + yy for zi in range(2) for yy in range(4)):
            voxels.append(wide[:, q, :].astype(BF))
            row = jnp.broadcast_to(slot_ref[q : q + 1, :].astype(F32), (16, 128)).astype(BF)
            row = jnp.concatenate([row] * 8, axis=0)
            member.append(jnp.where(row == faces, jnp.ones((), BF), jnp.zeros((), BF)))
        left = jnp.concatenate([jnp.concatenate(voxels, axis=1), pool_x8], axis=0)
        out = dot(left, jnp.concatenate(member, axis=1), NT)
        sums = sums + out[:32]
        for x4 in range(4):
            part = out[32 + 8 * x4 : 40 + 8 * x4]
            cells[x4, 8 * yc : 8 * yc + 8, :] = part
            count = count + part
    total[0:32] += sums
    total[32:40] += count
    for x4 in range(4):
        cnt_ref[x4 // 2, 128 * (x4 % 2) : 128 * (x4 % 2) + 128, :] = cells[x4].T.astype(BF)

    @pl.when(step == last)
    def _():
        number = jnp.sum(total[32:40], axis=0, keepdims=True)
        stacked = jnp.concatenate(
            [jnp.zeros((64, 128), F32), total[0:32], jnp.broadcast_to(number, (32, 128))], axis=0
        )
        face_ref[...] = jnp.where(i1 == 97, order[1], stacked.T)
        for tap in range(9):
            bands = banded(tap, lambda t, k: w1_ref[3 * t + k])
            w1a_ref[pl.ds(128 * tap, 128), :] = jnp.concatenate(bands, axis=0)
            w1b_ref[pl.ds(128 * tap, 128), :] = jnp.concatenate(bands[2:] + bands[:2], axis=0)
            bands = banded(tap, lambda t, k: w2_ref[3 * t + k].astype(F32).T.astype(BF))
            w2a_ref[pl.ds(256 * tap, 256), :] = jnp.concatenate(bands, axis=0)


def faces(emb, slot, edge, w1, w2):
    whole = lambda *shape: pl.BlockSpec(shape, lambda i: (0,) * len(shape))
    return pl.pallas_call(
        face_kernel,
        grid=(2,),
        in_specs=[
            pl.BlockSpec((32, 128, 128), lambda i: (0, i, 0)),
            pl.BlockSpec((128, 128), lambda i: (i, 0)),
            whole(1, 128),
            whole(27, 32, 64),
            whole(27, 64, 64),
        ],
        out_specs=[
            pl.BlockSpec((2, 256, 128), lambda i: (i, 0, 0)),
            whole(128, 128),
            whole(1152, 128),
            whole(1152, 128),
            whole(2304, 128),
        ],
        out_shape=[
            jax.ShapeDtypeStruct((4, 256, 128), BF),
            jax.ShapeDtypeStruct((128, 128), F32),
            jax.ShapeDtypeStruct((1152, 128), BF),
            jax.ShapeDtypeStruct((1152, 128), BF),
            jax.ShapeDtypeStruct((2304, 128), BF),
        ],
        scratch_shapes=[
            pltpu.VMEM((32, 128, 128), F32),
            pltpu.VMEM((2, 128, 128), F32),
            pltpu.VMEM((4, 128, 128), F32),
            pltpu.VMEM((40, 128), F32),
        ],
        compiler_params=pltpu.CompilerParams(vmem_limit_bytes=32 << 20),
        cost_estimate=pl.CostEstimate(flops=600_000_000, bytes_accessed=4_000_000, transcendentals=0),
        name="faces",
    )(emb, slot, edge, w1, w2)


HEAD = 16
ROWS1 = 6 * 20 * 16
ROWS2 = 4 * 18 * 16


def conv_kernel(spot_ref, own_ref, za_ref, zb_ref, ya_ref, yb_ref, xl_ref, xr_ref, w1a_ref, w1b_ref, b1_ref, w2_ref,
                b2_ref, cnt_ref, face_ref, ctx_ref, send_ref, field, this, mixed, h0f, h0b, h0n, h1b, fine):
    gz, gy, gx = spot_ref[0], spot_ref[1], spot_ref[2]
    z_even, y_even = (gz & 1) == 0, (gy & 1) == 0
    widen = lambda ref, *at: ref[at].astype(F32) if at else ref[...].astype(F32)

    za, zb, own = widen(za_ref), widen(zb_ref), widen(own_ref)
    zs = (jnp.where(z_even, zb, za), own, jnp.where(z_even, za, zb))
    ya, yb = widen(ya_ref), widen(yb_ref)
    y_low, y_high = jnp.where(y_even, yb, ya), jnp.where(y_even, ya, yb)

    def by_z(parts):
        a, mid, b = parts
        return (jnp.where(z_even, b, a), mid, jnp.where(z_even, a, b))

    y_low = by_z([y_low[32 * i : 32 * i + 32] for i in range(3)])
    y_high = by_z([y_high[32 * i : 32 * i + 32] for i in range(3)])
    sides = []
    for ref in (xl_ref, xr_ref):
        whole = widen(ref)
        parts = by_z([whole[2 * i : 2 * i + 2] for i in range(3)])
        sides.append(parts)
    for part in range(3):
        for i in range(2):
            base = HEAD + (2 * part + i) * 320
            for y in range(16):
                field[pl.ds(base + 32 + 16 * y, 8), :] = zs[part][128 * i + 8 * y : 128 * i + 8 * y + 8]
            for y in range(2):
                field[pl.ds(base + 16 * y, 8), :] = y_low[part][16 * i + 8 * y : 16 * i + 8 * y + 8]
                field[pl.ds(base + 288 + 16 * y, 8), :] = y_high[part][16 * i + 8 * y : 16 * i + 8 * y + 8]
            for side, at in ((sides[0], -1), (sides[1], 8)):
                rows = side[part][i]
                a, b = rows[16:18], rows[18:20]
                low, high = jnp.where(y_even, b, a), jnp.where(y_even, a, b)
                column = jnp.concatenate([low, rows[0:16], high], axis=0)
                for y in range(20):
                    field[pl.ds(base + 16 * y + at, 1), :] = column[y : y + 1]

    lane = iota((320, 128), 1)
    for z in range(6):
        now = field[pl.ds(HEAD + 320 * z, 320), :]
        before = field[pl.ds(HEAD + 320 * z - 1, 320), :]
        this[pl.ds(320 * z, 320), :] = now.astype(BF)
        mixed[pl.ds(320 * z, 320), :] = jnp.where(lane < 64, now, before).astype(BF)

    row, lane = iota((288, 128), 0), iota((288, 128), 1)
    slot = row & 15
    keep = jnp.where((row < 16) & (gy == 0), 0.0, 1.0)
    keep = jnp.where((row >= 272) & (gy == 3), 0.0, keep)
    keep0 = jnp.where((slot == 0) & (lane < 64) & (gx == 0), 0.0, keep)
    keep0 = jnp.where((slot == 8) & (lane >= 64) & (gx == 7), 0.0, keep0)
    b1, b2 = b1_ref[...], b2_ref[...]

    def conv1(source, weights, z):
        total = None
        for t in range(0, 9, 2):
            group = range(t, min(t + 2, 9))
            at = [((z + tap // 3) * 20 + tap % 3) * 16 for tap in group]
            left = jnp.concatenate([source[pl.ds(r, 288), :] for r in at], axis=1)
            term = dot(left, weights[pl.ds(128 * t, 128 * len(at)), :])
            total = term if total is None else total + term
        return jnp.maximum(total + b1, 0.0)

    for z in range(4):
        inside = 1.0
        if z == 0:
            inside = jnp.where(gz == 0, 0.0, 1.0)
        if z == 3:
            inside = jnp.where(gz == 7, 0.0, 1.0)
        h0f[pl.ds(288 * z, 288), :] = conv1(mixed, w1b_ref, z) * (keep0 * inside)
        h1b[pl.ds(288 * z, 288), :] = (conv1(this, w1a_ref, z) * (keep * inside)).astype(BF)
    for z in range(4):
        h0b[pl.ds(288 * z, 288), :] = h0f[pl.ds(288 * z, 288), :].astype(BF)
        h0n[pl.ds(288 * z, 288), :] = h0f[pl.ds(288 * z + 1, 288), :].astype(BF)

    def conv2(first, second, z):
        total = None
        for tap in range(9):
            r = ((z + tap // 3) * 18 + tap % 3) * 16
            left = jnp.concatenate([first[pl.ds(r, 256), :], second[pl.ds(r, 256), :]], axis=1)
            term = dot(left, w2_ref[pl.ds(256 * tap, 256), :])
            total = term if total is None else total + term
        total = total.reshape(16, 16, 128)[:, :8, :].reshape(128, 128)
        return (total + b2).astype(BF)

    sums = None
    for z in range(2):
        for p, (first, second) in enumerate(((h0b, h1b), (h1b, h0n))):
            ctx = conv2(first, second, z)
            wide = ctx.astype(F32)
            fine[pl.ds(512 * z + 2 * p, 128, stride=4), :] = wide
            fine[pl.ds(512 * z + 2 * p + 1, 128, stride=4), :] = pltpu.roll(wide, 64, 1)
            term = dot(cnt_ref[2 * z + p], ctx)
            sums = term if sums is None else sums + term
    ctx_ref[...] = fine[...][:, :64].astype(BF)
    both = sums[:128] + pltpu.roll(sums[128:], 64, 1)
    send_ref[...] = jnp.where(iota((128, 128), 1) < 64, both, face_ref[...])


def convolve(spot, *arrays):
    return pl.pallas_call(
        conv_kernel,
        in_specs=[pl.BlockSpec(memory_space=pltpu.SMEM)] + [pl.BlockSpec(memory_space=pltpu.VMEM)] * len(arrays),
        out_specs=[pl.BlockSpec(memory_space=pltpu.VMEM)] * 2,
        out_shape=[jax.ShapeDtypeStruct((1024, 64), BF), jax.ShapeDtypeStruct((128, 128), F32)],
        scratch_shapes=[
            pltpu.VMEM((HEAD + ROWS1, 128), F32),
            pltpu.VMEM((ROWS1, 128), BF),
            pltpu.VMEM((ROWS1, 128), BF),
            pltpu.VMEM((ROWS2 + 16, 128), F32),
            pltpu.VMEM((ROWS2, 128), BF),
            pltpu.VMEM((ROWS2, 128), BF),
            pltpu.VMEM((ROWS2, 128), BF),
            pltpu.VMEM((1024, 128), F32),
        ],
        compiler_params=pltpu.CompilerParams(vmem_limit_bytes=32 << 20),
        cost_estimate=pl.CostEstimate(flops=1_000_000_000, bytes_accessed=3_000_000, transcendentals=0),
        name="convolve",
    )(spot, *arrays)


def edge_kernel(rows_ref, emb_ref, ctx_ref):
    rows = rows_ref[...]
    hits = jnp.where(rows[:, 97:98] == iota((128, 64), 1).astype(F32), 1.0, 0.0).astype(BF)
    sums = sum(dot(part, hits) for part in split3(rows.T))
    scale = jnp.maximum(sums[96:97], 1.0)
    ctx_ref[...] = sums[:64] / scale
    emb_ref[...] = sums[64:96] / scale


def edges(rows):
    return pl.pallas_call(
        edge_kernel,
        out_shape=[jax.ShapeDtypeStruct((32, 64), F32), jax.ShapeDtypeStruct((64, 64), F32)],
        name="edges",
    )(rows)


def pairs(first, count):
    return [pair for i in range(first, count - 1, 2) for pair in ((i, i + 1), (i + 1, i))]


def per_device(embedding, face_slot, face_edge, conv1_w, conv1_b, conv2_w, conv2_b):
    emb = embedding.reshape(32, 256, 128)
    gz, gy, gx = (lax.axis_index(a) for a in ("gz", "gy", "gx"))
    own = pool(emb)
    za = lax.ppermute(own, "gz", pairs(0, 8))
    zb = lax.ppermute(own, "gz", pairs(1, 8))
    cnt, face, w1a, w1b, w2a = faces(
        emb,
        face_slot.reshape(256, 128),
        face_edge.reshape(1, 128),
        jnp.swapaxes(conv1_w, 3, 4).reshape(27, 32, 64),
        conv2_w.reshape(27, 64, 64),
    )
    planes = [a.reshape(2, 16, 8, 128) for a in (za, own, zb)]
    y_even = (gy & 1) == 0

    def y_edge(high):
        first = jnp.where(high, 14, 0)
        return jnp.concatenate([lax.dynamic_slice_in_dim(a, first, 2, axis=1) for a in planes], axis=0)

    ya = lax.ppermute(y_edge(y_even), "gy", pairs(0, 4))
    yb = lax.ppermute(y_edge(jnp.logical_not(y_even)), "gy", pairs(1, 4))

    def x_edge(g):
        mid = jnp.concatenate([a[:, :, g] for a in planes], axis=0)
        return jnp.concatenate([mid, ya[:, :, g], yb[:, :, g]], axis=1)

    right = [(i, i + 1) for i in range(7)]
    xl = lax.ppermute(x_edge(7), "gx", right)
    xr = lax.ppermute(x_edge(0), "gx", [(b, a) for a, b in right])
    spot = jnp.stack([gz, gy, gx]).astype(jnp.int32)
    twice = lambda b: jnp.concatenate([b, b]).reshape(1, 128)
    context, send = convolve(
        spot, own, za, zb, ya.reshape(96, 128), yb.reshape(96, 128), xl, xr, w1a, w1b, twice(conv1_b), w2a,
        twice(conv2_b), cnt, face,
    )
    rows = lax.all_to_all(send, "gx", 0, 0, tiled=True)
    edge_emb, edge_ctx = edges(rows)
    context = jnp.transpose(context.reshape(2, 16, 32, 64), (3, 0, 1, 2))
    return (context, edge_emb, edge_ctx)


def solution(mesh):
    in_specs = (P(None, "gz", "gy", "gx"), P("gz", "gy", "gx"), P(("gz", "gy", "gx")), P(), P(), P(), P())
    out_specs = (P(None, "gz", "gy", "gx"), P(None, ("gz", "gy", "gx")), P(None, ("gz", "gy", "gx")))
    return jax.shard_map(per_device, mesh=mesh, in_specs=in_specs, out_specs=out_specs, check_vma=False)
```

time: 246 us -> 60.6 us (0.25)
  the two profiles are of different devices: /device:TPU:70 before, /device:TPU:40 now
where the time goes in v1:
time: 60.6 us; the launch traced here: 60.3 us
  blocking collectives  24.9 us (41%)
  Pallas kernels  15 us (25%)
  starting transfers between devices  12.3 us (20%)
  waiting for transfers between devices  5.11 us (8%)
  local copies, waits for them, and re-layouts  1.82 us (3%)
  between operations  0.95 us (2%)
    all_to_all x1, blocking collectives, per_device(): rows = lax.all_to_all(send, 'gx', 0, 0, tiled=True)  24.9 us
    pallas_call x1, Pallas kernels, faces(): pl.pallas_call(face_kernel, grid=(2,), in_specs=[pl.BlockSpec((32, 128, 1...  7.16 us
    pallas_call x1, Pallas kernels, convolve(): pl.pallas_call(conv_kernel, in_specs=[pl.BlockSpec(memory_space=pltpu.SME...  4.51 us
    ppermute x1, starting transfers between devices, per_device(): yb = lax.ppermute(y_edge(jnp.logical_not(y_even)), 'gy', pairs(1, 4))  3.49 us
    ppermute x1, starting transfers between devices, per_device(): xl = lax.ppermute(x_edge(7), 'gx', right)  3.4 us
    ppermute x1, starting transfers between devices, per_device(): za = lax.ppermute(own, 'gz', pairs(0, 8))  2.11 us
    ppermute x1, waiting for transfers between devices, per_device(): yb = lax.ppermute(y_edge(jnp.logical_not(y_even)), 'gy', pairs(1, 4))  2.03 us
    ppermute x1, starting transfers between devices, per_device(): zb = lax.ppermute(own, 'gz', pairs(1, 8))  1.91 us
  transfers between devices with their start and end apart: 6, of which 3 were waited for; matrix products, arithmetic and copies ran while one was open for 1% of the time, Pallas kernels for 12%

profile of v1, /device:TPU:40, one launch (start us, length us, event | category | flops | bytes accessed | tf_op | source)
XLA Modules:
  0.0 60.3 jit_solution(12516235162203168631)
XLA Ops:
  0.6 0.0 copy-start.7
  0.6 0.0 copy-start.6
  0.7 0.0 copy-start.5
  0.7 0.0 copy-start
  0.7 1.6 %copy-done = bf16[32,4,64,128]{3,2,1,0:T(8,128)(2,1)S(1)} copy-done((bf16[32,4,64,128]{3,2,1,0:T(8,128)(2,1)S(1)}, bf16[32,4,64,128]{3,2,1,0:T(8,128)(2,1)}, u32[]{:S(2)}) %copy-start) | copy-done | bytes 2097176
  2.3 0.0 copy-start.1
  2.3 0.0 copy-start.2
  2.3 0.0 copy-start.3
  2.3 0.0 copy-start.4
  2.3 1.6 %pool.1.own_ref = bf16[256,128]{1,0:T(8,128)(2,1)S(1)} custom-call(bf16[32,256,128]{2,1,0:T(8,128)(2,1)S(1)} %bitcast.46), custom_call_target="tpu_custom_call" | custom-call | flops 80000000 | bytes 2200000 | tf_op jit(solution)/shard_map/pool/pallas_call | solution.py:66
  3.9 1.9 %collective-permute-start.1 = (bf16[256,128]{1,0:T(8,128)(2,1)S(1)}, bf16[256,128]{1,0:T(8,128)(2,1)S(1)}, u32[]{:S(2)}, u32[]{:S(2)}) collective-permute-start(bf16[256,128]{1,0:T(8,128)(2,1)S(1)} %pool.1.own_ref), channel_id=1, source_target_pairs={{32,64},{64,32},{96,128},{128,96},{160,192},{192,160},{33,65},{65,... | collective-permute-start | bytes 196616 | tf_op jit(solution)/shard_map/ppermute | solution.py:335
  5.8 2.1 %collective-permute-start = (bf16[256,128]{1,0:T(8,128)(2,1)S(1)}, bf16[256,128]{1,0:T(8,128)(2,1)S(1)}, u32[]{:S(2)}, u32[]{:S(2)}) collective-permute-start(bf16[256,128]{1,0:T(8,128)(2,1)S(1)} %pool.1.own_ref), channel_id=1, source_target_pairs={{0,32},{32,0},{64,96},{96,64},{128,160},{160,128},{192,224},{224,1... | collective-permute-start | bytes 196616 | tf_op jit(solution)/shard_map/ppermute | solution.py:334
  8.0 0.0 copy-done.7
  8.0 0.0 copy-done.6
  8.0 0.1 maximum_bitcast_fusion
  8.1 0.1 pad_add_fusion.spot_ref
  8.1 1.3 %collective-permute-done.1.zb_ref = bf16[256,128]{1,0:T(8,128)(2,1)S(1)} collective-permute-done((bf16[256,128]{1,0:T(8,128)(2,1)S(1)}, bf16[256,128]{1,0:T(8,128)(2,1)S(1)}, u32[]{:S(2)}, u32[]{:S(2)}) %collective-permute-start.1) | collective-permute-done | bytes 65568 | tf_op jit(solution)/shard_map/ppermute | solution.py:335
  9.5 0.0 collective-permute-done.za_ref
  9.6 3.5 %collective-permute-start.3 = (bf16[6,2,8,128]{3,1,0,2:T(2,128)(2,1)S(1)}, bf16[6,2,8,128]{3,1,0,2:T(2,128)(2,1)S(1)}, u32[]{:S(2)}, u32[]{:S(2)}) collective-permute-start(bf16[6,2,8,128]{3,1,0,2:T(2,128)(2,1)S(1)} %pad_maximum_fusion.3), channel_id=1, source_target_pairs={{8,16},{16,8},{9,17},{17,9},{10,18},{18,10},{11,19},{19,11},{12,20... | collective-permute-start | bytes 73736 | tf_op jit(solution)/shard_map/ppermute | solution.py:351
  13.2 0.1 collective-permute-start.2
  13.3 2.0 %collective-permute-done.3 = bf16[6,2,8,128]{3,1,0,2:T(2,128)(2,1)S(1)} collective-permute-done((bf16[6,2,8,128]{3,1,0,2:T(2,128)(2,1)S(1)}, bf16[6,2,8,128]{3,1,0,2:T(2,128)(2,1)S(1)}, u32[]{:S(2)}, u32[]{:S(2)}) %collective-permute-start.3) | collective-permute-done | bytes 24608 | tf_op jit(solution)/shard_map/ppermute | solution.py:351
  15.4 1.8 %collective-permute-done.2 = bf16[6,2,8,128]{3,1,0,2:T(2,128)(2,1)S(1)} collective-permute-done((bf16[6,2,8,128]{3,1,0,2:T(2,128)(2,1)S(1)}, bf16[6,2,8,128]{3,1,0,2:T(2,128)(2,1)S(1)}, u32[]{:S(2)}, u32[]{:S(2)}) %collective-permute-start.2) | collective-permute-done | bytes 24608 | tf_op jit(solution)/shard_map/ppermute | solution.py:350
  17.2 3.4 %collective-permute-start.4 = (bf16[6,20,128]{2,1,0:T(8,128)(2,1)S(1)}, bf16[6,20,128]{2,1,0:T(8,128)(2,1)S(1)}, u32[]{:S(2)}, u32[]{:S(2)}) collective-permute-start(bf16[6,20,128]{2,1,0:T(8,128)(2,1)S(1)} %pad_maximum_fusion), channel_id=1, source_target_pairs={{0,1},{1,2},{2,3},{3,4},{4,5},{5,6},{6,7},{8,9},{9,10},{10,11},{11... | collective-permute-start | bytes 92168 | tf_op jit(solution)/shard_map/ppermute | solution.py:358
  20.6 1.3 %collective-permute-start.5 = (bf16[6,20,128]{2,1,0:T(8,128)(2,1)S(1)}, bf16[6,20,128]{2,1,0:T(8,128)(2,1)S(1)}, u32[]{:S(2)}, u32[]{:S(2)}) collective-permute-start(bf16[6,20,128]{2,1,0:T(8,128)(2,1)S(1)} %pad_maximum_fusion.1), channel_id=1, source_target_pairs={{1,0},{2,1},{3,2},{4,3},{5,4},{6,5},{7,6},{9,8},{10,9},{11,10},{12... | collective-permute-start | bytes 92168 | tf_op jit(solution)/shard_map/ppermute | solution.py:359
  21.9 0.0 copy-done.5
  21.9 0.0 copy-done.1
  21.9 0.0 copy-done.2
  21.9 0.0 copy-done.3
  21.9 0.0 copy-done.4
  22.0 7.2 %faces.1 = (bf16[4,256,128]{2,1,0:T(8,128)(2,1)S(1)}, f32[128,128]{1,0:T(8,128)S(1)}, bf16[1152,128]{1,0:T(8,128)(2,1)S(1)}, bf16[1152,128]{1,0:T(8,128)(2,1)S(1)}, bf16[2304,128]{1,0:T(8,128)(2,1)S(1)}) custom-call(bf16[32,256,128]{2,1,0:T(8,128)(2,1)S(1)} %bitcast.47, s32[256,128]{1,0:T(8,128)S(1)} %bitcast.52, s32[1,128]{1,0:T(1,128)S(1)} %bitcast.60, ...), custom_call_target="tpu_custom_call" | custom-call | flops 600000000 | bytes 4000000 | tf_op jit(solution)/shard_map/faces/pallas_call | solution.py:147
  29.1 0.0 collective-permute-done.4.xl_ref
  29.2 0.0 collective-permute-done.5.xr_ref
  29.2 4.5 %convolve.1 = (bf16[1024,64]{1,0:T(8,128)(2,1)}, f32[128,128]{1,0:T(8,128)S(1)}) custom-call(s32[3]{0:T(128)S(1)} %pad_add_fusion.spot_ref, bf16[256,128]{1,0:T(8,128)(2,1)S(1)} %pool.1.own_ref, bf16[256,128]{1,0:T(8,128)(2,1)S(1)} %collective-permute-done.za_ref, bf16[256,128]{1,0:T(8,128)(2,1)S(1)} %collective-permute-done.1.zb_ref, ...), custom_call_target="tpu_custom_call" | custom-call | flops 1000000000 | bytes 3000000 | tf_op jit(solution)/shard_map/convolve/pallas_call | solution.py:288
  33.7 24.9 %all_to_all.11 = f32[8,16,128]{2,1,0:T(8,128)} all-to-all(f32[8,16,128]{2,1,0:T(8,128)S(1)} %bitcast.53), channel_id=1, replica_groups=mesh['gz'=8,'gy'=4,'gx'=8] {'gx'}, dimensions={0} | all-to-all | bytes 131072 | tf_op jit(solution)/shard_map/all_to_all | solution.py:366
  58.6 1.7 %edges.1 = (f32[32,64]{1,0:T(8,128)}, f32[64,64]{1,0:T(8,128)}) custom-call(f32[128,128]{1,0:T(8,128)} %bitcast.61), custom_call_target="tpu_custom_call" | custom-call | tf_op jit(solution)/shard_map/edges/pallas_call | solution.py:319
  (23 shorter events, 0.3 us)
Async XLA Ops:
  0.6 7.3 %copy-start.7 = (f32[64]{0:T(128)S(1)}, f32[64]{0:T(128)}, u32[]{:S(2)}) copy-start(f32[64]{0:T(128)} %param.13) | copy-start | bytes 772
  0.6 7.3 %copy-start.6 = (f32[64]{0:T(128)S(1)}, f32[64]{0:T(128)}, u32[]{:S(2)}) copy-start(f32[64]{0:T(128)} %param.11) | copy-start | bytes 772
  0.7 21.3 %copy-start.5 = (s32[128]{0:T(128)S(1)}, s32[128]{0:T(128)}, u32[]{:S(2)}) copy-start(s32[128]{0:T(128)} %param.9) | copy-start | bytes 1540
  0.7 1.6 %copy-start = (bf16[32,4,64,128]{3,2,1,0:T(8,128)(2,1)S(1)}, bf16[32,4,64,128]{3,2,1,0:T(8,128)(2,1)}, u32[]{:S(2)}) copy-start(bf16[32,4,64,128]{3,2,1,0:T(8,128)(2,1)} %param.7) | copy-start | bytes 6291460
  2.3 19.6 %copy-start.1 = (bf16[32,4,64,128]{3,2,1,0:T(8,128)(2,1)S(1)}, bf16[32,4,64,128]{3,2,1,0:T(8,128)(2,1)}, u32[]{:S(2)}) copy-start(bf16[32,4,64,128]{3,2,1,0:T(8,128)(2,1)} %param.7) | copy-start | bytes 6291460
  2.3 19.6 %copy-start.2 = (bf16[3,3,3,64,64]{4,3,2,1,0:T(8,128)(2,1)S(1)}, bf16[3,3,3,64,64]{4,3,2,1,0:T(8,128)(2,1)}, u32[]{:S(2)}) copy-start(bf16[3,3,3,64,64]{4,3,2,1,0:T(8,128)(2,1)} %param.12) | copy-start | bytes 663556
  2.3 19.7 %copy-start.3 = (bf16[3,3,3,64,32]{3,4,2,1,0:T(8,128)(2,1)S(1)}, bf16[3,3,3,64,32]{3,4,2,1,0:T(8,128)(2,1)}, u32[]{:S(2)}) copy-start(bf16[3,3,3,64,32]{3,4,2,1,0:T(8,128)(2,1)} %param.10) | copy-start | bytes 331780
  2.3 19.7 %copy-start.4 = (s32[4,64,128]{2,1,0:T(8,128)S(1)}, s32[4,64,128]{2,1,0:T(8,128)}, u32[]{:S(2)}) copy-start(s32[4,64,128]{2,1,0:T(8,128)} %param.8) | copy-start | bytes 393220
  3.9 5.6 %collective-permute-start.1 = (bf16[256,128]{1,0:T(8,128)(2,1)S(1)}, bf16[256,128]{1,0:T(8,128)(2,1)S(1)}, u32[]{:S(2)}, u32[]{:S(2)}) collective-permute-start(bf16[256,128]{1,0:T(8,128)(2,1)S(1)} %pool.1.own_ref), channel_id=1, source_target_pairs={{32,64},{64,32},{96,128},{128,96},{160,192},{192,160},{33,65},{65,... | collective-permute-start | bytes 196616 | tf_op jit(solution)/shard_map/ppermute | solution.py:335
  5.8 3.7 %collective-permute-start = (bf16[256,128]{1,0:T(8,128)(2,1)S(1)}, bf16[256,128]{1,0:T(8,128)(2,1)S(1)}, u32[]{:S(2)}, u32[]{:S(2)}) collective-permute-start(bf16[256,128]{1,0:T(8,128)(2,1)S(1)} %pool.1.own_ref), channel_id=1, source_target_pairs={{0,32},{32,0},{64,96},{96,64},{128,160},{160,128},{192,224},{224,1... | collective-permute-start | bytes 196616 | tf_op jit(solution)/shard_map/ppermute | solution.py:334
  9.6 5.7 %collective-permute-start.3 = (bf16[6,2,8,128]{3,1,0,2:T(2,128)(2,1)S(1)}, bf16[6,2,8,128]{3,1,0,2:T(2,128)(2,1)S(1)}, u32[]{:S(2)}, u32[]{:S(2)}) collective-permute-start(bf16[6,2,8,128]{3,1,0,2:T(2,128)(2,1)S(1)} %pad_maximum_fusion.3), channel_id=1, source_target_pairs={{8,16},{16,8},{9,17},{17,9},{10,18},{18,10},{11,19},{19,11},{12,20... | collective-permute-start | bytes 73736 | tf_op jit(solution)/shard_map/ppermute | solution.py:351
  13.2 3.9 %collective-permute-start.2 = (bf16[6,2,8,128]{3,1,0,2:T(2,128)(2,1)S(1)}, bf16[6,2,8,128]{3,1,0,2:T(2,128)(2,1)S(1)}, u32[]{:S(2)}, u32[]{:S(2)}) collective-permute-start(bf16[6,2,8,128]{3,1,0,2:T(2,128)(2,1)S(1)} %pad_maximum_fusion.2), channel_id=1, source_target_pairs={{0,8},{8,0},{16,24},{24,16},{1,9},{9,1},{17,25},{25,17},{2,10},{10... | collective-permute-start | bytes 73736 | tf_op jit(solution)/shard_map/ppermute | solution.py:350
  17.2 12.0 %collective-permute-start.4 = (bf16[6,20,128]{2,1,0:T(8,128)(2,1)S(1)}, bf16[6,20,128]{2,1,0:T(8,128)(2,1)S(1)}, u32[]{:S(2)}, u32[]{:S(2)}) collective-permute-start(bf16[6,20,128]{2,1,0:T(8,128)(2,1)S(1)} %pad_maximum_fusion), channel_id=1, source_target_pairs={{0,1},{1,2},{2,3},{3,4},{4,5},{5,6},{6,7},{8,9},{9,10},{10,11},{11... | collective-permute-start | bytes 92168 | tf_op jit(solution)/shard_map/ppermute | solution.py:358
  20.6 8.6 %collective-permute-start.5 = (bf16[6,20,128]{2,1,0:T(8,128)(2,1)S(1)}, bf16[6,20,128]{2,1,0:T(8,128)(2,1)S(1)}, u32[]{:S(2)}, u32[]{:S(2)}) collective-permute-start(bf16[6,20,128]{2,1,0:T(8,128)(2,1)S(1)} %pad_maximum_fusion.1), channel_id=1, source_target_pairs={{1,0},{2,1},{3,2},{4,3},{5,4},{6,5},{7,6},{9,8},{10,9},{11,10},{12... | collective-permute-start | bytes 92168 | tf_op jit(solution)/shard_map/ppermute | solution.py:359

commit v2 on v1

--- a/solution.py
+++ b/solution.py
@@ -33,47 +33,54 @@
     return jnp.where((col >> 2) == cell, 1.0, 0.0).astype(BF)
 
 
-def pool_kernel(emb_ref, out_ref, sums):
-    step = pl.program_id(0)
+def pool_kernel(emb_ref, out_ref, block, sums, arrived):
+    chunks = arrived.shape[0]
+    per = 32 // chunks
+    copies = [
+        pltpu.make_async_copy(emb_ref.at[pl.ds(per * i, per)], block.at[pl.ds(per * i, per)], arrived.at[i])
+        for i in range(chunks)
+    ]
+    for copy in copies:
+        copy.start()
     row, col = iota((32, 256), 0), iota((32, 256), 1)
     cell = ((col >> 7) << 4) + ((col & 63) >> 2)
     pool_zy = jnp.where(cell == row, 1.0, 0.0).astype(BF)
-    per = emb_ref.shape[0]
-    for i in range(per):
-        sums[step * per + i] = dot(pool_zy, emb_ref[i])
-
-    @pl.when(step == pl.num_programs(0) - 1)
-    def _():
-        pool_x = pool_x_matrix()
-        lane = iota((8, 128), 1)
-        for block in range(8):
-            rows = jnp.concatenate([sums[:, 4 * block + i, :] for i in range(4)], axis=0)
-            cells = sum(dot(pool_x, part, NT) for part in split3(rows)) * (1.0 / 32.0)
-            v = [cells[8 * i : 8 * i + 8] for i in range(4)]
-            far = lane < 64
-            a = [jnp.where(far, v[i], pltpu.roll(v[i + 2], 64, 1)) for i in range(2)]
-            b = [jnp.where(far, pltpu.roll(v[i], 64, 1), v[i + 2]) for i in range(2)]
-            near = (lane & 32) == 0
-            done = []
-            for lo, hi in (a, b):
-                done.append(jnp.where(near, lo, pltpu.roll(hi, 32, 1)))
-                done.append(jnp.where(near, pltpu.roll(lo, 96, 1), hi))
-            out_ref[pl.ds(32 * block, 32), :] = jnp.concatenate(done, axis=0).astype(BF)
+    pool_x = pool_x_matrix()
+    lane = iota((8, 128), 1)
+    far, near = lane < 64, (lane & 32) == 0
+    for i in range(chunks):
+        copies[i].wait()
+        for c in range(per * i, per * i + per):
+            sums[c] = dot(pool_zy, block[c])
+    for part in range(8):
+        rows = jnp.concatenate([sums[:, 4 * part + i, :] for i in range(4)], axis=0)
+        cells = sum(dot(pool_x, term, NT) for term in split3(rows)) * (1.0 / 32.0)
+        v = [cells[8 * i : 8 * i + 8] for i in range(4)]
+        a = [jnp.where(far, v[i], pltpu.roll(v[i + 2], 64, 1)) for i in range(2)]
+        b = [jnp.where(far, pltpu.roll(v[i], 64, 1), v[i + 2]) for i in range(2)]
+        done = []
+        for lo, hi in (a, b):
+            done.append(jnp.where(near, lo, pltpu.roll(hi, 32, 1)))
+            done.append(jnp.where(near, pltpu.roll(lo, 96, 1), hi))
+        out_ref[pl.ds(32 * part, 32), :] = jnp.concatenate(done, axis=0).astype(BF)
 
 
 def pool(emb):
-    steps = 4
+    chunks = 2
     return pl.pallas_call(
         pool_kernel,
-        grid=(steps,),
-        in_specs=[pl.BlockSpec((32 // steps, 256, 128), lambda i: (i, 0, 0))],
-        out_specs=pl.BlockSpec((256, 128), lambda i: (0, 0)),
-        out_shape=jax.ShapeDtypeStruct((256, 128), BF),
-        scratch_shapes=[pltpu.VMEM((32, 32, 128), F32)],
-        compiler_params=pltpu.CompilerParams(vmem_limit_bytes=16 << 20),
+        in_specs=[pl.BlockSpec(memory_space=pl.ANY)],
+        out_specs=pl.BlockSpec(memory_space=pltpu.VMEM),
+        out_shape=pltpu.VMEM((256, 128), BF),
+        scratch_shapes=[
+            pltpu.VMEM((32, 256, 128), BF),
+            pltpu.VMEM((32, 32, 128), F32),
+            pltpu.SemaphoreType.DMA((chunks,)),
+        ],
+        compiler_params=pltpu.CompilerParams(vmem_limit_bytes=32 << 20),
         cost_estimate=pl.CostEstimate(flops=80_000_000, bytes_accessed=2_200_000, transcendentals=0),
         name="pool",
-    )(emb)
+    )(pltpu.with_memory_space_constraint(emb, pltpu.HBM))
 
 
 def banded(tap, taps):
@@ -83,13 +90,18 @@
 
 
 def face_kernel(emb_ref, slot_ref, edge_ref, w1_ref, w2_ref, cnt_ref, face_ref, w1a_ref, w1b_ref, w2a_ref,
-                wide, order, cells, total):
+                block, wide, order, cells, total, arrived):
     step = pl.program_id(0)
     last = pl.num_programs(0) - 1
+    copies = [
+        pltpu.make_async_copy(emb_ref.at[:, pl.ds(128 * i, 128), :], block.at[i], arrived.at[i]) for i in range(2)
+    ]
     i0, i1 = iota((128, 128), 0), iota((128, 128), 1)
 
     @pl.when(step == 0)
     def _():
+        for copy in copies:
+            copy.start()
         label = jnp.broadcast_to(edge_ref[...], (128, 128))
         owner = ((label >> 6) & 7).astype(F32)
         local = (label & 63).astype(F32)
@@ -101,9 +113,21 @@
         order[0] = jnp.broadcast_to(face, (128, 128))
         order[1] = jnp.broadcast_to(edge, (128, 128))
         total[...] = jnp.zeros_like(total)
-
-    wide[...] = emb_ref[...].astype(F32)
-    faces = order[0].astype(BF)
+        for tap in range(9):
+            bands = banded(tap, lambda t, k: w1_ref[3 * t + k])
+            w1a_ref[pl.ds(128 * tap, 128), :] = jnp.concatenate(bands, axis=0)
+            w1b_ref[pl.ds(128 * tap, 128), :] = jnp.concatenate(bands[2:] + bands[:2], axis=0)
+            bands = banded(tap, lambda t, k: w2_ref[3 * t + k].astype(F32).T.astype(BF))
+            w2a_ref[pl.ds(256 * tap, 256), :] = jnp.concatenate(bands, axis=0)
+
+    for i in range(2):
+
+        @pl.when(step == i)
+        def _():
+            copies[i].wait()
+
+    wide[...] = block[step].astype(F32).reshape(4096, 128)
+    faces = order[0].astype(jnp.int32)
     pool_x = pool_x_matrix()
     pool_x8 = jnp.concatenate([pool_x] * 8, axis=1)
     sums = jnp.zeros((32, 128), F32)
@@ -111,10 +135,9 @@
     for yc in range(16):
         voxels, member = [], []
         for q in (64 * zi + 4 * yc + yy for zi in range(2) for yy in range(4)):
-            voxels.append(wide[:, q, :].astype(BF))
-            row = jnp.broadcast_to(slot_ref[q : q + 1, :].astype(F32), (16, 128)).astype(BF)
-            row = jnp.concatenate([row] * 8, axis=0)
-            member.append(jnp.where(row == faces, jnp.ones((), BF), jnp.zeros((), BF)))
+            voxels.append(wide[pl.ds(q, 32, stride=128), :].astype(BF))
+            row = jnp.broadcast_to(slot_ref[q : q + 1, :], (128, 128))
+            member.append(jnp.where(row == faces, 1.0, 0.0).astype(BF))
         left = jnp.concatenate([jnp.concatenate(voxels, axis=1), pool_x8], axis=0)
         out = dot(left, jnp.concatenate(member, axis=1), NT)
         sums = sums + out[:32]
@@ -134,12 +157,6 @@
             [jnp.zeros((64, 128), F32), total[0:32], jnp.broadcast_to(number, (32, 128))], axis=0
         )
         face_ref[...] = jnp.where(i1 == 97, order[1], stacked.T)
-        for tap in range(9):
-            bands = banded(tap, lambda t, k: w1_ref[3 * t + k])
-            w1a_ref[pl.ds(128 * tap, 128), :] = jnp.concatenate(bands, axis=0)
-            w1b_ref[pl.ds(128 * tap, 128), :] = jnp.concatenate(bands[2:] + bands[:2], axis=0)
-            bands = banded(tap, lambda t, k: w2_ref[3 * t + k].astype(F32).T.astype(BF))
-            w2a_ref[pl.ds(256 * tap, 256), :] = jnp.concatenate(bands, axis=0)
 
 
 def faces(emb, slot, edge, w1, w2):
@@ -148,7 +165,7 @@
         face_kernel,
         grid=(2,),
         in_specs=[
-            pl.BlockSpec((32, 128, 128), lambda i: (0, i, 0)),
+            pl.BlockSpec(memory_space=pl.ANY),
             pl.BlockSpec((128, 128), lambda i: (i, 0)),
             whole(1, 128),
             whole(27, 32, 64),
@@ -169,15 +186,17 @@
             jax.ShapeDtypeStruct((2304, 128), BF),
         ],
         scratch_shapes=[
-            pltpu.VMEM((32, 128, 128), F32),
+            pltpu.VMEM((2, 32, 128, 128), BF),
+            pltpu.VMEM((4096, 128), F32),
             pltpu.VMEM((2, 128, 128), F32),
             pltpu.VMEM((4, 128, 128), F32),
             pltpu.VMEM((40, 128), F32),
+            pltpu.SemaphoreType.DMA((2,)),
         ],
         compiler_params=pltpu.CompilerParams(vmem_limit_bytes=32 << 20),
         cost_estimate=pl.CostEstimate(flops=600_000_000, bytes_accessed=4_000_000, transcendentals=0),
         name="faces",
-    )(emb, slot, edge, w1, w2)
+    )(pltpu.with_memory_space_constraint(emb, pltpu.HBM), slot, edge, w1, w2)
 
 
 HEAD = 16
@@ -185,8 +204,8 @@
 ROWS2 = 4 * 18 * 16
 
 
-def conv_kernel(spot_ref, own_ref, za_ref, zb_ref, ya_ref, yb_ref, xl_ref, xr_ref, w1a_ref, w1b_ref, b1_ref, w2_ref,
-                b2_ref, cnt_ref, face_ref, ctx_ref, send_ref, field, this, mixed, h0f, h0b, h0n, h1b, fine):
+def conv_kernel(spot_ref, own_ref, za_ref, zb_ref, ya_ref, yb_ref, xl_ref, xr_ref, far_ref, w1a_ref, w1b_ref, b1_ref,
+                w2_ref, b2_ref, cnt_ref, face_ref, ctx_ref, send_ref, field, this, mixed, h0f, h0b, h0n, h1b, fine):
     gz, gy, gx = spot_ref[0], spot_ref[1], spot_ref[2]
     z_even, y_even = (gz & 1) == 0, (gy & 1) == 0
     widen = lambda ref, *at: ref[at].astype(F32) if at else ref[...].astype(F32)
@@ -203,8 +222,9 @@
     y_low = by_z([y_low[32 * i : 32 * i + 32] for i in range(3)])
     y_high = by_z([y_high[32 * i : 32 * i + 32] for i in range(3)])
     sides = []
-    for ref in (xl_ref, xr_ref):
-        whole = widen(ref)
+    far = widen(far_ref)
+    for ref, end in ((xl_ref, 4), (xr_ref, 3)):
+        whole = jnp.where(gx == end, far, widen(ref))
         parts = by_z([whole[2 * i : 2 * i + 2] for i in range(3)])
         sides.append(parts)
     for part in range(3):
@@ -354,13 +374,15 @@
         mid = jnp.concatenate([a[:, :, g] for a in planes], axis=0)
         return jnp.concatenate([mid, ya[:, :, g], yb[:, :, g]], axis=1)
 
-    right = [(i, i + 1) for i in range(7)]
-    xl = lax.ppermute(x_edge(7), "gx", right)
-    xr = lax.ppermute(x_edge(0), "gx", [(b, a) for a, b in right])
+    low, high = x_edge(0), x_edge(7)
+    far = lax.ppermute(jnp.where(gx == 3, high, low), "gx", [(3, 4), (4, 3)])
+    right = [(i, i + 1) for i in range(7) if i != 3]
+    xl = lax.ppermute(high, "gx", right)
+    xr = lax.ppermute(low, "gx", [(b, a) for a, b in right])
     spot = jnp.stack([gz, gy, gx]).astype(jnp.int32)
     twice = lambda b: jnp.concatenate([b, b]).reshape(1, 128)
     context, send = convolve(
-        spot, own, za, zb, ya.reshape(96, 128), yb.reshape(96, 128), xl, xr, w1a, w1b, twice(conv1_b), w2a,
+        spot, own, za, zb, ya.reshape(96, 128), yb.reshape(96, 128), xl, xr, far, w1a, w1b, twice(conv1_b), w2a,
         twice(conv2_b), cnt, face,
     )
     rows = lax.all_to_all(send, "gx", 0, 0, tiled=True)

time: 60.6 us -> 56.4 us (0.931)
  blocking collectives: 24.9 us -> 22.8 us
  local copies, waits for them, and re-layouts: 1.82 us -> 0.22 us
  Pallas kernels: 15 us -> 13.7 us
  starting transfers between devices: 12.3 us -> 13 us
    all_to_all x1, blocking collectives: 24.9 us -> 22.8 us  [per_device(): rows = lax.all_to_all(send, 'gx', 0, 0, tiled=True)]
    unnamed x24 -> x20, local copies, waits for them, and re-layouts: 1.68 us -> 0.08 us
    pallas_call x2, Pallas kernels: 8.73 us -> 7.47 us  [the longest x1 4.9 us: faces(): pl.pallas_call(face_kernel, grid=(2,), in_specs=[pl.BlockSpec(memory_spac...]
    ppermute x2 -> x3, starting transfers between devices: 4.69 us -> 5.35 us  [the longest x1 3.4 us: per_device(): xl = lax.ppermute(high, 'gx', right)]
  transfers between devices with their start and end apart: 6 -> 7, of which waited for: 3 -> 3; matrix products, arithmetic and copies ran while one was open for 1% -> 1% of each run, Pallas kernels for 12% -> 9%
where the time goes in v2:
time: 56.4 us; the launch traced here: 56.1 us
  blocking collectives  22.8 us (40%)
  Pallas kernels  13.7 us (24%)
  starting transfers between devices  13 us (23%)
  waiting for transfers between devices  5.11 us (9%)
  between operations  0.98 us (2%)
    all_to_all x1, blocking collectives, per_device(): rows = lax.all_to_all(send, 'gx', 0, 0, tiled=True)  22.8 us
    pallas_call x1, Pallas kernels, faces(): pl.pallas_call(face_kernel, grid=(2,), in_specs=[pl.BlockSpec(memory_spac...  4.9 us
    pallas_call x1, Pallas kernels, convolve(): pl.pallas_call(conv_kernel, in_specs=[pl.BlockSpec(memory_space=pltpu.SME...  4.54 us
    ppermute x1, starting transfers between devices, per_device(): yb = lax.ppermute(y_edge(jnp.logical_not(y_even)), 'gy', pairs(1, 4))  3.48 us
    ppermute x1, starting transfers between devices, per_device(): xl = lax.ppermute(high, 'gx', right)  3.4 us
    pallas_call x1, Pallas kernels, pool(): pl.pallas_call(pool_kernel, in_specs=[pl.BlockSpec(memory_space=pl.ANY)],...  2.58 us
    ppermute x1, starting transfers between devices, per_device(): za = lax.ppermute(own, 'gz', pairs(0, 8))  2.11 us
    ppermute x1, waiting for transfers between devices, per_device(): yb = lax.ppermute(y_edge(jnp.logical_not(y_even)), 'gy', pairs(1, 4))  2.03 us
  transfers between devices with their start and end apart: 7, of which 3 were waited for; matrix products, arithmetic and copies ran while one was open for 1% of the time, Pallas kernels for 9%

profile of v2, /device:TPU:40, one launch (start us, length us, event | category | flops | bytes accessed | tf_op | source)
XLA Modules:
  0.0 56.1 jit_solution(1000895624596846967)
XLA Ops:
  0.6 0.0 copy-start.5
  0.6 0.0 copy-start.4
  0.7 0.0 copy-start
  0.7 0.0 copy-start.1
  0.7 0.0 copy-start.3
  0.7 0.0 copy-start.2
  0.7 2.6 %pool.1.own_ref = bf16[256,128]{1,0:T(8,128)(2,1)S(1)} custom-call(bf16[32,256,128]{2,1,0:T(8,128)(2,1)} %bitcast.59), custom_call_target="tpu_custom_call" | custom-call | flops 80000000 | bytes 2200000 | tf_op jit(solution)/shard_map/pool/pallas_call | solution.py:70
  3.3 1.9 %collective-permute-start.1 = (bf16[256,128]{1,0:T(8,128)(2,1)S(1)}, bf16[256,128]{1,0:T(8,128)(2,1)S(1)}, u32[]{:S(2)}, u32[]{:S(2)}) collective-permute-start(bf16[256,128]{1,0:T(8,128)(2,1)S(1)} %pool.1.own_ref), channel_id=1, source_target_pairs={{32,64},{64,32},{96,128},{128,96},{160,192},{192,160},{33,65},{65,... | collective-permute-start | bytes 196616 | tf_op jit(solution)/shard_map/ppermute | solution.py:355
  5.2 2.1 %collective-permute-start = (bf16[256,128]{1,0:T(8,128)(2,1)S(1)}, bf16[256,128]{1,0:T(8,128)(2,1)S(1)}, u32[]{:S(2)}, u32[]{:S(2)}) collective-permute-start(bf16[256,128]{1,0:T(8,128)(2,1)S(1)} %pool.1.own_ref), channel_id=1, source_target_pairs={{0,32},{32,0},{64,96},{96,64},{128,160},{160,128},{192,224},{224,1... | collective-permute-start | bytes 196616 | tf_op jit(solution)/shard_map/ppermute | solution.py:354
  7.4 0.0 copy-done.5
  7.4 0.0 copy-done.4
  7.4 0.1 maximum_bitcast_fusion
  7.5 0.1 pad_add_fusion.spot_ref
  7.6 1.3 %collective-permute-done.1.zb_ref = bf16[256,128]{1,0:T(8,128)(2,1)S(1)} collective-permute-done((bf16[256,128]{1,0:T(8,128)(2,1)S(1)}, bf16[256,128]{1,0:T(8,128)(2,1)S(1)}, u32[]{:S(2)}, u32[]{:S(2)}) %collective-permute-start.1) | collective-permute-done | bytes 65568 | tf_op jit(solution)/shard_map/ppermute | solution.py:355
  8.9 0.0 collective-permute-done.za_ref
  9.1 3.5 %collective-permute-start.3 = (bf16[6,2,8,128]{3,1,0,2:T(2,128)(2,1)S(1)}, bf16[6,2,8,128]{3,1,0,2:T(2,128)(2,1)S(1)}, u32[]{:S(2)}, u32[]{:S(2)}) collective-permute-start(bf16[6,2,8,128]{3,1,0,2:T(2,128)(2,1)S(1)} %pad_maximum_fusion.3), channel_id=1, source_target_pairs={{8,16},{16,8},{9,17},{17,9},{10,18},{18,10},{11,19},{19,11},{12,20... | collective-permute-start | bytes 73736 | tf_op jit(solution)/shard_map/ppermute | solution.py:371
  12.7 0.1 collective-permute-start.2
  12.8 2.0 %collective-permute-done.3 = bf16[6,2,8,128]{3,1,0,2:T(2,128)(2,1)S(1)} collective-permute-done((bf16[6,2,8,128]{3,1,0,2:T(2,128)(2,1)S(1)}, bf16[6,2,8,128]{3,1,0,2:T(2,128)(2,1)S(1)}, u32[]{:S(2)}, u32[]{:S(2)}) %collective-permute-start.3) | collective-permute-done | bytes 24608 | tf_op jit(solution)/shard_map/ppermute | solution.py:371
  14.8 1.8 %collective-permute-done.2 = bf16[6,2,8,128]{3,1,0,2:T(2,128)(2,1)S(1)} collective-permute-done((bf16[6,2,8,128]{3,1,0,2:T(2,128)(2,1)S(1)}, bf16[6,2,8,128]{3,1,0,2:T(2,128)(2,1)S(1)}, u32[]{:S(2)}, u32[]{:S(2)}) %collective-permute-start.2) | collective-permute-done | bytes 24608 | tf_op jit(solution)/shard_map/ppermute | solution.py:370
  16.6 0.7 %collective-permute-start.6 = (bf16[6,20,128]{2,1,0:T(8,128)(2,1)S(1)}, bf16[6,20,128]{2,1,0:T(8,128)(2,1)S(1)}, u32[]{:S(2)}, u32[]{:S(2)}) collective-permute-start(bf16[6,20,128]{2,1,0:T(8,128)(2,1)S(1)} %get-tuple-element.33), channel_id=1, source_target_pairs={{3,4},{4,3},{11,12},{12,11},{19,20},{20,19},{27,28},{28,27},{35,36... | collective-permute-start | bytes 92168 | tf_op jit(solution)/shard_map/ppermute | solution.py:378
  17.3 3.4 %collective-permute-start.4 = (bf16[6,20,128]{2,1,0:T(8,128)(2,1)S(1)}, bf16[6,20,128]{2,1,0:T(8,128)(2,1)S(1)}, u32[]{:S(2)}, u32[]{:S(2)}) collective-permute-start(bf16[6,20,128]{2,1,0:T(8,128)(2,1)S(1)} %get-tuple-element.34), channel_id=1, source_target_pairs={{0,1},{1,2},{2,3},{4,5},{5,6},{6,7},{8,9},{9,10},{10,11},{12,13},{... | collective-permute-start | bytes 92168 | tf_op jit(solution)/shard_map/ppermute | solution.py:380
  20.7 1.3 %collective-permute-start.5 = (bf16[6,20,128]{2,1,0:T(8,128)(2,1)S(1)}, bf16[6,20,128]{2,1,0:T(8,128)(2,1)S(1)}, u32[]{:S(2)}, u32[]{:S(2)}) collective-permute-start(bf16[6,20,128]{2,1,0:T(8,128)(2,1)S(1)} %pad_maximum_fusion.1), channel_id=1, source_target_pairs={{1,0},{2,1},{3,2},{5,4},{6,5},{7,6},{9,8},{10,9},{11,10},{13,12},{... | collective-permute-start | bytes 92168 | tf_op jit(solution)/shard_map/ppermute | solution.py:381
  22.0 0.0 copy-done
  22.0 0.0 copy-done.1
  22.0 0.0 copy-done.3
  22.0 0.0 copy-done.2
  22.1 4.9 %faces.1 = (bf16[4,256,128]{2,1,0:T(8,128)(2,1)S(1)}, f32[128,128]{1,0:T(8,128)S(1)}, bf16[1152,128]{1,0:T(8,128)(2,1)S(1)}, bf16[1152,128]{1,0:T(8,128)(2,1)S(1)}, bf16[2304,128]{1,0:T(8,128)(2,1)S(1)}) custom-call(bf16[32,256,128]{2,1,0:T(8,128)(2,1)} %bitcast.60, s32[256,128]{1,0:T(8,128)S(1)} %bitcast.50, s32[1,128]{1,0:T(1,128)S(1)} %bitcast.58, ...), custom_call_target="tpu_custom_call" | custom-call | flops 600000000 | bytes 4000000 | tf_op jit(solution)/shard_map/faces/pallas_call | solution.py:164
  27.0 0.0 collective-permute-done.6.far_ref
  27.0 0.0 collective-permute-done.4.xl_ref
  27.0 0.0 collective-permute-done.5.xr_ref
  27.0 4.5 %convolve.1 = (bf16[1024,64]{1,0:T(8,128)(2,1)}, f32[128,128]{1,0:T(8,128)S(1)}) custom-call(s32[3]{0:T(128)S(1)} %pad_add_fusion.spot_ref, bf16[256,128]{1,0:T(8,128)(2,1)S(1)} %pool.1.own_ref, bf16[256,128]{1,0:T(8,128)(2,1)S(1)} %collective-permute-done.za_ref, bf16[256,128]{1,0:T(8,128)(2,1)S(1)} %collective-permute-done.1.zb_ref, ...), custom_call_target="tpu_custom_call" | custom-call | flops 1000000000 | bytes 3000000 | tf_op jit(solution)/shard_map/convolve/pallas_call | solution.py:308
  31.6 22.8 %all_to_all.11 = f32[8,16,128]{2,1,0:T(8,128)} all-to-all(f32[8,16,128]{2,1,0:T(8,128)S(1)} %bitcast.51), channel_id=1, replica_groups=mesh['gz'=8,'gy'=4,'gx'=8] {'gx'}, dimensions={0} | all-to-all | bytes 131072 | tf_op jit(solution)/shard_map/all_to_all | solution.py:388
  54.3 1.7 %edges.1 = (f32[32,64]{1,0:T(8,128)}, f32[64,64]{1,0:T(8,128)}) custom-call(f32[128,128]{1,0:T(8,128)} %bitcast.61), custom_call_target="tpu_custom_call" | custom-call | tf_op jit(solution)/shard_map/edges/pallas_call | solution.py:339
  (23 shorter events, 0.3 us)
Async XLA Ops:
  0.6 6.8 %copy-start.5 = (f32[64]{0:T(128)S(1)}, f32[64]{0:T(128)}, u32[]{:S(2)}) copy-start(f32[64]{0:T(128)} %param.13) | copy-start | bytes 772
  0.6 6.8 %copy-start.4 = (f32[64]{0:T(128)S(1)}, f32[64]{0:T(128)}, u32[]{:S(2)}) copy-start(f32[64]{0:T(128)} %param.11) | copy-start | bytes 772
  0.7 21.4 %copy-start = (bf16[3,3,3,64,64]{4,3,2,1,0:T(8,128)(2,1)S(1)}, bf16[3,3,3,64,64]{4,3,2,1,0:T(8,128)(2,1)}, u32[]{:S(2)}) copy-start(bf16[3,3,3,64,64]{4,3,2,1,0:T(8,128)(2,1)} %param.12) | copy-start | bytes 663556
  0.7 21.4 %copy-start.1 = (bf16[3,3,3,64,32]{3,4,2,1,0:T(8,128)(2,1)S(1)}, bf16[3,3,3,64,32]{3,4,2,1,0:T(8,128)(2,1)}, u32[]{:S(2)}) copy-start(bf16[3,3,3,64,32]{3,4,2,1,0:T(8,128)(2,1)} %param.10) | copy-start | bytes 331780
  0.7 21.4 %copy-start.3 = (s32[128]{0:T(128)S(1)}, s32[128]{0:T(128)}, u32[]{:S(2)}) copy-start(s32[128]{0:T(128)} %param.9) | copy-start | bytes 1540
  0.7 21.4 %copy-start.2 = (s32[4,64,128]{2,1,0:T(8,128)S(1)}, s32[4,64,128]{2,1,0:T(8,128)}, u32[]{:S(2)}) copy-start(s32[4,64,128]{2,1,0:T(8,128)} %param.8) | copy-start | bytes 393220
  3.3 5.6 %collective-permute-start.1 = (bf16[256,128]{1,0:T(8,128)(2,1)S(1)}, bf16[256,128]{1,0:T(8,128)(2,1)S(1)}, u32[]{:S(2)}, u32[]{:S(2)}) collective-permute-start(bf16[256,128]{1,0:T(8,128)(2,1)S(1)} %pool.1.own_ref), channel_id=1, source_target_pairs={{32,64},{64,32},{96,128},{128,96},{160,192},{192,160},{33,65},{65,... | collective-permute-start | bytes 196616 | tf_op jit(solution)/shard_map/ppermute | solution.py:355
  5.2 3.7 %collective-permute-start = (bf16[256,128]{1,0:T(8,128)(2,1)S(1)}, bf16[256,128]{1,0:T(8,128)(2,1)S(1)}, u32[]{:S(2)}, u32[]{:S(2)}) collective-permute-start(bf16[256,128]{1,0:T(8,128)(2,1)S(1)} %pool.1.own_ref), channel_id=1, source_target_pairs={{0,32},{32,0},{64,96},{96,64},{128,160},{160,128},{192,224},{224,1... | collective-permute-start | bytes 196616 | tf_op jit(solution)/shard_map/ppermute | solution.py:354
  9.1 5.7 %collective-permute-start.3 = (bf16[6,2,8,128]{3,1,0,2:T(2,128)(2,1)S(1)}, bf16[6,2,8,128]{3,1,0,2:T(2,128)(2,1)S(1)}, u32[]{:S(2)}, u32[]{:S(2)}) collective-permute-start(bf16[6,2,8,128]{3,1,0,2:T(2,128)(2,1)S(1)} %pad_maximum_fusion.3), channel_id=1, source_target_pairs={{8,16},{16,8},{9,17},{17,9},{10,18},{18,10},{11,19},{19,11},{12,20... | collective-permute-start | bytes 73736 | tf_op jit(solution)/shard_map/ppermute | solution.py:371
  12.7 3.9 %collective-permute-start.2 = (bf16[6,2,8,128]{3,1,0,2:T(2,128)(2,1)S(1)}, bf16[6,2,8,128]{3,1,0,2:T(2,128)(2,1)S(1)}, u32[]{:S(2)}, u32[]{:S(2)}) collective-permute-start(bf16[6,2,8,128]{3,1,0,2:T(2,128)(2,1)S(1)} %pad_maximum_fusion.2), channel_id=1, source_target_pairs={{0,8},{8,0},{16,24},{24,16},{1,9},{9,1},{17,25},{25,17},{2,10},{10... | collective-permute-start | bytes 73736 | tf_op jit(solution)/shard_map/ppermute | solution.py:370
  16.6 10.4 %collective-permute-start.6 = (bf16[6,20,128]{2,1,0:T(8,128)(2,1)S(1)}, bf16[6,20,128]{2,1,0:T(8,128)(2,1)S(1)}, u32[]{:S(2)}, u32[]{:S(2)}) collective-permute-start(bf16[6,20,128]{2,1,0:T(8,128)(2,1)S(1)} %get-tuple-element.33), channel_id=1, source_target_pairs={{3,4},{4,3},{11,12},{12,11},{19,20},{20,19},{27,28},{28,27},{35,36... | collective-permute-start | bytes 92168 | tf_op jit(solution)/shard_map/ppermute | solution.py:378
  17.3 9.7 %collective-permute-start.4 = (bf16[6,20,128]{2,1,0:T(8,128)(2,1)S(1)}, bf16[6,20,128]{2,1,0:T(8,128)(2,1)S(1)}, u32[]{:S(2)}, u32[]{:S(2)}) collective-permute-start(bf16[6,20,128]{2,1,0:T(8,128)(2,1)S(1)} %get-tuple-element.34), channel_id=1, source_target_pairs={{0,1},{1,2},{2,3},{4,5},{5,6},{6,7},{8,9},{9,10},{10,11},{12,13},{... | collective-permute-start | bytes 92168 | tf_op jit(solution)/shard_map/ppermute | solution.py:380
  20.7 6.3 %collective-permute-start.5 = (bf16[6,20,128]{2,1,0:T(8,128)(2,1)S(1)}, bf16[6,20,128]{2,1,0:T(8,128)(2,1)S(1)}, u32[]{:S(2)}, u32[]{:S(2)}) collective-permute-start(bf16[6,20,128]{2,1,0:T(8,128)(2,1)S(1)} %pad_maximum_fusion.1), channel_id=1, source_target_pairs={{1,0},{2,1},{3,2},{5,4},{6,5},{7,6},{9,8},{10,9},{11,10},{13,12},{... | collective-permute-start | bytes 92168 | tf_op jit(solution)/shard_map/ppermute | solution.py:381

commit v3 on v2

--- a/solution.py
+++ b/solution.py
@@ -1,3 +1,5 @@
+import functools
+
 import jax
 import jax.numpy as jnp
 from jax import lax
@@ -13,6 +15,10 @@
 
 def dot(a, b, dims=NN):
     return lax.dot_general(a, b, dims, preferred_element_type=F32)
+
+
+def keep(array):
+    return pltpu.with_memory_space_constraint(array, pltpu.VMEM)
 
 
 def iota(shape, dim):
@@ -70,10 +76,9 @@
     return pl.pallas_call(
         pool_kernel,
         in_specs=[pl.BlockSpec(memory_space=pl.ANY)],
-        out_specs=pl.BlockSpec(memory_space=pltpu.VMEM),
-        out_shape=pltpu.VMEM((256, 128), BF),
+        out_specs=[pl.BlockSpec(memory_space=pltpu.VMEM)] * 2,
+        out_shape=[pltpu.VMEM((256, 128), BF), pltpu.VMEM((32, 256, 128), BF)],
         scratch_shapes=[
-            pltpu.VMEM((32, 256, 128), BF),
             pltpu.VMEM((32, 32, 128), F32),
             pltpu.SemaphoreType.DMA((chunks,)),
         ],
@@ -89,54 +94,54 @@
     return [jnp.concatenate([w[k + 1], w[k]], axis=1) for k in range(4)]
 
 
-def face_kernel(emb_ref, slot_ref, edge_ref, w1_ref, w2_ref, cnt_ref, face_ref, w1a_ref, w1b_ref, w2a_ref,
-                block, wide, order, cells, total, arrived):
-    step = pl.program_id(0)
-    last = pl.num_programs(0) - 1
-    copies = [
-        pltpu.make_async_copy(emb_ref.at[:, pl.ds(128 * i, 128), :], block.at[i], arrived.at[i]) for i in range(2)
-    ]
+def prepare_kernel(edge_ref, w1_ref, w2_ref, order_ref, w1a_ref, w1b_ref, w2a_ref):
     i0, i1 = iota((128, 128), 0), iota((128, 128), 1)
-
-    @pl.when(step == 0)
-    def _():
-        for copy in copies:
-            copy.start()
-        label = jnp.broadcast_to(edge_ref[...], (128, 128))
-        owner = ((label >> 6) & 7).astype(F32)
-        local = (label & 63).astype(F32)
-        ahead = jnp.where((owner == owner.T) & (i0 < i1), 1.0, 0.0)
-        place = owner[0:1, :] * 16.0 + jnp.sum(ahead, axis=0, keepdims=True)
-        chosen = place == i0.astype(F32)
-        face = jnp.sum(jnp.where(chosen, i1.astype(F32), 0.0), axis=1, keepdims=True)
-        edge = jnp.sum(jnp.where(chosen, local, 0.0), axis=1, keepdims=True)
-        order[0] = jnp.broadcast_to(face, (128, 128))
-        order[1] = jnp.broadcast_to(edge, (128, 128))
-        total[...] = jnp.zeros_like(total)
-        for tap in range(9):
-            bands = banded(tap, lambda t, k: w1_ref[3 * t + k])
-            w1a_ref[pl.ds(128 * tap, 128), :] = jnp.concatenate(bands, axis=0)
-            w1b_ref[pl.ds(128 * tap, 128), :] = jnp.concatenate(bands[2:] + bands[:2], axis=0)
-            bands = banded(tap, lambda t, k: w2_ref[3 * t + k].astype(F32).T.astype(BF))
-            w2a_ref[pl.ds(256 * tap, 256), :] = jnp.concatenate(bands, axis=0)
-
-    for i in range(2):
-
-        @pl.when(step == i)
-        def _():
-            copies[i].wait()
-
-    wide[...] = block[step].astype(F32).reshape(4096, 128)
-    faces = order[0].astype(jnp.int32)
-    pool_x = pool_x_matrix()
-    pool_x8 = jnp.concatenate([pool_x] * 8, axis=1)
+    label = jnp.broadcast_to(edge_ref[...], (128, 128))
+    owner = ((label >> 6) & 7).astype(F32)
+    local = (label & 63).astype(F32)
+    ahead = jnp.where((owner == owner.T) & (i0 < i1), 1.0, 0.0)
+    place = owner[0:1, :] * 16.0 + jnp.sum(ahead, axis=0, keepdims=True)
+    chosen = place == i0.astype(F32)
+    face = jnp.sum(jnp.where(chosen, i1.astype(F32), 0.0), axis=1, keepdims=True)
+    edge = jnp.sum(jnp.where(chosen, local, 0.0), axis=1, keepdims=True)
+    order_ref[0] = jnp.broadcast_to(face, (128, 128))
+    order_ref[1] = jnp.broadcast_to(edge, (128, 128))
+    for tap in range(9):
+        bands = banded(tap, lambda t, k: w1_ref[3 * t + k])
+        w1a_ref[pl.ds(128 * tap, 128), :] = jnp.concatenate(bands, axis=0)
+        w1b_ref[pl.ds(128 * tap, 128), :] = jnp.concatenate(bands[2:] + bands[:2], axis=0)
+        bands = banded(tap, lambda t, k: w2_ref[3 * t + k].astype(F32).T.astype(BF))
+        w2a_ref[pl.ds(256 * tap, 256), :] = jnp.concatenate(bands, axis=0)
+
+
+def prepare(edge, w1, w2):
+    return pl.pallas_call(
+        prepare_kernel,
+        in_specs=[pl.BlockSpec(memory_space=pltpu.VMEM)] * 3,
+        out_specs=[pl.BlockSpec(memory_space=pltpu.VMEM)] * 4,
+        out_shape=[
+            pltpu.VMEM((2, 128, 128), F32),
+            pltpu.VMEM((1152, 128), BF),
+            pltpu.VMEM((1152, 128), BF),
+            pltpu.VMEM((2304, 128), BF),
+        ],
+        compiler_params=pltpu.CompilerParams(vmem_limit_bytes=16 << 20),
+        cost_estimate=pl.CostEstimate(flops=1_000_000_000, bytes_accessed=2_000_000, transcendentals=0),
+        name="prepare",
+    )(edge, w1, w2)
+
+
+def face_kernel(half, emb_ref, slot_ref, order_ref, before_ref, cnt_ref, after_ref, wide, cells):
+    wide[...] = emb_ref[:, pl.ds(128 * half, 128), :].astype(F32).reshape(4096, 128)
+    faces = order_ref[0].astype(jnp.int32)
+    pool_x8 = jnp.concatenate([pool_x_matrix()] * 8, axis=1)
     sums = jnp.zeros((32, 128), F32)
     count = jnp.zeros((8, 128), F32)
     for yc in range(16):
         voxels, member = [], []
         for q in (64 * zi + 4 * yc + yy for zi in range(2) for yy in range(4)):
             voxels.append(wide[pl.ds(q, 32, stride=128), :].astype(BF))
-            row = jnp.broadcast_to(slot_ref[q : q + 1, :], (128, 128))
+            row = jnp.broadcast_to(slot_ref[128 * half + q : 128 * half + q + 1, :], (128, 128))
             member.append(jnp.where(row == faces, 1.0, 0.0).astype(BF))
         left = jnp.concatenate([jnp.concatenate(voxels, axis=1), pool_x8], axis=0)
         out = dot(left, jnp.concatenate(member, axis=1), NT)
@@ -145,58 +150,29 @@
             part = out[32 + 8 * x4 : 40 + 8 * x4]
             cells[x4, 8 * yc : 8 * yc + 8, :] = part
             count = count + part
-    total[0:32] += sums
-    total[32:40] += count
     for x4 in range(4):
         cnt_ref[x4 // 2, 128 * (x4 % 2) : 128 * (x4 % 2) + 128, :] = cells[x4].T.astype(BF)
-
-    @pl.when(step == last)
-    def _():
-        number = jnp.sum(total[32:40], axis=0, keepdims=True)
-        stacked = jnp.concatenate(
-            [jnp.zeros((64, 128), F32), total[0:32], jnp.broadcast_to(number, (32, 128))], axis=0
-        )
-        face_ref[...] = jnp.where(i1 == 97, order[1], stacked.T)
-
-
-def faces(emb, slot, edge, w1, w2):
-    whole = lambda *shape: pl.BlockSpec(shape, lambda i: (0,) * len(shape))
-    return pl.pallas_call(
-        face_kernel,
-        grid=(2,),
-        in_specs=[
-            pl.BlockSpec(memory_space=pl.ANY),
-            pl.BlockSpec((128, 128), lambda i: (i, 0)),
-            whole(1, 128),
-            whole(27, 32, 64),
-            whole(27, 64, 64),
-        ],
-        out_specs=[
-            pl.BlockSpec((2, 256, 128), lambda i: (i, 0, 0)),
-            whole(128, 128),
-            whole(1152, 128),
-            whole(1152, 128),
-            whole(2304, 128),
-        ],
-        out_shape=[
-            jax.ShapeDtypeStruct((4, 256, 128), BF),
-            jax.ShapeDtypeStruct((128, 128), F32),
-            jax.ShapeDtypeStruct((1152, 128), BF),
-            jax.ShapeDtypeStruct((1152, 128), BF),
-            jax.ShapeDtypeStruct((2304, 128), BF),
-        ],
-        scratch_shapes=[
-            pltpu.VMEM((2, 32, 128, 128), BF),
-            pltpu.VMEM((4096, 128), F32),
-            pltpu.VMEM((2, 128, 128), F32),
-            pltpu.VMEM((4, 128, 128), F32),
-            pltpu.VMEM((40, 128), F32),
-            pltpu.SemaphoreType.DMA((2,)),
-        ],
-        compiler_params=pltpu.CompilerParams(vmem_limit_bytes=32 << 20),
-        cost_estimate=pl.CostEstimate(flops=600_000_000, bytes_accessed=4_000_000, transcendentals=0),
+    if half == 0:
+        after_ref[0:32] = sums
+        after_ref[32:40] = count
+    else:
+        sums = sums + before_ref[0:32]
+        number = jnp.sum(count + before_ref[32:40], axis=0, keepdims=True)
+        stacked = jnp.concatenate([jnp.zeros((64, 128), F32), sums, jnp.broadcast_to(number, (32, 128))], axis=0)
+        after_ref[...] = jnp.where(iota((128, 128), 1) == 97, order_ref[1], stacked.T)
+
+
+def faces(half, emb, slot, order, before):
+    return pl.pallas_call(
+        functools.partial(face_kernel, half),
+        in_specs=[pl.BlockSpec(memory_space=pltpu.VMEM)] * 4,
+        out_specs=[pl.BlockSpec(memory_space=pltpu.VMEM)] * 2,
+        out_shape=[pltpu.VMEM((2, 256, 128), BF), pltpu.VMEM((128 if half else 40, 128), F32)],
+        scratch_shapes=[pltpu.VMEM((4096, 128), F32), pltpu.VMEM((4, 128, 128), F32)],
+        compiler_params=pltpu.CompilerParams(vmem_limit_bytes=16 << 20),
+        cost_estimate=pl.CostEstimate(flops=2_000_000_000, bytes_accessed=4_000_000, transcendentals=0),
         name="faces",
-    )(pltpu.with_memory_space_constraint(emb, pltpu.HBM), slot, edge, w1, w2)
+    )(keep(emb), slot, keep(order), keep(before))
 
 
 HEAD = 16
@@ -204,10 +180,10 @@
 ROWS2 = 4 * 18 * 16
 
 
-def conv_kernel(spot_ref, own_ref, za_ref, zb_ref, ya_ref, yb_ref, xl_ref, xr_ref, far_ref, w1a_ref, w1b_ref, b1_ref,
-                w2_ref, b2_ref, cnt_ref, face_ref, ctx_ref, send_ref, field, this, mixed, h0f, h0b, h0n, h1b, fine):
+def conv_kernel(spot_ref, own_ref, za_ref, zb_ref, ya_ref, yb_ref, xa_ref, xb_ref, w1a_ref, w1b_ref, b1_ref, w2_ref,
+                b2_ref, cnt0_ref, cnt1_ref, face_ref, ctx_ref, send_ref, field, this, mixed, h0f, h0b, h0n, h1b, fine):
     gz, gy, gx = spot_ref[0], spot_ref[1], spot_ref[2]
-    z_even, y_even = (gz & 1) == 0, (gy & 1) == 0
+    z_even, y_even, x_even = (gz & 1) == 0, (gy & 1) == 0, (gx & 1) == 0
     widen = lambda ref, *at: ref[at].astype(F32) if at else ref[...].astype(F32)
 
     za, zb, own = widen(za_ref), widen(zb_ref), widen(own_ref)
@@ -222,9 +198,8 @@
     y_low = by_z([y_low[32 * i : 32 * i + 32] for i in range(3)])
     y_high = by_z([y_high[32 * i : 32 * i + 32] for i in range(3)])
     sides = []
-    far = widen(far_ref)
-    for ref, end in ((xl_ref, 4), (xr_ref, 3)):
-        whole = jnp.where(gx == end, far, widen(ref))
+    xa, xb = widen(xa_ref), widen(xb_ref)
+    for whole in (jnp.where(x_even, xb, xa), jnp.where(x_even, xa, xb)):
         parts = by_z([whole[2 * i : 2 * i + 2] for i in range(3)])
         sides.append(parts)
     for part in range(3):
@@ -252,10 +227,10 @@
 
     row, lane = iota((288, 128), 0), iota((288, 128), 1)
     slot = row & 15
-    keep = jnp.where((row < 16) & (gy == 0), 0.0, 1.0)
-    keep = jnp.where((row >= 272) & (gy == 3), 0.0, keep)
-    keep0 = jnp.where((slot == 0) & (lane < 64) & (gx == 0), 0.0, keep)
-    keep0 = jnp.where((slot == 8) & (lane >= 64) & (gx == 7), 0.0, keep0)
+    stay = jnp.where((row < 16) & (gy == 0), 0.0, 1.0)
+    stay = jnp.where((row >= 272) & (gy == 3), 0.0, stay)
+    stay0 = jnp.where((slot == 0) & (lane < 64) & (gx == 0), 0.0, stay)
+    stay0 = jnp.where((slot == 8) & (lane >= 64) & (gx == 7), 0.0, stay0)
     b1, b2 = b1_ref[...], b2_ref[...]
 
     def conv1(source, weights, z):
@@ -274,8 +249,8 @@
             inside = jnp.where(gz == 0, 0.0, 1.0)
         if z == 3:
             inside = jnp.where(gz == 7, 0.0, 1.0)
-        h0f[pl.ds(288 * z, 288), :] = conv1(mixed, w1b_ref, z) * (keep0 * inside)
-        h1b[pl.ds(288 * z, 288), :] = (conv1(this, w1a_ref, z) * (keep * inside)).astype(BF)
+        h0f[pl.ds(288 * z, 288), :] = conv1(mixed, w1b_ref, z) * (stay0 * inside)
+        h1b[pl.ds(288 * z, 288), :] = (conv1(this, w1a_ref, z) * (stay * inside)).astype(BF)
     for z in range(4):
         h0b[pl.ds(288 * z, 288), :] = h0f[pl.ds(288 * z, 288), :].astype(BF)
         h0n[pl.ds(288 * z, 288), :] = h0f[pl.ds(288 * z + 1, 288), :].astype(BF)
@@ -297,7 +272,7 @@
             wide = ctx.astype(F32)
             fine[pl.ds(512 * z + 2 * p, 128, stride=4), :] = wide
             fine[pl.ds(512 * z + 2 * p + 1, 128, stride=4), :] = pltpu.roll(wide, 64, 1)
-            term = dot(cnt_ref[2 * z + p], ctx)
+            term = dot((cnt0_ref, cnt1_ref)[z][p], ctx)
             sums = term if sums is None else sums + term
     ctx_ref[...] = fine[...][:, :64].astype(BF)
     both = sums[:128] + pltpu.roll(sums[128:], 64, 1)
@@ -309,7 +284,7 @@
         conv_kernel,
         in_specs=[pl.BlockSpec(memory_space=pltpu.SMEM)] + [pl.BlockSpec(memory_space=pltpu.VMEM)] * len(arrays),
         out_specs=[pl.BlockSpec(memory_space=pltpu.VMEM)] * 2,
-        out_shape=[jax.ShapeDtypeStruct((1024, 64), BF), jax.ShapeDtypeStruct((128, 128), F32)],
+        out_shape=[jax.ShapeDtypeStruct((1024, 64), BF), pltpu.VMEM((128, 128), F32)],
         scratch_shapes=[
             pltpu.VMEM((HEAD + ROWS1, 128), F32),
             pltpu.VMEM((ROWS1, 128), BF),
@@ -350,40 +325,41 @@
 def per_device(embedding, face_slot, face_edge, conv1_w, conv1_b, conv2_w, conv2_b):
     emb = embedding.reshape(32, 256, 128)
     gz, gy, gx = (lax.axis_index(a) for a in ("gz", "gy", "gx"))
-    own = pool(emb)
+    slot = face_slot.reshape(256, 128)
+    own, voxels = pool(emb)
+    zb = lax.ppermute(own, "gz", pairs(1, 8))
     za = lax.ppermute(own, "gz", pairs(0, 8))
-    zb = lax.ppermute(own, "gz", pairs(1, 8))
-    cnt, face, w1a, w1b, w2a = faces(
-        emb,
-        face_slot.reshape(256, 128),
+    order, w1a, w1b, w2a = prepare(
         face_edge.reshape(1, 128),
         jnp.swapaxes(conv1_w, 3, 4).reshape(27, 32, 64),
         conv2_w.reshape(27, 64, 64),
     )
+    za, zb, order = lax.optimization_barrier((za, zb, order))
     planes = [a.reshape(2, 16, 8, 128) for a in (za, own, zb)]
-    y_even = (gy & 1) == 0
+    y_even, x_even = (gy & 1) == 0, (gx & 1) == 0
 
     def y_edge(high):
         first = jnp.where(high, 14, 0)
         return jnp.concatenate([lax.dynamic_slice_in_dim(a, first, 2, axis=1) for a in planes], axis=0)
 
+    yb = lax.ppermute(y_edge(jnp.logical_not(y_even)), "gy", pairs(1, 4))
     ya = lax.ppermute(y_edge(y_even), "gy", pairs(0, 4))
-    yb = lax.ppermute(y_edge(jnp.logical_not(y_even)), "gy", pairs(1, 4))
+    cnt0, half = faces(0, voxels, slot, order, order[0, :40])
+    ya, yb, half = lax.optimization_barrier((ya, yb, half))
 
     def x_edge(g):
         mid = jnp.concatenate([a[:, :, g] for a in planes], axis=0)
         return jnp.concatenate([mid, ya[:, :, g], yb[:, :, g]], axis=1)
 
     low, high = x_edge(0), x_edge(7)
-    far = lax.ppermute(jnp.where(gx == 3, high, low), "gx", [(3, 4), (4, 3)])
-    right = [(i, i + 1) for i in range(7) if i != 3]
-    xl = lax.ppermute(high, "gx", right)
-    xr = lax.ppermute(low, "gx", [(b, a) for a, b in right])
+    xb = lax.ppermute(jnp.where(x_even, low, high), "gx", pairs(1, 8))
+    xa = lax.ppermute(jnp.where(x_even, high, low), "gx", pairs(0, 8))
+    cnt1, face = faces(1, voxels, slot, order, half)
     spot = jnp.stack([gz, gy, gx]).astype(jnp.int32)
     twice = lambda b: jnp.concatenate([b, b]).reshape(1, 128)
     context, send = convolve(
-        spot, own, za, zb, ya.reshape(96, 128), yb.reshape(96, 128), xl, xr, far, w1a, w1b, twice(conv1_b), w2a,
-        twice(conv2_b), cnt, face,
+        spot, own, za, zb, ya.reshape(96, 128), yb.reshape(96, 128), xa, xb, keep(w1a), keep(w1b), twice(conv1_b),
+        keep(w2a), twice(conv2_b), keep(cnt0), keep(cnt1), keep(face),
     )
     rows = lax.all_to_all(send, "gx", 0, 0, tiled=True)
     edge_emb, edge_ctx = edges(rows)

time: 56.4 us -> 52.8 us (0.936)
  starting transfers between devices: 13 us -> 10.8 us
  Pallas kernels: 13.7 us -> 13 us
    ppermute x1, starting transfers between devices: 2.11 us -> 0.09 us  [per_device(): za = lax.ppermute(own, 'gz', pairs(0, 8))]
    ppermute x1, waiting for transfers between devices: 2.03 us -> 0.08 us  [per_device(): yb = lax.ppermute(y_edge(jnp.logical_not(y_even)), 'gy', pairs(1, 4))]
    ppermute x1, waiting for transfers between devices: 1.29 us -> 2.67 us  [per_device(): zb = lax.ppermute(own, 'gz', pairs(1, 8))]
    pallas_call x1 -> x3, Pallas kernels: 4.9 us -> 4.15 us  [the longest x2 3.68 us: faces(): pl.pallas_call(functools.partial(face_kernel, half), in_specs=[pl.BlockSp...]
    ppermute x3 -> x2, starting transfers between devices: 5.35 us -> 4.98 us  [the longest x1 4.31 us: per_device(): xa = lax.ppermute(jnp.where(x_even, high, low), 'gx', pairs(0, 8))]
  transfers between devices with their start and end apart: 7 -> 6, of which waited for: 3 -> 4; matrix products, arithmetic and copies ran while one was open for 1% -> 1% of each run, Pallas kernels for 9% -> 8%
where the time goes in v3:
time: 52.8 us; the launch traced here: 52.5 us
  blocking collectives  22.7 us (43%)
  Pallas kernels  13 us (25%)
  starting transfers between devices  10.8 us (20%)
  waiting for transfers between devices  4.65 us (9%)
  between operations  0.98 us (2%)
    all_to_all x1, blocking collectives, per_device(): rows = lax.all_to_all(send, 'gx', 0, 0, tiled=True)  22.7 us
    pallas_call x1, Pallas kernels, convolve(): pl.pallas_call(conv_kernel, in_specs=[pl.BlockSpec(memory_space=pltpu.SME...  4.54 us
    ppermute x1, starting transfers between devices, per_device(): xa = lax.ppermute(jnp.where(x_even, high, low), 'gx', pairs(0, 8))  4.31 us
    pallas_call x2, Pallas kernels, faces(): pl.pallas_call(functools.partial(face_kernel, half), in_specs=[pl.BlockSp...  3.68 us
    ppermute x1, starting transfers between devices, per_device(): yb = lax.ppermute(y_edge(jnp.logical_not(y_even)), 'gy', pairs(1, 4))  3.49 us
    ppermute x1, waiting for transfers between devices, per_device(): zb = lax.ppermute(own, 'gz', pairs(1, 8))  2.67 us
    pallas_call x1, Pallas kernels, pool(): pl.pallas_call(pool_kernel, in_specs=[pl.BlockSpec(memory_space=pl.ANY)],...  2.57 us
    ppermute x1, starting transfers between devices, per_device(): zb = lax.ppermute(own, 'gz', pairs(1, 8))  2.11 us
  transfers between devices with their start and end apart: 6, of which 4 were waited for; matrix products, arithmetic and copies ran while one was open for 1% of the time, Pallas kernels for 8%

profile of v3, /device:TPU:40, one launch (start us, length us, event | category | flops | bytes accessed | tf_op | source)
XLA Modules:
  0.0 52.5 jit_solution(7977991188310671556)
XLA Ops:
  0.6 0.0 copy-start.4
  0.6 0.0 copy-start.5
  0.7 0.0 copy-start.3
  0.7 0.0 copy-start.1
  0.7 0.0 copy-start
  0.7 2.6 %pool.1 = (bf16[256,128]{1,0:T(8,128)(2,1)S(1)}, bf16[32,256,128]{2,1,0:T(8,128)(2,1)S(1)}) custom-call(bf16[32,256,128]{2,1,0:T(8,128)(2,1)} %bitcast.60), custom_call_target="tpu_custom_call" | custom-call | flops 80000000 | bytes 2200000 | tf_op jit(solution)/shard_map/pool/pallas_call | solution.py:76
  3.3 0.1 collective-permute-start
  3.4 2.1 %collective-permute-start.1 = (bf16[256,128]{1,0:T(8,128)(2,1)S(1)}, bf16[256,128]{1,0:T(8,128)(2,1)S(1)}, u32[]{:S(2)}, u32[]{:S(2)}) collective-permute-start(bf16[256,128]{1,0:T(8,128)(2,1)S(1)} %get-tuple-element.23.own_ref), channel_id=1, source_target_pairs={{32,64},{64,32},{96,128},{128,96},{160,192},{192,160},{33,65},{65,... | collective-permute-start | bytes 196616 | tf_op jit(solution)/shard_map/ppermute | solution.py:330
  5.6 0.0 copy-done.4
  5.6 0.0 copy-done.5
  5.6 0.1 maximum_bitcast_fusion
  5.7 0.1 pad_add_fusion.spot_ref
  5.8 0.0 copy-done.3
  5.8 0.0 copy-done.1
  5.8 0.0 copy-done
  5.8 0.0 copy-start.2
  5.8 0.5 prepare.1
  6.3 0.0 collective-permute-done.za_ref
  6.3 2.7 %collective-permute-done.1.zb_ref = bf16[256,128]{1,0:T(8,128)(2,1)S(1)} collective-permute-done((bf16[256,128]{1,0:T(8,128)(2,1)S(1)}, bf16[256,128]{1,0:T(8,128)(2,1)S(1)}, u32[]{:S(2)}, u32[]{:S(2)}) %collective-permute-start.1) | collective-permute-done | bytes 65568 | tf_op jit(solution)/shard_map/ppermute | solution.py:330
  9.1 3.5 %collective-permute-start.3 = (bf16[6,2,8,128]{3,1,0,2:T(2,128)(2,1)S(1)}, bf16[6,2,8,128]{3,1,0,2:T(2,128)(2,1)S(1)}, u32[]{:S(2)}, u32[]{:S(2)}) collective-permute-start(bf16[6,2,8,128]{3,1,0,2:T(2,128)(2,1)S(1)} %pad_maximum_fusion.3), channel_id=1, source_target_pairs={{8,16},{16,8},{9,17},{17,9},{10,18},{18,10},{11,19},{19,11},{12,20... | collective-permute-start | bytes 73736 | tf_op jit(solution)/shard_map/ppermute | solution.py:345
  12.7 0.1 collective-permute-start.2
  12.8 0.0 copy-done.2
  12.8 1.9 %faces.2 = (bf16[2,256,128]{2,1,0:T(8,128)(2,1)S(1)}, f32[40,128]{1,0:T(8,128)S(1)}) custom-call(bf16[32,256,128]{2,1,0:T(8,128)(2,1)S(1)} %get-tuple-element.27.emb_ref, s32[256,128]{1,0:T(8,128)S(1)} %bitcast.57, f32[2,128,128]{2,1,0:T(8,128)S(1)} %get-tuple-element.28.order_ref, f32[40,128]{1,0:T(8,128)S(1)} %slice_bitcast_fusion.before_ref), custom_call_target="tpu_custom_call" | custom-call | flops 2000000000 | bytes 4000000 | tf_op jit(solution)/shard_map/faces/pallas_call | solution.py:166
  14.7 0.1 collective-permute-done.3
  14.8 1.8 %collective-permute-done.2 = bf16[6,2,8,128]{3,1,0,2:T(2,128)(2,1)S(1)} collective-permute-done((bf16[6,2,8,128]{3,1,0,2:T(2,128)(2,1)S(1)}, bf16[6,2,8,128]{3,1,0,2:T(2,128)(2,1)S(1)}, u32[]{:S(2)}, u32[]{:S(2)}) %collective-permute-start.2) | collective-permute-done | bytes 24608 | tf_op jit(solution)/shard_map/ppermute | solution.py:346
  16.7 0.7 %collective-permute-start.5 = (bf16[6,20,128]{2,1,0:T(8,128)(2,1)S(1)}, bf16[6,20,128]{2,1,0:T(8,128)(2,1)S(1)}, u32[]{:S(2)}, u32[]{:S(2)}) collective-permute-start(bf16[6,20,128]{2,1,0:T(8,128)(2,1)S(1)} %broadcast_select_fusion), channel_id=1, source_target_pairs={{1,2},{2,1},{3,4},{4,3},{5,6},{6,5},{9,10},{10,9},{11,12},{12,11},... | collective-permute-start | bytes 92168 | tf_op jit(solution)/shard_map/ppermute | solution.py:355
  17.4 4.3 %collective-permute-start.4 = (bf16[6,20,128]{2,1,0:T(8,128)(2,1)S(1)}, bf16[6,20,128]{2,1,0:T(8,128)(2,1)S(1)}, u32[]{:S(2)}, u32[]{:S(2)}) collective-permute-start(bf16[6,20,128]{2,1,0:T(8,128)(2,1)S(1)} %broadcast_select_fusion.1), channel_id=1, source_target_pairs={{0,1},{1,0},{2,3},{3,2},{4,5},{5,4},{6,7},{7,6},{8,9},{9,8},{10,11... | collective-permute-start | bytes 92168 | tf_op jit(solution)/shard_map/ppermute | solution.py:356
  21.7 1.8 %faces.3 = (bf16[2,256,128]{2,1,0:T(8,128)(2,1)S(1)}, f32[128,128]{1,0:T(8,128)S(1)}) custom-call(bf16[32,256,128]{2,1,0:T(8,128)(2,1)S(1)} %get-tuple-element.27.emb_ref, s32[256,128]{1,0:T(8,128)S(1)} %bitcast.58, f32[2,128,128]{2,1,0:T(8,128)S(1)} %get-tuple-element.28.order_ref, f32[40,128]{1,0:T(8,128)S(1)} %get-tuple-element.36.before_ref), custom_call_target="tpu_custom_call" | custom-call | flops 2000000000 | bytes 4000000 | tf_op jit(solution)/shard_map/faces/pallas_call | solution.py:166
  23.5 0.0 collective-permute-done.5.xb_ref
  23.5 0.1 collective-permute-done.4.xa_ref
  23.6 4.5 %convolve.1 = (bf16[1024,64]{1,0:T(8,128)(2,1)}, f32[128,128]{1,0:T(8,128)S(1)}) custom-call(s32[3]{0:T(128)S(1)} %pad_add_fusion.spot_ref, bf16[256,128]{1,0:T(8,128)(2,1)S(1)} %get-tuple-element.23.own_ref, bf16[256,128]{1,0:T(8,128)(2,1)S(1)} %collective-permute-done.za_ref, bf16[256,128]{1,0:T(8,128)(2,1)S(1)} %collective-permute-done.1.zb_ref, ...), custom_call_target="tpu_custom_call" | custom-call | flops 1000000000 | bytes 3000000 | tf_op jit(solution)/shard_map/convolve/pallas_call | solution.py:283
  28.2 22.7 %all_to_all.11 = f32[8,16,128]{2,1,0:T(8,128)} all-to-all(f32[8,16,128]{2,1,0:T(8,128)S(1)} %bitcast.46), channel_id=1, replica_groups=mesh['gz'=8,'gy'=4,'gx'=8] {'gx'}, dimensions={0} | all-to-all | bytes 131072 | tf_op jit(solution)/shard_map/all_to_all | solution.py:364
  50.8 1.7 %edges.1 = (f32[32,64]{1,0:T(8,128)}, f32[64,64]{1,0:T(8,128)}) custom-call(f32[128,128]{1,0:T(8,128)} %bitcast.61), custom_call_target="tpu_custom_call" | custom-call | tf_op jit(solution)/shard_map/edges/pallas_call | solution.py:314
  (23 shorter events, 0.3 us)
Async XLA Ops:
  0.6 5.0 %copy-start.4 = (f32[64]{0:T(128)S(1)}, f32[64]{0:T(128)}, u32[]{:S(2)}) copy-start(f32[64]{0:T(128)} %param.11) | copy-start | bytes 772
  0.6 5.0 %copy-start.5 = (f32[64]{0:T(128)S(1)}, f32[64]{0:T(128)}, u32[]{:S(2)}) copy-start(f32[64]{0:T(128)} %param.13) | copy-start | bytes 772
  0.7 5.1 %copy-start.3 = (s32[128]{0:T(128)S(1)}, s32[128]{0:T(128)}, u32[]{:S(2)}) copy-start(s32[128]{0:T(128)} %param.9) | copy-start | bytes 1540
  0.7 5.1 %copy-start.1 = (bf16[3,3,3,64,32]{3,4,2,1,0:T(8,128)(2,1)S(1)}, bf16[3,3,3,64,32]{3,4,2,1,0:T(8,128)(2,1)}, u32[]{:S(2)}) copy-start(bf16[3,3,3,64,32]{3,4,2,1,0:T(8,128)(2,1)} %param.10) | copy-start | bytes 331780
  0.7 5.1 %copy-start = (bf16[3,3,3,64,64]{4,3,2,1,0:T(8,128)(2,1)S(1)}, bf16[3,3,3,64,64]{4,3,2,1,0:T(8,128)(2,1)}, u32[]{:S(2)}) copy-start(bf16[3,3,3,64,64]{4,3,2,1,0:T(8,128)(2,1)} %param.12) | copy-start | bytes 663556
  3.3 3.0 %collective-permute-start = (bf16[256,128]{1,0:T(8,128)(2,1)S(1)}, bf16[256,128]{1,0:T(8,128)(2,1)S(1)}, u32[]{:S(2)}, u32[]{:S(2)}) collective-permute-start(bf16[256,128]{1,0:T(8,128)(2,1)S(1)} %get-tuple-element.23.own_ref), channel_id=1, source_target_pairs={{0,32},{32,0},{64,96},{96,64},{128,160},{160,128},{192,224},{224,1... | collective-permute-start | bytes 196616 | tf_op jit(solution)/shard_map/ppermute | solution.py:331
  3.4 5.6 %collective-permute-start.1 = (bf16[256,128]{1,0:T(8,128)(2,1)S(1)}, bf16[256,128]{1,0:T(8,128)(2,1)S(1)}, u32[]{:S(2)}, u32[]{:S(2)}) collective-permute-start(bf16[256,128]{1,0:T(8,128)(2,1)S(1)} %get-tuple-element.23.own_ref), channel_id=1, source_target_pairs={{32,64},{64,32},{96,128},{128,96},{160,192},{192,160},{33,65},{65,... | collective-permute-start | bytes 196616 | tf_op jit(solution)/shard_map/ppermute | solution.py:330
  5.8 7.0 %copy-start.2 = (s32[4,64,128]{2,1,0:T(8,128)S(1)}, s32[4,64,128]{2,1,0:T(8,128)}, u32[]{:S(2)}) copy-start(s32[4,64,128]{2,1,0:T(8,128)} %param.8) | copy-start | bytes 393220
  9.1 5.7 %collective-permute-start.3 = (bf16[6,2,8,128]{3,1,0,2:T(2,128)(2,1)S(1)}, bf16[6,2,8,128]{3,1,0,2:T(2,128)(2,1)S(1)}, u32[]{:S(2)}, u32[]{:S(2)}) collective-permute-start(bf16[6,2,8,128]{3,1,0,2:T(2,128)(2,1)S(1)} %pad_maximum_fusion.3), channel_id=1, source_target_pairs={{8,16},{16,8},{9,17},{17,9},{10,18},{18,10},{11,19},{19,11},{12,20... | collective-permute-start | bytes 73736 | tf_op jit(solution)/shard_map/ppermute | solution.py:345
  12.7 3.9 %collective-permute-start.2 = (bf16[6,2,8,128]{3,1,0,2:T(2,128)(2,1)S(1)}, bf16[6,2,8,128]{3,1,0,2:T(2,128)(2,1)S(1)}, u32[]{:S(2)}, u32[]{:S(2)}) collective-permute-start(bf16[6,2,8,128]{3,1,0,2:T(2,128)(2,1)S(1)} %pad_maximum_fusion.2), channel_id=1, source_target_pairs={{0,8},{8,0},{16,24},{24,16},{1,9},{9,1},{17,25},{25,17},{2,10},{10... | collective-permute-start | bytes 73736 | tf_op jit(solution)/shard_map/ppermute | solution.py:346
  16.7 6.8 %collective-permute-start.5 = (bf16[6,20,128]{2,1,0:T(8,128)(2,1)S(1)}, bf16[6,20,128]{2,1,0:T(8,128)(2,1)S(1)}, u32[]{:S(2)}, u32[]{:S(2)}) collective-permute-start(bf16[6,20,128]{2,1,0:T(8,128)(2,1)S(1)} %broadcast_select_fusion), channel_id=1, source_target_pairs={{1,2},{2,1},{3,4},{4,3},{5,6},{6,5},{9,10},{10,9},{11,12},{12,11},... | collective-permute-start | bytes 92168 | tf_op jit(solution)/shard_map/ppermute | solution.py:355
  17.4 6.3 %collective-permute-start.4 = (bf16[6,20,128]{2,1,0:T(8,128)(2,1)S(1)}, bf16[6,20,128]{2,1,0:T(8,128)(2,1)S(1)}, u32[]{:S(2)}, u32[]{:S(2)}) collective-permute-start(bf16[6,20,128]{2,1,0:T(8,128)(2,1)S(1)} %broadcast_select_fusion.1), channel_id=1, source_target_pairs={{0,1},{1,0},{2,3},{3,2},{4,5},{5,4},{6,7},{7,6},{8,9},{9,8},{10,11... | collective-permute-start | bytes 92168 | tf_op jit(solution)/shard_map/ppermute | solution.py:356

commit v4 on v3

--- a/solution.py
+++ b/solution.py
@@ -175,48 +175,48 @@
     )(keep(emb), slot, keep(order), keep(before))
 
 
-HEAD = 16
 ROWS1 = 6 * 20 * 16
 ROWS2 = 4 * 18 * 16
-
-
-def conv_kernel(spot_ref, own_ref, za_ref, zb_ref, ya_ref, yb_ref, xa_ref, xb_ref, w1a_ref, w1b_ref, b1_ref, w2_ref,
-                b2_ref, cnt0_ref, cnt1_ref, face_ref, ctx_ref, send_ref, field, this, mixed, h0f, h0b, h0n, h1b, fine):
-    gz, gy, gx = spot_ref[0], spot_ref[1], spot_ref[2]
-    z_even, y_even, x_even = (gz & 1) == 0, (gy & 1) == 0, (gx & 1) == 0
-    widen = lambda ref, *at: ref[at].astype(F32) if at else ref[...].astype(F32)
-
-    za, zb, own = widen(za_ref), widen(zb_ref), widen(own_ref)
-    zs = (jnp.where(z_even, zb, za), own, jnp.where(z_even, za, zb))
-    ya, yb = widen(ya_ref), widen(yb_ref)
-    y_low, y_high = jnp.where(y_even, yb, ya), jnp.where(y_even, ya, yb)
-
-    def by_z(parts):
-        a, mid, b = parts
-        return (jnp.where(z_even, b, a), mid, jnp.where(z_even, a, b))
-
-    y_low = by_z([y_low[32 * i : 32 * i + 32] for i in range(3)])
-    y_high = by_z([y_high[32 * i : 32 * i + 32] for i in range(3)])
-    sides = []
-    xa, xb = widen(xa_ref), widen(xb_ref)
-    for whole in (jnp.where(x_even, xb, xa), jnp.where(x_even, xa, xb)):
-        parts = by_z([whole[2 * i : 2 * i + 2] for i in range(3)])
-        sides.append(parts)
+HEAD = 16
+
+
+def ordered(even, a, b):
+    return jnp.where(even, b, a), jnp.where(even, a, b)
+
+
+def taps_dot(lefts, weights, depth):
+    total = None
+    per = 256 // depth
+    for t in range(0, 9, per):
+        group = lefts[t : t + per]
+        left = group[0] if len(group) == 1 else jnp.concatenate(group, axis=1)
+        term = dot(left, weights[pl.ds(depth * t, depth * len(group)), :])
+        total = term if total is None else total + term
+    return total
+
+
+def inner_kernel(spot_ref, own_ref, za_ref, zb_ref, ya_ref, yb_ref, w1a_ref, w1b_ref, b1_ref, w2_ref, b2_ref, cnt0_ref,
+                 cnt1_ref, fine_ref, sums_ref, ends_ref, near_ref, field, this, mixed, h0f, h1f, h0b, h0n, h1b):
+    gz, gy = spot_ref[0], spot_ref[1]
+    z_even, y_even = (gz & 1) == 0, (gy & 1) == 0
+    z_low, z_high = ordered(z_even, za_ref[...].astype(F32), zb_ref[...].astype(F32))
+    zs = (z_low, own_ref[...].astype(F32), z_high)
+    ya, yb = ya_ref[...].astype(F32), yb_ref[...].astype(F32)
+    ys = []
+    for whole in ordered(y_even, ya, yb):
+        low, high = ordered(z_even, whole[0:32], whole[64:96])
+        ys.append((low, whole[32:64], high))
     for part in range(3):
         for i in range(2):
-            base = HEAD + (2 * part + i) * 320
+            plane = 2 * part + i
+            base = HEAD + plane * 320
             for y in range(16):
                 field[pl.ds(base + 32 + 16 * y, 8), :] = zs[part][128 * i + 8 * y : 128 * i + 8 * y + 8]
             for y in range(2):
-                field[pl.ds(base + 16 * y, 8), :] = y_low[part][16 * i + 8 * y : 16 * i + 8 * y + 8]
-                field[pl.ds(base + 288 + 16 * y, 8), :] = y_high[part][16 * i + 8 * y : 16 * i + 8 * y + 8]
-            for side, at in ((sides[0], -1), (sides[1], 8)):
-                rows = side[part][i]
-                a, b = rows[16:18], rows[18:20]
-                low, high = jnp.where(y_even, b, a), jnp.where(y_even, a, b)
-                column = jnp.concatenate([low, rows[0:16], high], axis=0)
-                for y in range(20):
-                    field[pl.ds(base + 16 * y + at, 1), :] = column[y : y + 1]
+                field[pl.ds(base + 16 * y, 8), :] = ys[0][part][16 * i + 8 * y : 16 * i + 8 * y + 8]
+                field[pl.ds(base + 288 + 16 * y, 8), :] = ys[1][part][16 * i + 8 * y : 16 * i + 8 * y + 8]
+            for k, g in enumerate((0, 7)):
+                ends_ref[k, pl.ds(24 * plane, 20), :] = field[pl.ds(base + g, 20, stride=16), :]
 
     lane = iota((320, 128), 1)
     for z in range(6):
@@ -225,23 +225,14 @@
         this[pl.ds(320 * z, 320), :] = now.astype(BF)
         mixed[pl.ds(320 * z, 320), :] = jnp.where(lane < 64, now, before).astype(BF)
 
-    row, lane = iota((288, 128), 0), iota((288, 128), 1)
-    slot = row & 15
+    row = iota((288, 128), 0)
     stay = jnp.where((row < 16) & (gy == 0), 0.0, 1.0)
     stay = jnp.where((row >= 272) & (gy == 3), 0.0, stay)
-    stay0 = jnp.where((slot == 0) & (lane < 64) & (gx == 0), 0.0, stay)
-    stay0 = jnp.where((slot == 8) & (lane >= 64) & (gx == 7), 0.0, stay0)
     b1, b2 = b1_ref[...], b2_ref[...]
 
     def conv1(source, weights, z):
-        total = None
-        for t in range(0, 9, 2):
-            group = range(t, min(t + 2, 9))
-            at = [((z + tap // 3) * 20 + tap % 3) * 16 for tap in group]
-            left = jnp.concatenate([source[pl.ds(r, 288), :] for r in at], axis=1)
-            term = dot(left, weights[pl.ds(128 * t, 128 * len(at)), :])
-            total = term if total is None else total + term
-        return jnp.maximum(total + b1, 0.0)
+        lefts = [source[pl.ds(((z + tap // 3) * 20 + tap % 3) * 16, 288), :] for tap in range(9)]
+        return jnp.maximum(taps_dot(lefts, weights, 128) + b1, 0.0)
 
     for z in range(4):
         inside = 1.0
@@ -249,73 +240,152 @@
             inside = jnp.where(gz == 0, 0.0, 1.0)
         if z == 3:
             inside = jnp.where(gz == 7, 0.0, 1.0)
-        h0f[pl.ds(288 * z, 288), :] = conv1(mixed, w1b_ref, z) * (stay0 * inside)
-        h1b[pl.ds(288 * z, 288), :] = (conv1(this, w1a_ref, z) * (stay * inside)).astype(BF)
+        h0f[pl.ds(288 * z, 288), :] = conv1(mixed, w1b_ref, z) * (stay * inside)
+        h1 = conv1(this, w1a_ref, z) * (stay * inside)
+        h1f[pl.ds(288 * z, 288), :] = h1
+        h1b[pl.ds(288 * z, 288), :] = h1.astype(BF)
+        for k, g in enumerate((0, 7)):
+            near_ref[k, pl.ds(24 * z, 18), :] = h1f[pl.ds(288 * z + g, 18, stride=16), :]
     for z in range(4):
         h0b[pl.ds(288 * z, 288), :] = h0f[pl.ds(288 * z, 288), :].astype(BF)
         h0n[pl.ds(288 * z, 288), :] = h0f[pl.ds(288 * z + 1, 288), :].astype(BF)
 
-    def conv2(first, second, z):
-        total = None
-        for tap in range(9):
-            r = ((z + tap // 3) * 18 + tap % 3) * 16
-            left = jnp.concatenate([first[pl.ds(r, 256), :], second[pl.ds(r, 256), :]], axis=1)
-            term = dot(left, w2_ref[pl.ds(256 * tap, 256), :])
-            total = term if total is None else total + term
-        total = total.reshape(16, 16, 128)[:, :8, :].reshape(128, 128)
-        return (total + b2).astype(BF)
-
+    group = iota((128, 128), 0) & 7
     sums = None
     for z in range(2):
         for p, (first, second) in enumerate(((h0b, h1b), (h1b, h0n))):
-            ctx = conv2(first, second, z)
+            at = [((z + tap // 3) * 18 + tap % 3) * 16 for tap in range(9)]
+            lefts = [jnp.concatenate([first[pl.ds(r, 256), :], second[pl.ds(r, 256), :]], axis=1) for r in at]
+            total = taps_dot(lefts, w2_ref, 256).reshape(16, 16, 128)[:, :8, :].reshape(128, 128)
+            ctx = jnp.where(group == 7 * p, 0.0, total + b2).astype(BF)
             wide = ctx.astype(F32)
-            fine[pl.ds(512 * z + 2 * p, 128, stride=4), :] = wide
-            fine[pl.ds(512 * z + 2 * p + 1, 128, stride=4), :] = pltpu.roll(wide, 64, 1)
+            fine_ref[pl.ds(512 * z + 2 * p, 128, stride=4), :] = wide
+            fine_ref[pl.ds(512 * z + 2 * p + 1, 128, stride=4), :] = pltpu.roll(wide, 64, 1)
             term = dot((cnt0_ref, cnt1_ref)[z][p], ctx)
             sums = term if sums is None else sums + term
-    ctx_ref[...] = fine[...][:, :64].astype(BF)
-    both = sums[:128] + pltpu.roll(sums[128:], 64, 1)
-    send_ref[...] = jnp.where(iota((128, 128), 1) < 64, both, face_ref[...])
-
-
-def convolve(spot, *arrays):
-    return pl.pallas_call(
-        conv_kernel,
+    sums_ref[...] = sums
+
+
+def inner(spot, *arrays):
+    return pl.pallas_call(
+        inner_kernel,
         in_specs=[pl.BlockSpec(memory_space=pltpu.SMEM)] + [pl.BlockSpec(memory_space=pltpu.VMEM)] * len(arrays),
-        out_specs=[pl.BlockSpec(memory_space=pltpu.VMEM)] * 2,
-        out_shape=[jax.ShapeDtypeStruct((1024, 64), BF), pltpu.VMEM((128, 128), F32)],
+        out_specs=[pl.BlockSpec(memory_space=pltpu.VMEM)] * 4,
+        out_shape=[
+            pltpu.VMEM((1024, 128), F32),
+            pltpu.VMEM((256, 128), F32),
+            pltpu.VMEM((2, 144, 128), F32),
+            pltpu.VMEM((2, 96, 128), F32),
+        ],
         scratch_shapes=[
             pltpu.VMEM((HEAD + ROWS1, 128), F32),
             pltpu.VMEM((ROWS1, 128), BF),
             pltpu.VMEM((ROWS1, 128), BF),
             pltpu.VMEM((ROWS2 + 16, 128), F32),
+            pltpu.VMEM((ROWS2, 128), F32),
             pltpu.VMEM((ROWS2, 128), BF),
             pltpu.VMEM((ROWS2, 128), BF),
             pltpu.VMEM((ROWS2, 128), BF),
+        ],
+        compiler_params=pltpu.CompilerParams(vmem_limit_bytes=16 << 20),
+        cost_estimate=pl.CostEstimate(flops=3_000_000_000, bytes_accessed=3_000_000, transcendentals=0),
+        name="inner",
+    )(spot, *arrays)
+
+
+def outer_kernel(spot_ref, xb_ref, xa_ref, ends_ref, near_ref, fine_ref, sums_ref, w1b_ref, b1_ref, w2_ref, b2_ref, cnt0_ref,
+                 cnt1_ref, face_ref, ctx_ref, send_ref, column, hidden, patch, sparse):
+    gz, gy, gx = spot_ref[0], spot_ref[1], spot_ref[2]
+    z_even, y_even, x_even = (gz & 1) == 0, (gy & 1) == 0, (gx & 1) == 0
+    lane = iota((24, 128), 1)
+    column[...] = jnp.zeros_like(column)
+    patch[...] = fine_ref[...]
+    sparse[...] = jnp.zeros_like(sparse)
+    for k, whole in enumerate(ordered(x_even, xa_ref[...].astype(F32), xb_ref[...].astype(F32))):
+        low, high = ordered(z_even, whole[0:2], whole[4:6])
+        for plane, rows in enumerate((low[0], low[1], whole[2], whole[3], high[0], high[1])):
+            first, last = ordered(y_even, rows[16:18], rows[18:20])
+            halo = jnp.concatenate([first, rows[0:16], last, jnp.zeros((4, 128), F32)], axis=0)
+            own = ends_ref[k, pl.ds(24 * plane, 24), :]
+            left, right = (own, halo) if k == 0 else (halo, own)
+            column[k, pl.ds(24 * plane, 24), :] = jnp.where(lane < 64, left, right)
+
+    row, lane = iota((96, 128), 0), iota((96, 128), 1)
+    z_of = jnp.where(row < 24, 0, jnp.where(row < 48, 1, jnp.where(row < 72, 2, 3)))
+    y_of = row - 24 * z_of
+    gone = ((z_of == 0) & (gz == 0)) | ((z_of == 3) & (gz == 7)) | ((y_of == 0) & (gy == 0)) | ((y_of == 17) & (gy == 3))
+    out0 = gone | ((lane < 64) & (gx == 0))
+    out1 = gone | ((lane >= 64) & (gx == 7))
+    at = [24 * (tap // 3) + tap % 3 for tap in range(9)]
+    lefts = [jnp.concatenate([column[k, pl.ds(r, 96), :] for k in range(2)], axis=0).astype(BF) for r in at]
+    total = jnp.maximum(taps_dot(lefts, w1b_ref, 128) + b1_ref[...], 0.0)
+    hidden[0, 0:96] = jnp.where(out0, 0.0, total[0:96])
+    hidden[1, 0:96] = near_ref[0]
+    hidden[2, 0:96] = near_ref[1]
+    hidden[3, 0:96] = jnp.where(out1, 0.0, total[96:192])
+
+    lefts = []
+    for r in at:
+        h = [hidden[k, pl.ds(r, 40), :].astype(BF) for k in range(4)]
+        h = [jnp.concatenate(h[2 * k : 2 * k + 2], axis=1) for k in range(2)]
+        lefts.append(jnp.concatenate(h, axis=0))
+    ctx = (taps_dot(lefts, w2_ref, 256) + b2_ref[...]).astype(BF).astype(F32)
+    for k, (x, g) in enumerate(((0, 0), (30, 7))):
+        for z in range(2):
+            wide = ctx[40 * k + 24 * z : 40 * k + 24 * z + 16]
+            patch[pl.ds(512 * z + x, 16, stride=32), :] = wide
+            patch[pl.ds(512 * z + x + 1, 16, stride=32), :] = pltpu.roll(wide, 64, 1)
+            sparse[pl.ds(128 * (2 * k + z) + g, 16, stride=8), :] = wide
+    left = jnp.concatenate([cnt0_ref[0], cnt1_ref[0], cnt0_ref[1], cnt1_ref[1]], axis=1)
+    sums = sums_ref[...] + dot(left, sparse[...].astype(BF))
+    ctx_ref[...] = patch[...][:, :64].astype(BF)
+    both = sums[:128] + pltpu.roll(sums[128:], 64, 1)
+    send_ref[...] = jnp.where(iota((128, 128), 1) < 64, both, face_ref[...])
+
+
+def outer(spot, *arrays):
+    return pl.pallas_call(
+        outer_kernel,
+        in_specs=[pl.BlockSpec(memory_space=pltpu.SMEM)] + [pl.BlockSpec(memory_space=pltpu.VMEM)] * len(arrays),
+        out_specs=[pl.BlockSpec(memory_space=pltpu.VMEM)] * 2,
+        out_shape=[pltpu.VMEM((1024, 64), BF), pltpu.VMEM((128, 128), F32)],
+        scratch_shapes=[
+            pltpu.VMEM((2, 152, 128), F32),
+            pltpu.VMEM((4, 96, 128), F32),
             pltpu.VMEM((1024, 128), F32),
-        ],
-        compiler_params=pltpu.CompilerParams(vmem_limit_bytes=32 << 20),
-        cost_estimate=pl.CostEstimate(flops=1_000_000_000, bytes_accessed=3_000_000, transcendentals=0),
-        name="convolve",
+            pltpu.VMEM((512, 128), F32),
+        ],
+        compiler_params=pltpu.CompilerParams(vmem_limit_bytes=16 << 20),
+        cost_estimate=pl.CostEstimate(flops=200_000_000, bytes_accessed=3_000_000, transcendentals=0),
+        name="outer",
     )(spot, *arrays)
 
 
-def edge_kernel(rows_ref, emb_ref, ctx_ref):
+def edge_kernel(rows_ref, ctx_ref, edge_emb_ref, edge_ctx_ref, out_ref, sent):
+    copy = pltpu.make_async_copy(ctx_ref, out_ref, sent)
+    copy.start()
     rows = rows_ref[...]
     hits = jnp.where(rows[:, 97:98] == iota((128, 64), 1).astype(F32), 1.0, 0.0).astype(BF)
     sums = sum(dot(part, hits) for part in split3(rows.T))
     scale = jnp.maximum(sums[96:97], 1.0)
-    ctx_ref[...] = sums[:64] / scale
-    emb_ref[...] = sums[64:96] / scale
-
-
-def edges(rows):
+    edge_ctx_ref[...] = sums[:64] / scale
+    edge_emb_ref[...] = sums[64:96] / scale
+    copy.wait()
+
+
+def edges(rows, context):
     return pl.pallas_call(
         edge_kernel,
-        out_shape=[jax.ShapeDtypeStruct((32, 64), F32), jax.ShapeDtypeStruct((64, 64), F32)],
+        in_specs=[pl.BlockSpec(memory_space=pltpu.VMEM)] * 2,
+        out_specs=[pl.BlockSpec(memory_space=pltpu.VMEM)] * 2 + [pl.BlockSpec(memory_space=pl.ANY)],
+        out_shape=[
+            jax.ShapeDtypeStruct((32, 64), F32),
+            jax.ShapeDtypeStruct((64, 64), F32),
+            jax.ShapeDtypeStruct((1024, 64), BF),
+        ],
+        scratch_shapes=[pltpu.SemaphoreType.DMA],
         name="edges",
-    )(rows)
+    )(rows, keep(context))
 
 
 def pairs(first, count):
@@ -352,17 +422,23 @@
         return jnp.concatenate([mid, ya[:, :, g], yb[:, :, g]], axis=1)
 
     low, high = x_edge(0), x_edge(7)
-    xb = lax.ppermute(jnp.where(x_even, low, high), "gx", pairs(1, 8))
-    xa = lax.ppermute(jnp.where(x_even, high, low), "gx", pairs(0, 8))
+    to_b, half, x_even = lax.optimization_barrier((jnp.where(x_even, low, high), half, x_even))
+    xb = lax.ppermute(to_b, "gx", pairs(1, 8))
+    to_a, half = lax.optimization_barrier((jnp.where(x_even, high, low), half))
+    xa = lax.ppermute(to_a, "gx", pairs(0, 8))
     cnt1, face = faces(1, voxels, slot, order, half)
     spot = jnp.stack([gz, gy, gx]).astype(jnp.int32)
     twice = lambda b: jnp.concatenate([b, b]).reshape(1, 128)
-    context, send = convolve(
-        spot, own, za, zb, ya.reshape(96, 128), yb.reshape(96, 128), xa, xb, keep(w1a), keep(w1b), twice(conv1_b),
-        keep(w2a), twice(conv2_b), keep(cnt0), keep(cnt1), keep(face),
+    b1, b2 = twice(conv1_b), twice(conv2_b)
+    w1a, w1b, w2a, cnt0, cnt1 = (keep(a) for a in (w1a, w1b, w2a, cnt0, cnt1))
+    fine, sums, ends, near = inner(
+        spot, own, za, zb, ya.reshape(96, 128), yb.reshape(96, 128), w1a, w1b, b1, w2a, b2, cnt0, cnt1
+    )
+    context, send = outer(
+        spot, xb, xa, keep(ends), keep(near), keep(fine), keep(sums), w1b, b1, w2a, b2, cnt0, cnt1, keep(face)
     )
     rows = lax.all_to_all(send, "gx", 0, 0, tiled=True)
-    edge_emb, edge_ctx = edges(rows)
+    edge_emb, edge_ctx, context = edges(rows, context)
     context = jnp.transpose(context.reshape(2, 16, 32, 64), (3, 0, 1, 2))
     return (context, edge_emb, edge_ctx)
 

time: 52.8 us -> 49.8 us (0.943)
  blocking collectives: 22.7 us -> 18.9 us
  waiting for transfers between devices: 4.65 us -> 2.69 us
  Pallas kernels: 13 us -> 14.2 us
  starting transfers between devices: 10.8 us -> 12 us
    all_to_all x1, blocking collectives: 22.7 us -> 18.9 us  [per_device(): rows = lax.all_to_all(send, 'gx', 0, 0, tiled=True)]
    ppermute x1, waiting for transfers between devices: 1.77 us -> 0.01 us  [per_device(): ya = lax.ppermute(y_edge(y_even), 'gy', pairs(0, 4))]
    pallas_call x2 -> x3, Pallas kernels: 6.27 us -> 7.5 us  [the longest x1 3.88 us: inner(): pl.pallas_call(inner_kernel, in_specs=[pl.BlockSpec(memory_space=pltpu.SM...]
    ppermute x1, starting transfers between devices: 0.09 us -> 0.74 us  [per_device(): ya = lax.ppermute(y_edge(y_even), 'gy', pairs(0, 4))]
    ppermute x1, starting transfers between devices: 3.49 us -> 4.12 us  [per_device(): yb = lax.ppermute(y_edge(jnp.logical_not(y_even)), 'gy', pairs(1, 4))]
  transfers between devices with their start and end apart: 6 -> 6, of which waited for: 4 -> 1; matrix products, arithmetic and copies ran while one was open for 1% -> 1% of each run, Pallas kernels for 8% -> 16%
where the time goes in v4:
time: 49.8 us; the launch traced here: 49.3 us
  blocking collectives  18.9 us (38%)
  Pallas kernels  14.2 us (29%)
  starting transfers between devices  12 us (24%)
  waiting for transfers between devices  2.69 us (5%)
  between operations  1 us (2%)
    all_to_all x1, blocking collectives, per_device(): rows = lax.all_to_all(send, 'gx', 0, 0, tiled=True)  18.9 us
    ppermute x1, starting transfers between devices, per_device(): xa = lax.ppermute(to_a, 'gx', pairs(0, 8))  4.32 us
    ppermute x1, starting transfers between devices, per_device(): yb = lax.ppermute(y_edge(jnp.logical_not(y_even)), 'gy', pairs(1, 4))  4.12 us
    pallas_call x1, Pallas kernels, inner(): pl.pallas_call(inner_kernel, in_specs=[pl.BlockSpec(memory_space=pltpu.SM...  3.88 us
    pallas_call x2, Pallas kernels, faces(): pl.pallas_call(functools.partial(face_kernel, half), in_specs=[pl.BlockSp...  3.68 us
    ppermute x1, waiting for transfers between devices, per_device(): zb = lax.ppermute(own, 'gz', pairs(1, 8))  2.68 us
    pallas_call x1, Pallas kernels, pool(): pl.pallas_call(pool_kernel, in_specs=[pl.BlockSpec(memory_space=pl.ANY)],...  2.57 us
    pallas_call x1, Pallas kernels, edges(): pl.pallas_call(edge_kernel, in_specs=[pl.BlockSpec(memory_space=pltpu.VME...  2.17 us
  transfers between devices with their start and end apart: 6, of which 1 were waited for; matrix products, arithmetic and copies ran while one was open for 1% of the time, Pallas kernels for 16%

profile of v4, /device:TPU:40, one launch (start us, length us, event | category | flops | bytes accessed | tf_op | source)
XLA Modules:
  0.0 49.3 jit_solution(16933738125998830265)
XLA Ops:
  0.6 0.0 copy-start.4
  0.6 0.0 copy-start.5
  0.7 0.0 copy-start.3
  0.7 0.0 copy-start.1
  0.7 0.0 copy-start
  0.7 2.6 %pool.1 = (bf16[256,128]{1,0:T(8,128)(2,1)S(1)}, bf16[32,256,128]{2,1,0:T(8,128)(2,1)S(1)}) custom-call(bf16[32,256,128]{2,1,0:T(8,128)(2,1)} %bitcast.60), custom_call_target="tpu_custom_call" | custom-call | flops 80000000 | bytes 2200000 | tf_op jit(solution)/shard_map/pool/pallas_call | solution.py:76
  3.3 0.1 collective-permute-start
  3.4 2.1 %collective-permute-start.1 = (bf16[256,128]{1,0:T(8,128)(2,1)S(1)}, bf16[256,128]{1,0:T(8,128)(2,1)S(1)}, u32[]{:S(2)}, u32[]{:S(2)}) collective-permute-start(bf16[256,128]{1,0:T(8,128)(2,1)S(1)} %get-tuple-element.33.own_ref), channel_id=1, source_target_pairs={{32,64},{64,32},{96,128},{128,96},{160,192},{192,160},{33,65},{65,... | collective-permute-start | bytes 196616 | tf_op jit(solution)/shard_map/ppermute | solution.py:400
  5.6 0.0 copy-done.4
  5.6 0.0 copy-done.5
  5.6 0.1 maximum_bitcast_fusion
  5.7 0.1 pad_add_fusion.spot_ref
  5.8 0.0 copy-done.3
  5.8 0.0 copy-done.1
  5.8 0.0 copy-done
  5.8 0.0 copy-start.2
  5.8 0.5 prepare.1
  6.3 0.0 collective-permute-done.za_ref
  6.3 2.7 %collective-permute-done.1.zb_ref = bf16[256,128]{1,0:T(8,128)(2,1)S(1)} collective-permute-done((bf16[256,128]{1,0:T(8,128)(2,1)S(1)}, bf16[256,128]{1,0:T(8,128)(2,1)S(1)}, u32[]{:S(2)}, u32[]{:S(2)}) %collective-permute-start.1) | collective-permute-done | bytes 65568 | tf_op jit(solution)/shard_map/ppermute | solution.py:400
  9.1 0.7 %collective-permute-start.2 = (bf16[6,2,8,128]{3,1,0,2:T(2,128)(2,1)S(1)}, bf16[6,2,8,128]{3,1,0,2:T(2,128)(2,1)S(1)}, u32[]{:S(2)}, u32[]{:S(2)}) collective-permute-start(bf16[6,2,8,128]{3,1,0,2:T(2,128)(2,1)S(1)} %pad_maximum_fusion.2), channel_id=1, source_target_pairs={{0,8},{8,0},{16,24},{24,16},{1,9},{9,1},{17,25},{25,17},{2,10},{10... | collective-permute-start | bytes 73736 | tf_op jit(solution)/shard_map/ppermute | solution.py:416
  9.9 4.1 %collective-permute-start.3 = (bf16[6,2,8,128]{3,1,0,2:T(2,128)(2,1)S(1)}, bf16[6,2,8,128]{3,1,0,2:T(2,128)(2,1)S(1)}, u32[]{:S(2)}, u32[]{:S(2)}) collective-permute-start(bf16[6,2,8,128]{3,1,0,2:T(2,128)(2,1)S(1)} %pad_maximum_fusion.3), channel_id=1, source_target_pairs={{8,16},{16,8},{9,17},{17,9},{10,18},{18,10},{11,19},{19,11},{12,20... | collective-permute-start | bytes 73736 | tf_op jit(solution)/shard_map/ppermute | solution.py:415
  14.1 0.0 copy-done.2
  14.1 1.9 %faces.2 = (bf16[2,256,128]{2,1,0:T(8,128)(2,1)S(1)}, f32[40,128]{1,0:T(8,128)S(1)}) custom-call(bf16[32,256,128]{2,1,0:T(8,128)(2,1)S(1)} %get-tuple-element.37.emb_ref, s32[256,128]{1,0:T(8,128)S(1)} %bitcast.57, f32[2,128,128]{2,1,0:T(8,128)S(1)} %get-tuple-element.38.order_ref, f32[40,128]{1,0:T(8,128)S(1)} %slice_bitcast_fusion.before_ref), custom_call_target="tpu_custom_call" | custom-call | flops 2000000000 | bytes 4000000 | tf_op jit(solution)/shard_map/faces/pallas_call | solution.py:166
  16.0 0.0 collective-permute-done.2
  16.0 0.0 collective-permute-done.3
  16.1 0.7 %collective-permute-start.4 = (bf16[6,20,128]{2,1,0:T(8,128)(2,1)S(1)}, bf16[6,20,128]{2,1,0:T(8,128)(2,1)S(1)}, u32[]{:S(2)}, u32[]{:S(2)}) collective-permute-start(bf16[6,20,128]{2,1,0:T(8,128)(2,1)S(1)} %broadcast_select_fusion.1), channel_id=1, source_target_pairs={{1,2},{2,1},{3,4},{4,3},{5,6},{6,5},{9,10},{10,9},{11,12},{12,11},... | collective-permute-start | bytes 92168 | tf_op jit(solution)/shard_map/ppermute | solution.py:426
  16.8 4.3 %collective-permute-start.5 = (bf16[6,20,128]{2,1,0:T(8,128)(2,1)S(1)}, bf16[6,20,128]{2,1,0:T(8,128)(2,1)S(1)}, u32[]{:S(2)}, u32[]{:S(2)}) collective-permute-start(bf16[6,20,128]{2,1,0:T(8,128)(2,1)S(1)} %broadcast_select_fusion), channel_id=1, source_target_pairs={{0,1},{1,0},{2,3},{3,2},{4,5},{5,4},{6,7},{7,6},{8,9},{9,8},{10,11... | collective-permute-start | bytes 92168 | tf_op jit(solution)/shard_map/ppermute | solution.py:428
  21.1 1.8 %faces.3 = (bf16[2,256,128]{2,1,0:T(8,128)(2,1)S(1)}, f32[128,128]{1,0:T(8,128)S(1)}) custom-call(bf16[32,256,128]{2,1,0:T(8,128)(2,1)S(1)} %get-tuple-element.37.emb_ref, s32[256,128]{1,0:T(8,128)S(1)} %bitcast.58, f32[2,128,128]{2,1,0:T(8,128)S(1)} %get-tuple-element.38.order_ref, f32[40,128]{1,0:T(8,128)S(1)} %get-tuple-element.51.before_ref), custom_call_target="tpu_custom_call" | custom-call | flops 2000000000 | bytes 4000000 | tf_op jit(solution)/shard_map/faces/pallas_call | solution.py:166
  22.9 3.9 %inner.1 = (f32[1024,128]{1,0:T(8,128)S(1)}, f32[256,128]{1,0:T(8,128)S(1)}, f32[2,144,128]{2,1,0:T(8,128)S(1)}, f32[2,96,128]{2,1,0:T(8,128)S(1)}) custom-call(s32[3]{0:T(128)S(1)} %pad_add_fusion.spot_ref, bf16[256,128]{1,0:T(8,128)(2,1)S(1)} %get-tuple-element.33.own_ref, bf16[256,128]{1,0:T(8,128)(2,1)S(1)} %collective-permute-done.za_ref, ...), custom_call_target="tpu_custom_call" | custom-call | flops 3000000000 | bytes 3000000 | tf_op jit(solution)/shard_map/inner/pallas_call | solution.py:270
  26.8 0.0 collective-permute-done.4.xb_ref
  26.8 0.0 collective-permute-done.5.xa_ref
  26.8 1.4 %outer.1 = (bf16[1024,64]{1,0:T(8,128)(2,1)S(1)}, f32[128,128]{1,0:T(8,128)S(1)}) custom-call(s32[3]{0:T(128)S(1)} %pad_add_fusion.spot_ref, bf16[6,20,128]{2,1,0:T(8,128)(2,1)S(1)} %collective-permute-done.4.xb_ref, bf16[6,20,128]{2,1,0:T(8,128)(2,1)S(1)} %collective-permute-done.5.xa_ref, f32[2,144,128]{2,1,0:T(8,128)S(1)} %get-tuple-element.53.ends_ref, ...), custom_call_target="tpu_custom_call" | custom-call | flops 200000000 | bytes 3000000 | tf_op jit(solution)/shard_map/outer/pallas_call | solution.py:347
  28.3 18.9 %all_to_all.11 = f32[8,16,128]{2,1,0:T(8,128)} all-to-all(f32[8,16,128]{2,1,0:T(8,128)S(1)} %bitcast.46), channel_id=1, replica_groups=mesh['gz'=8,'gy'=4,'gx'=8] {'gx'}, dimensions={0} | all-to-all | bytes 131072 | tf_op jit(solution)/shard_map/all_to_all | solution.py:440
  47.2 2.2 %edges.1 = (f32[32,64]{1,0:T(8,128)}, f32[64,64]{1,0:T(8,128)}, bf16[1024,64]{1,0:T(8,128)(2,1)}) custom-call(f32[128,128]{1,0:T(8,128)} %bitcast.61, bf16[1024,64]{1,0:T(8,128)(2,1)S(1)} %get-tuple-element.59.ctx_ref), custom_call_target="tpu_custom_call" | custom-call | tf_op jit(solution)/shard_map/edges/pallas_call | solution.py:377
  (23 shorter events, 0.3 us)
Async XLA Ops:
  0.6 5.0 %copy-start.4 = (f32[64]{0:T(128)S(1)}, f32[64]{0:T(128)}, u32[]{:S(2)}) copy-start(f32[64]{0:T(128)} %param.11) | copy-start | bytes 772
  0.6 5.0 %copy-start.5 = (f32[64]{0:T(128)S(1)}, f32[64]{0:T(128)}, u32[]{:S(2)}) copy-start(f32[64]{0:T(128)} %param.13) | copy-start | bytes 772
  0.7 5.1 %copy-start.3 = (s32[128]{0:T(128)S(1)}, s32[128]{0:T(128)}, u32[]{:S(2)}) copy-start(s32[128]{0:T(128)} %param.9) | copy-start | bytes 1540
  0.7 5.1 %copy-start.1 = (bf16[3,3,3,64,32]{3,4,2,1,0:T(8,128)(2,1)S(1)}, bf16[3,3,3,64,32]{3,4,2,1,0:T(8,128)(2,1)}, u32[]{:S(2)}) copy-start(bf16[3,3,3,64,32]{3,4,2,1,0:T(8,128)(2,1)} %param.10) | copy-start | bytes 331780
  0.7 5.1 %copy-start = (bf16[3,3,3,64,64]{4,3,2,1,0:T(8,128)(2,1)S(1)}, bf16[3,3,3,64,64]{4,3,2,1,0:T(8,128)(2,1)}, u32[]{:S(2)}) copy-start(bf16[3,3,3,64,64]{4,3,2,1,0:T(8,128)(2,1)} %param.12) | copy-start | bytes 663556
  3.3 3.0 %collective-permute-start = (bf16[256,128]{1,0:T(8,128)(2,1)S(1)}, bf16[256,128]{1,0:T(8,128)(2,1)S(1)}, u32[]{:S(2)}, u32[]{:S(2)}) collective-permute-start(bf16[256,128]{1,0:T(8,128)(2,1)S(1)} %get-tuple-element.33.own_ref), channel_id=1, source_target_pairs={{0,32},{32,0},{64,96},{96,64},{128,160},{160,128},{192,224},{224,1... | collective-permute-start | bytes 196616 | tf_op jit(solution)/shard_map/ppermute | solution.py:401
  3.4 5.6 %collective-permute-start.1 = (bf16[256,128]{1,0:T(8,128)(2,1)S(1)}, bf16[256,128]{1,0:T(8,128)(2,1)S(1)}, u32[]{:S(2)}, u32[]{:S(2)}) collective-permute-start(bf16[256,128]{1,0:T(8,128)(2,1)S(1)} %get-tuple-element.33.own_ref), channel_id=1, source_target_pairs={{32,64},{64,32},{96,128},{128,96},{160,192},{192,160},{33,65},{65,... | collective-permute-start | bytes 196616 | tf_op jit(solution)/shard_map/ppermute | solution.py:400
  5.8 8.3 %copy-start.2 = (s32[4,64,128]{2,1,0:T(8,128)S(1)}, s32[4,64,128]{2,1,0:T(8,128)}, u32[]{:S(2)}) copy-start(s32[4,64,128]{2,1,0:T(8,128)} %param.8) | copy-start | bytes 393220
  9.1 6.9 %collective-permute-start.2 = (bf16[6,2,8,128]{3,1,0,2:T(2,128)(2,1)S(1)}, bf16[6,2,8,128]{3,1,0,2:T(2,128)(2,1)S(1)}, u32[]{:S(2)}, u32[]{:S(2)}) collective-permute-start(bf16[6,2,8,128]{3,1,0,2:T(2,128)(2,1)S(1)} %pad_maximum_fusion.2), channel_id=1, source_target_pairs={{0,8},{8,0},{16,24},{24,16},{1,9},{9,1},{17,25},{25,17},{2,10},{10... | collective-permute-start | bytes 73736 | tf_op jit(solution)/shard_map/ppermute | solution.py:416
  9.9 6.1 %collective-permute-start.3 = (bf16[6,2,8,128]{3,1,0,2:T(2,128)(2,1)S(1)}, bf16[6,2,8,128]{3,1,0,2:T(2,128)(2,1)S(1)}, u32[]{:S(2)}, u32[]{:S(2)}) collective-permute-start(bf16[6,2,8,128]{3,1,0,2:T(2,128)(2,1)S(1)} %pad_maximum_fusion.3), channel_id=1, source_target_pairs={{8,16},{16,8},{9,17},{17,9},{10,18},{18,10},{11,19},{19,11},{12,20... | collective-permute-start | bytes 73736 | tf_op jit(solution)/shard_map/ppermute | solution.py:415
  16.1 10.7 %collective-permute-start.4 = (bf16[6,20,128]{2,1,0:T(8,128)(2,1)S(1)}, bf16[6,20,128]{2,1,0:T(8,128)(2,1)S(1)}, u32[]{:S(2)}, u32[]{:S(2)}) collective-permute-start(bf16[6,20,128]{2,1,0:T(8,128)(2,1)S(1)} %broadcast_select_fusion.1), channel_id=1, source_target_pairs={{1,2},{2,1},{3,4},{4,3},{5,6},{6,5},{9,10},{10,9},{11,12},{12,11},... | collective-permute-start | bytes 92168 | tf_op jit(solution)/shard_map/ppermute | solution.py:426
  16.8 10.0 %collective-permute-start.5 = (bf16[6,20,128]{2,1,0:T(8,128)(2,1)S(1)}, bf16[6,20,128]{2,1,0:T(8,128)(2,1)S(1)}, u32[]{:S(2)}, u32[]{:S(2)}) collective-permute-start(bf16[6,20,128]{2,1,0:T(8,128)(2,1)S(1)} %broadcast_select_fusion), channel_id=1, source_target_pairs={{0,1},{1,0},{2,3},{3,2},{4,5},{5,4},{6,7},{7,6},{8,9},{9,8},{10,11... | collective-permute-start | bytes 92168 | tf_op jit(solution)/shard_map/ppermute | solution.py:428

commit v5 on v4

--- a/solution.py
+++ b/solution.py
@@ -51,16 +51,16 @@
     row, col = iota((32, 256), 0), iota((32, 256), 1)
     cell = ((col >> 7) << 4) + ((col & 63) >> 2)
     pool_zy = jnp.where(cell == row, 1.0, 0.0).astype(BF)
-    pool_x = pool_x_matrix()
+    pool_x = jnp.concatenate([pool_x_matrix()] * 3, axis=1)
     lane = iota((8, 128), 1)
     far, near = lane < 64, (lane & 32) == 0
     for i in range(chunks):
         copies[i].wait()
         for c in range(per * i, per * i + per):
-            sums[c] = dot(pool_zy, block[c])
+            sums[pl.ds(32 * c, 32), :] = dot(pool_zy, block[c])
     for part in range(8):
-        rows = jnp.concatenate([sums[:, 4 * part + i, :] for i in range(4)], axis=0)
-        cells = sum(dot(pool_x, term, NT) for term in split3(rows)) * (1.0 / 32.0)
+        rows = jnp.concatenate([sums[pl.ds(4 * part + i, 32, stride=32), :] for i in range(4)], axis=0)
+        cells = dot(pool_x, jnp.concatenate(split3(rows), axis=1), NT) * (1.0 / 32.0)
         v = [cells[8 * i : 8 * i + 8] for i in range(4)]
         a = [jnp.where(far, v[i], pltpu.roll(v[i + 2], 64, 1)) for i in range(2)]
         b = [jnp.where(far, pltpu.roll(v[i], 64, 1), v[i + 2]) for i in range(2)]
@@ -79,7 +79,7 @@
         out_specs=[pl.BlockSpec(memory_space=pltpu.VMEM)] * 2,
         out_shape=[pltpu.VMEM((256, 128), BF), pltpu.VMEM((32, 256, 128), BF)],
         scratch_shapes=[
-            pltpu.VMEM((32, 32, 128), F32),
+            pltpu.VMEM((1024, 128), F32),
             pltpu.SemaphoreType.DMA((chunks,)),
         ],
         compiler_params=pltpu.CompilerParams(vmem_limit_bytes=32 << 20),
@@ -126,7 +126,7 @@
             pltpu.VMEM((2304, 128), BF),
         ],
         compiler_params=pltpu.CompilerParams(vmem_limit_bytes=16 << 20),
-        cost_estimate=pl.CostEstimate(flops=1_000_000_000, bytes_accessed=2_000_000, transcendentals=0),
+        cost_estimate=pl.CostEstimate(flops=1_000_000, bytes_accessed=10_000, transcendentals=0),
         name="prepare",
     )(edge, w1, w2)
 
@@ -170,14 +170,14 @@
         out_shape=[pltpu.VMEM((2, 256, 128), BF), pltpu.VMEM((128 if half else 40, 128), F32)],
         scratch_shapes=[pltpu.VMEM((4096, 128), F32), pltpu.VMEM((4, 128, 128), F32)],
         compiler_params=pltpu.CompilerParams(vmem_limit_bytes=16 << 20),
-        cost_estimate=pl.CostEstimate(flops=2_000_000_000, bytes_accessed=4_000_000, transcendentals=0),
+        cost_estimate=pl.CostEstimate(flops=1_000_000, bytes_accessed=10_000, transcendentals=0),
         name="faces",
     )(keep(emb), slot, keep(order), keep(before))
 
 
-ROWS1 = 6 * 20 * 16
-ROWS2 = 4 * 18 * 16
-HEAD = 16
+ROWS1 = 6 * 20 * 8
+ROWS2 = 4 * 18 * 8
+HEAD = 8
 
 
 def ordered(even, a, b):
@@ -195,9 +195,13 @@
     return total
 
 
-def inner_kernel(spot_ref, own_ref, za_ref, zb_ref, ya_ref, yb_ref, w1a_ref, w1b_ref, b1_ref, w2_ref, b2_ref, cnt0_ref,
+def window(source, tap, z, plane, rows):
+    return source[tap % 3 & 1, pl.ds((z + tap // 3) * plane + 16 * (tap % 3 >> 1), rows), :]
+
+
+def inner_kernel(own_ref, za_ref, zb_ref, ya_ref, yb_ref, w1a_ref, w1b_ref, b1_ref, w2_ref, b2_ref, cnt0_ref,
                  cnt1_ref, fine_ref, sums_ref, ends_ref, near_ref, field, this, mixed, h0f, h1f, h0b, h0n, h1b):
-    gz, gy = spot_ref[0], spot_ref[1]
+    gz, gy = lax.axis_index("gz"), lax.axis_index("gy")
     z_even, y_even = (gz & 1) == 0, (gy & 1) == 0
     z_low, z_high = ordered(z_even, za_ref[...].astype(F32), zb_ref[...].astype(F32))
     zs = (z_low, own_ref[...].astype(F32), z_high)
@@ -206,32 +210,30 @@
     for whole in ordered(y_even, ya, yb):
         low, high = ordered(z_even, whole[0:32], whole[64:96])
         ys.append((low, whole[32:64], high))
-    for part in range(3):
-        for i in range(2):
-            plane = 2 * part + i
-            base = HEAD + plane * 320
-            for y in range(16):
-                field[pl.ds(base + 32 + 16 * y, 8), :] = zs[part][128 * i + 8 * y : 128 * i + 8 * y + 8]
-            for y in range(2):
-                field[pl.ds(base + 16 * y, 8), :] = ys[0][part][16 * i + 8 * y : 16 * i + 8 * y + 8]
-                field[pl.ds(base + 288 + 16 * y, 8), :] = ys[1][part][16 * i + 8 * y : 16 * i + 8 * y + 8]
-            for k, g in enumerate((0, 7)):
-                ends_ref[k, pl.ds(24 * plane, 20), :] = field[pl.ds(base + g, 20, stride=16), :]
-
-    lane = iota((320, 128), 1)
+    for plane in range(6):
+        part, i = plane // 2, plane % 2
+        base = HEAD + plane * 160
+        field[pl.ds(base, 16), :] = ys[0][part][16 * i : 16 * i + 16]
+        field[pl.ds(base + 16, 128), :] = zs[part][128 * i : 128 * i + 128]
+        field[pl.ds(base + 144, 16), :] = ys[1][part][16 * i : 16 * i + 16]
+        for k, g in enumerate((0, 7)):
+            ends_ref[k, pl.ds(24 * plane, 20), :] = field[pl.ds(base + g, 20, stride=8), :]
+
+    lane = iota((160, 128), 1)
     for z in range(6):
-        now = field[pl.ds(HEAD + 320 * z, 320), :]
-        before = field[pl.ds(HEAD + 320 * z - 1, 320), :]
-        this[pl.ds(320 * z, 320), :] = now.astype(BF)
-        mixed[pl.ds(320 * z, 320), :] = jnp.where(lane < 64, now, before).astype(BF)
-
-    row = iota((288, 128), 0)
-    stay = jnp.where((row < 16) & (gy == 0), 0.0, 1.0)
-    stay = jnp.where((row >= 272) & (gy == 3), 0.0, stay)
+        for shift in range(2):
+            now = field[pl.ds(HEAD + 160 * z + 8 * shift, 160), :]
+            before = field[pl.ds(HEAD + 160 * z + 8 * shift - 1, 160), :]
+            this[shift, pl.ds(160 * z, 160), :] = now.astype(BF)
+            mixed[shift, pl.ds(160 * z, 160), :] = jnp.where(lane < 64, now, before).astype(BF)
+
+    row = iota((144, 128), 0)
+    stay = jnp.where((row < 8) & (gy == 0), 0.0, 1.0)
+    stay = jnp.where((row >= 136) & (gy == 3), 0.0, stay)
     b1, b2 = b1_ref[...], b2_ref[...]
 
     def conv1(source, weights, z):
-        lefts = [source[pl.ds(((z + tap // 3) * 20 + tap % 3) * 16, 288), :] for tap in range(9)]
+        lefts = [window(source, tap, z, 160, 144) for tap in range(9)]
         return jnp.maximum(taps_dot(lefts, weights, 128) + b1, 0.0)
 
     for z in range(4):
@@ -240,24 +242,27 @@
             inside = jnp.where(gz == 0, 0.0, 1.0)
         if z == 3:
             inside = jnp.where(gz == 7, 0.0, 1.0)
-        h0f[pl.ds(288 * z, 288), :] = conv1(mixed, w1b_ref, z) * (stay * inside)
-        h1 = conv1(this, w1a_ref, z) * (stay * inside)
-        h1f[pl.ds(288 * z, 288), :] = h1
-        h1b[pl.ds(288 * z, 288), :] = h1.astype(BF)
+        h0f[pl.ds(144 * z, 144), :] = conv1(mixed, w1b_ref, z) * (stay * inside)
+        h1f[pl.ds(144 * z, 144), :] = conv1(this, w1a_ref, z) * (stay * inside)
+    for z in range(4):
         for k, g in enumerate((0, 7)):
-            near_ref[k, pl.ds(24 * z, 18), :] = h1f[pl.ds(288 * z + g, 18, stride=16), :]
-    for z in range(4):
-        h0b[pl.ds(288 * z, 288), :] = h0f[pl.ds(288 * z, 288), :].astype(BF)
-        h0n[pl.ds(288 * z, 288), :] = h0f[pl.ds(288 * z + 1, 288), :].astype(BF)
+            near_ref[k, pl.ds(24 * z, 18), :] = h1f[pl.ds(144 * z + g, 18, stride=8), :]
+        for shift in range(2):
+            at = 144 * z + 8 * shift
+            h0b[shift, pl.ds(144 * z, 144), :] = h0f[pl.ds(at, 144), :].astype(BF)
+            h0n[shift, pl.ds(144 * z, 144), :] = h0f[pl.ds(at + 1, 144), :].astype(BF)
+            h1b[shift, pl.ds(144 * z, 144), :] = h1f[pl.ds(at, 144), :].astype(BF)
 
     group = iota((128, 128), 0) & 7
     sums = None
     for z in range(2):
-        for p, (first, second) in enumerate(((h0b, h1b), (h1b, h0n))):
-            at = [((z + tap // 3) * 18 + tap % 3) * 16 for tap in range(9)]
-            lefts = [jnp.concatenate([first[pl.ds(r, 256), :], second[pl.ds(r, 256), :]], axis=1) for r in at]
-            total = taps_dot(lefts, w2_ref, 256).reshape(16, 16, 128)[:, :8, :].reshape(128, 128)
-            ctx = jnp.where(group == 7 * p, 0.0, total + b2).astype(BF)
+        lefts = []
+        for tap in range(9):
+            h = [window(source, tap, z, 144, 128) for source in (h0b, h1b, h0n)]
+            lefts.append(jnp.concatenate([jnp.concatenate(h[p : p + 2], axis=1) for p in range(2)], axis=0))
+        both = taps_dot(lefts, w2_ref, 256) + b2
+        for p in range(2):
+            ctx = jnp.where(group == 7 * p, 0.0, both[128 * p : 128 * p + 128]).astype(BF)
             wide = ctx.astype(F32)
             fine_ref[pl.ds(512 * z + 2 * p, 128, stride=4), :] = wide
             fine_ref[pl.ds(512 * z + 2 * p + 1, 128, stride=4), :] = pltpu.roll(wide, 64, 1)
@@ -266,10 +271,10 @@
     sums_ref[...] = sums
 
 
-def inner(spot, *arrays):
+def inner(*arrays):
     return pl.pallas_call(
         inner_kernel,
-        in_specs=[pl.BlockSpec(memory_space=pltpu.SMEM)] + [pl.BlockSpec(memory_space=pltpu.VMEM)] * len(arrays),
+        in_specs=[pl.BlockSpec(memory_space=pltpu.VMEM)] * len(arrays),
         out_specs=[pl.BlockSpec(memory_space=pltpu.VMEM)] * 4,
         out_shape=[
             pltpu.VMEM((1024, 128), F32),
@@ -278,24 +283,24 @@
             pltpu.VMEM((2, 96, 128), F32),
         ],
         scratch_shapes=[
-            pltpu.VMEM((HEAD + ROWS1, 128), F32),
-            pltpu.VMEM((ROWS1, 128), BF),
-            pltpu.VMEM((ROWS1, 128), BF),
+            pltpu.VMEM((HEAD + ROWS1 + 8, 128), F32),
+            pltpu.VMEM((2, ROWS1, 128), BF),
+            pltpu.VMEM((2, ROWS1, 128), BF),
             pltpu.VMEM((ROWS2 + 16, 128), F32),
-            pltpu.VMEM((ROWS2, 128), F32),
-            pltpu.VMEM((ROWS2, 128), BF),
-            pltpu.VMEM((ROWS2, 128), BF),
-            pltpu.VMEM((ROWS2, 128), BF),
+            pltpu.VMEM((ROWS2 + 16, 128), F32),
+            pltpu.VMEM((2, ROWS2, 128), BF),
+            pltpu.VMEM((2, ROWS2, 128), BF),
+            pltpu.VMEM((2, ROWS2, 128), BF),
         ],
         compiler_params=pltpu.CompilerParams(vmem_limit_bytes=16 << 20),
-        cost_estimate=pl.CostEstimate(flops=3_000_000_000, bytes_accessed=3_000_000, transcendentals=0),
+        cost_estimate=pl.CostEstimate(flops=1_000_000, bytes_accessed=10_000, transcendentals=0),
         name="inner",
-    )(spot, *arrays)
-
-
-def outer_kernel(spot_ref, xb_ref, xa_ref, ends_ref, near_ref, fine_ref, sums_ref, w1b_ref, b1_ref, w2_ref, b2_ref, cnt0_ref,
+    )(*arrays)
+
+
+def outer_kernel(xb_ref, xa_ref, ends_ref, near_ref, fine_ref, sums_ref, w1b_ref, b1_ref, w2_ref, b2_ref, cnt0_ref,
                  cnt1_ref, face_ref, ctx_ref, send_ref, column, hidden, patch, sparse):
-    gz, gy, gx = spot_ref[0], spot_ref[1], spot_ref[2]
+    gz, gy, gx = (lax.axis_index(a) for a in ("gz", "gy", "gx"))
     z_even, y_even, x_even = (gz & 1) == 0, (gy & 1) == 0, (gx & 1) == 0
     lane = iota((24, 128), 1)
     column[...] = jnp.zeros_like(column)
@@ -343,10 +348,10 @@
     send_ref[...] = jnp.where(iota((128, 128), 1) < 64, both, face_ref[...])
 
 
-def outer(spot, *arrays):
+def outer(*arrays):
     return pl.pallas_call(
         outer_kernel,
-        in_specs=[pl.BlockSpec(memory_space=pltpu.SMEM)] + [pl.BlockSpec(memory_space=pltpu.VMEM)] * len(arrays),
+        in_specs=[pl.BlockSpec(memory_space=pltpu.VMEM)] * len(arrays),
         out_specs=[pl.BlockSpec(memory_space=pltpu.VMEM)] * 2,
         out_shape=[pltpu.VMEM((1024, 64), BF), pltpu.VMEM((128, 128), F32)],
         scratch_shapes=[
@@ -358,7 +363,7 @@
         compiler_params=pltpu.CompilerParams(vmem_limit_bytes=16 << 20),
         cost_estimate=pl.CostEstimate(flops=200_000_000, bytes_accessed=3_000_000, transcendentals=0),
         name="outer",
-    )(spot, *arrays)
+    )(*arrays)
 
 
 def edge_kernel(rows_ref, ctx_ref, edge_emb_ref, edge_ctx_ref, out_ref, sent):
@@ -385,7 +390,7 @@
         ],
         scratch_shapes=[pltpu.SemaphoreType.DMA],
         name="edges",
-    )(rows, keep(context))
+    )(keep(rows), keep(context))
 
 
 def pairs(first, count):
@@ -394,7 +399,7 @@
 
 def per_device(embedding, face_slot, face_edge, conv1_w, conv1_b, conv2_w, conv2_b):
     emb = embedding.reshape(32, 256, 128)
-    gz, gy, gx = (lax.axis_index(a) for a in ("gz", "gy", "gx"))
+    gy, gx = lax.axis_index("gy"), lax.axis_index("gx")
     slot = face_slot.reshape(256, 128)
     own, voxels = pool(emb)
     zb = lax.ppermute(own, "gz", pairs(1, 8))
@@ -412,8 +417,9 @@
         first = jnp.where(high, 14, 0)
         return jnp.concatenate([lax.dynamic_slice_in_dim(a, first, 2, axis=1) for a in planes], axis=0)
 
-    yb = lax.ppermute(y_edge(jnp.logical_not(y_even)), "gy", pairs(1, 4))
-    ya = lax.ppermute(y_edge(y_even), "gy", pairs(0, 4))
+    to_a, to_b = lax.optimization_barrier((y_edge(y_even), y_edge(jnp.logical_not(y_even))))
+    ya = lax.ppermute(to_a, "gy", pairs(0, 4))
+    yb = lax.ppermute(to_b, "gy", pairs(1, 4))
     cnt0, half = faces(0, voxels, slot, order, order[0, :40])
     ya, yb, half = lax.optimization_barrier((ya, yb, half))
 
@@ -422,20 +428,18 @@
         return jnp.concatenate([mid, ya[:, :, g], yb[:, :, g]], axis=1)
 
     low, high = x_edge(0), x_edge(7)
-    to_b, half, x_even = lax.optimization_barrier((jnp.where(x_even, low, high), half, x_even))
+    to_b, to_a, half = lax.optimization_barrier((jnp.where(x_even, low, high), jnp.where(x_even, high, low), half))
+    xa = lax.ppermute(to_a, "gx", pairs(0, 8))
     xb = lax.ppermute(to_b, "gx", pairs(1, 8))
-    to_a, half = lax.optimization_barrier((jnp.where(x_even, high, low), half))
-    xa = lax.ppermute(to_a, "gx", pairs(0, 8))
     cnt1, face = faces(1, voxels, slot, order, half)
-    spot = jnp.stack([gz, gy, gx]).astype(jnp.int32)
     twice = lambda b: jnp.concatenate([b, b]).reshape(1, 128)
     b1, b2 = twice(conv1_b), twice(conv2_b)
     w1a, w1b, w2a, cnt0, cnt1 = (keep(a) for a in (w1a, w1b, w2a, cnt0, cnt1))
     fine, sums, ends, near = inner(
-        spot, own, za, zb, ya.reshape(96, 128), yb.reshape(96, 128), w1a, w1b, b1, w2a, b2, cnt0, cnt1
+        own, za, zb, ya.reshape(96, 128), yb.reshape(96, 128), w1a, w1b, b1, w2a, b2, cnt0, cnt1
     )
     context, send = outer(
-        spot, xb, xa, keep(ends), keep(near), keep(fine), keep(sums), w1b, b1, w2a, b2, cnt0, cnt1, keep(face)
+        xb, xa, keep(ends), keep(near), keep(fine), keep(sums), w1b, b1, w2a, b2, cnt0, cnt1, keep(face)
     )
     rows = lax.all_to_all(send, "gx", 0, 0, tiled=True)
     edge_emb, edge_ctx, context = edges(rows, context)

time: 49.8 us -> 48.2 us (0.968)
  Pallas kernels: 14.2 us -> 10.8 us
  blocking collectives: 18.9 us -> 20.6 us
    pallas_call x2, Pallas kernels: 5.33 us -> 2.91 us  [the longest x1 2.02 us: inner(): pl.pallas_call(inner_kernel, in_specs=[pl.BlockSpec(memory_space=pltpu.VM...]
    all_to_all x1, blocking collectives: 18.9 us -> 20.6 us  [per_device(): rows = lax.all_to_all(send, 'gx', 0, 0, tiled=True)]
    pallas_call x1, Pallas kernels: 2.17 us -> 1.33 us  [edges(): pl.pallas_call(edge_kernel, in_specs=[pl.BlockSpec(memory_space=pltpu.VME...]
  transfers between devices with their start and end apart: 6 -> 6, of which waited for: 1 -> 1; matrix products, arithmetic and copies ran while one was open for 1% -> 0% of each run, Pallas kernels for 16% -> 13%
where the time goes in v5:
time: 48.2 us; the launch traced here: 47.7 us
  blocking collectives  20.6 us (43%)
  starting transfers between devices  12 us (25%)
  Pallas kernels  10.8 us (22%)
  waiting for transfers between devices  2.86 us (6%)
  between operations  1 us (2%)
    all_to_all x1, blocking collectives, per_device(): rows = lax.all_to_all(send, 'gx', 0, 0, tiled=True)  20.6 us
    ppermute x1, starting transfers between devices, per_device(): xa = lax.ppermute(to_a, 'gx', pairs(0, 8))  4.31 us
    ppermute x1, starting transfers between devices, per_device(): yb = lax.ppermute(to_b, 'gy', pairs(1, 4))  4.11 us
    pallas_call x2, Pallas kernels, faces(): pl.pallas_call(functools.partial(face_kernel, half), in_specs=[pl.BlockSp...  3.68 us
    ppermute x1, waiting for transfers between devices, per_device(): zb = lax.ppermute(own, 'gz', pairs(1, 8))  2.84 us
    pallas_call x1, Pallas kernels, pool(): pl.pallas_call(pool_kernel, in_specs=[pl.BlockSpec(memory_space=pl.ANY)],...  2.44 us
    ppermute x1, starting transfers between devices, per_device(): zb = lax.ppermute(own, 'gz', pairs(1, 8))  2.11 us
    pallas_call x1, Pallas kernels, inner(): pl.pallas_call(inner_kernel, in_specs=[pl.BlockSpec(memory_space=pltpu.VM...  2.02 us
  transfers between devices with their start and end apart: 6, of which 1 were waited for; matrix products, arithmetic and copies ran while one was open for 0% of the time, Pallas kernels for 13%

profile of v5, /device:TPU:40, one launch (start us, length us, event | category | flops | bytes accessed | tf_op | source)
XLA Modules:
  0.0 47.7 jit_solution(18405004192645852929)
XLA Ops:
  0.6 0.0 copy-start.3
  0.6 0.0 copy-start.2
  0.7 0.0 copy-start.1
  0.7 0.0 copy-start
  0.7 2.4 %pool.1 = (bf16[256,128]{1,0:T(8,128)(2,1)S(1)}, bf16[32,256,128]{2,1,0:T(8,128)(2,1)S(1)}) custom-call(bf16[32,256,128]{2,1,0:T(8,128)(2,1)} %bitcast.58), custom_call_target="tpu_custom_call" | custom-call | flops 80000000 | bytes 2200000 | tf_op jit(solution)/shard_map/pool/pallas_call | solution.py:76
  3.1 0.0 copy-start.4
  3.1 0.0 copy-start.5
  3.1 0.1 collective-permute-start
  3.2 2.1 %collective-permute-start.1 = (bf16[256,128]{1,0:T(8,128)(2,1)S(1)}, bf16[256,128]{1,0:T(8,128)(2,1)S(1)}, u32[]{:S(2)}, u32[]{:S(2)}) collective-permute-start(bf16[256,128]{1,0:T(8,128)(2,1)S(1)} %get-tuple-element.33.own_ref), channel_id=1, source_target_pairs={{32,64},{64,32},{96,128},{128,96},{160,192},{192,160},{33,65},{65,... | collective-permute-start | bytes 196616 | tf_op jit(solution)/shard_map/ppermute | solution.py:405
  5.5 0.0 copy-done.3
  5.5 0.0 copy-done.2
  5.5 0.0 copy-done.1
  5.5 0.5 prepare.1
  6.0 0.0 collective-permute-done.za_ref
  6.0 2.8 %collective-permute-done.1.zb_ref = bf16[256,128]{1,0:T(8,128)(2,1)S(1)} collective-permute-done((bf16[256,128]{1,0:T(8,128)(2,1)S(1)}, bf16[256,128]{1,0:T(8,128)(2,1)S(1)}, u32[]{:S(2)}, u32[]{:S(2)}) %collective-permute-start.1) | collective-permute-done | bytes 65568 | tf_op jit(solution)/shard_map/ppermute | solution.py:405
  9.1 0.7 %collective-permute-start.2 = (bf16[6,2,8,128]{3,1,0,2:T(2,128)(2,1)S(1)}, bf16[6,2,8,128]{3,1,0,2:T(2,128)(2,1)S(1)}, u32[]{:S(2)}, u32[]{:S(2)}) collective-permute-start(bf16[6,2,8,128]{3,1,0,2:T(2,128)(2,1)S(1)} %pad_maximum_fusion.2), channel_id=1, source_target_pairs={{0,8},{8,0},{16,24},{24,16},{1,9},{9,1},{17,25},{25,17},{2,10},{10... | collective-permute-start | bytes 73736 | tf_op jit(solution)/shard_map/ppermute | solution.py:421
  9.8 4.1 %collective-permute-start.3 = (bf16[6,2,8,128]{3,1,0,2:T(2,128)(2,1)S(1)}, bf16[6,2,8,128]{3,1,0,2:T(2,128)(2,1)S(1)}, u32[]{:S(2)}, u32[]{:S(2)}) collective-permute-start(bf16[6,2,8,128]{3,1,0,2:T(2,128)(2,1)S(1)} %pad_maximum_fusion.3), channel_id=1, source_target_pairs={{8,16},{16,8},{9,17},{17,9},{10,18},{18,10},{11,19},{19,11},{12,20... | collective-permute-start | bytes 73736 | tf_op jit(solution)/shard_map/ppermute | solution.py:422
  14.0 0.0 copy-done
  14.0 1.9 %faces.2 = (bf16[2,256,128]{2,1,0:T(8,128)(2,1)S(1)}, f32[40,128]{1,0:T(8,128)S(1)}) custom-call(bf16[32,256,128]{2,1,0:T(8,128)(2,1)S(1)} %get-tuple-element.39.emb_ref, s32[256,128]{1,0:T(8,128)S(1)} %bitcast.43, f32[2,128,128]{2,1,0:T(8,128)S(1)} %get-tuple-element.40.order_ref, f32[40,128]{1,0:T(8,128)S(1)} %slice_bitcast_fusion.before_ref), custom_call_target="tpu_custom_call" | custom-call | flops 1000000 | bytes 10000 | tf_op jit(solution)/shard_map/faces/pallas_call | solution.py:166
  15.9 0.0 collective-permute-done.2
  15.9 0.0 collective-permute-done.3
  16.0 0.7 %collective-permute-start.4 = (bf16[6,20,128]{2,1,0:T(8,128)(2,1)S(1)}, bf16[6,20,128]{2,1,0:T(8,128)(2,1)S(1)}, u32[]{:S(2)}, u32[]{:S(2)}) collective-permute-start(bf16[6,20,128]{2,1,0:T(8,128)(2,1)S(1)} %broadcast_select_fusion.1), channel_id=1, source_target_pairs={{1,2},{2,1},{3,4},{4,3},{5,6},{6,5},{9,10},{10,9},{11,12},{12,11},... | collective-permute-start | bytes 92168 | tf_op jit(solution)/shard_map/ppermute | solution.py:433
  16.7 4.3 %collective-permute-start.5 = (bf16[6,20,128]{2,1,0:T(8,128)(2,1)S(1)}, bf16[6,20,128]{2,1,0:T(8,128)(2,1)S(1)}, u32[]{:S(2)}, u32[]{:S(2)}) collective-permute-start(bf16[6,20,128]{2,1,0:T(8,128)(2,1)S(1)} %broadcast_select_fusion), channel_id=1, source_target_pairs={{0,1},{1,0},{2,3},{3,2},{4,5},{5,4},{6,7},{7,6},{8,9},{9,8},{10,11... | collective-permute-start | bytes 92168 | tf_op jit(solution)/shard_map/ppermute | solution.py:432
  21.0 0.0 copy-done.4
  21.0 0.0 copy-done.5
  21.0 0.1 maximum_bitcast_fusion
  21.1 1.8 %faces.3 = (bf16[2,256,128]{2,1,0:T(8,128)(2,1)S(1)}, f32[128,128]{1,0:T(8,128)S(1)}) custom-call(bf16[32,256,128]{2,1,0:T(8,128)(2,1)S(1)} %get-tuple-element.39.emb_ref, s32[256,128]{1,0:T(8,128)S(1)} %bitcast.44, f32[2,128,128]{2,1,0:T(8,128)S(1)} %get-tuple-element.40.order_ref, f32[40,128]{1,0:T(8,128)S(1)} %get-tuple-element.51.before_ref), custom_call_target="tpu_custom_call" | custom-call | flops 1000000 | bytes 10000 | tf_op jit(solution)/shard_map/faces/pallas_call | solution.py:166
  22.9 2.0 %inner.1 = (f32[1024,128]{1,0:T(8,128)S(1)}, f32[256,128]{1,0:T(8,128)S(1)}, f32[2,144,128]{2,1,0:T(8,128)S(1)}, f32[2,96,128]{2,1,0:T(8,128)S(1)}) custom-call(bf16[256,128]{1,0:T(8,128)(2,1)S(1)} %get-tuple-element.33.own_ref, bf16[256,128]{1,0:T(8,128)(2,1)S(1)} %collective-permute-done.za_ref, bf16[256,128]{1,0:T(8,128)(2,1)S(1)} %collective-permute-done.1.zb_ref, ...), custom_call_target="tpu_custom_call" | custom-call | flops 1000000 | bytes 10000 | tf_op jit(solution)/shard_map/inner/pallas_call | solution.py:275
  24.9 0.0 collective-permute-done.4.xb_ref
  24.9 0.0 collective-permute-done.5.xa_ref
  24.9 0.9 %outer.1 = (bf16[1024,64]{1,0:T(8,128)(2,1)S(1)}, f32[128,128]{1,0:T(8,128)S(1)}) custom-call(bf16[6,20,128]{2,1,0:T(8,128)(2,1)S(1)} %collective-permute-done.4.xb_ref, bf16[6,20,128]{2,1,0:T(8,128)(2,1)S(1)} %collective-permute-done.5.xa_ref, f32[2,144,128]{2,1,0:T(8,128)S(1)} %get-tuple-element.53.ends_ref, f32[2,96,128]{2,1,0:T(8,128)S(1)} %get-tuple-element.54.near_ref, ...), custom_call_target="tpu_custom_call" | custom-call | flops 200000000 | bytes 3000000 | tf_op jit(solution)/shard_map/outer/pallas_call | solution.py:352
  25.8 20.6 %all_to_all.11 = f32[8,16,128]{2,1,0:T(8,128)S(1)} all-to-all(f32[8,16,128]{2,1,0:T(8,128)S(1)} %bitcast.56), channel_id=1, replica_groups=mesh['gz'=8,'gy'=4,'gx'=8] {'gx'}, dimensions={0} | all-to-all | bytes 131072 | tf_op jit(solution)/shard_map/all_to_all | solution.py:444
  46.4 1.3 %edges.1 = (f32[32,64]{1,0:T(8,128)}, f32[64,64]{1,0:T(8,128)}, bf16[1024,64]{1,0:T(8,128)(2,1)}) custom-call(f32[128,128]{1,0:T(8,128)S(1)} %bitcast.46, bf16[1024,64]{1,0:T(8,128)(2,1)S(1)} %get-tuple-element.59.ctx_ref), custom_call_target="tpu_custom_call" | custom-call | tf_op jit(solution)/shard_map/edges/pallas_call | solution.py:382
  (23 shorter events, 0.3 us)
Async XLA Ops:
  0.6 4.8 %copy-start.3 = (s32[128]{0:T(128)S(1)}, s32[128]{0:T(128)}, u32[]{:S(2)}) copy-start(s32[128]{0:T(128)} %param.9) | copy-start | bytes 1540
  0.6 4.8 %copy-start.2 = (bf16[3,3,3,64,32]{3,4,2,1,0:T(8,128)(2,1)S(1)}, bf16[3,3,3,64,32]{3,4,2,1,0:T(8,128)(2,1)}, u32[]{:S(2)}) copy-start(bf16[3,3,3,64,32]{3,4,2,1,0:T(8,128)(2,1)} %param.10) | copy-start | bytes 331780
  0.7 4.8 %copy-start.1 = (bf16[3,3,3,64,64]{4,3,2,1,0:T(8,128)(2,1)S(1)}, bf16[3,3,3,64,64]{4,3,2,1,0:T(8,128)(2,1)}, u32[]{:S(2)}) copy-start(bf16[3,3,3,64,64]{4,3,2,1,0:T(8,128)(2,1)} %param.12) | copy-start | bytes 663556
  0.7 13.3 %copy-start = (s32[4,64,128]{2,1,0:T(8,128)S(1)}, s32[4,64,128]{2,1,0:T(8,128)}, u32[]{:S(2)}) copy-start(s32[4,64,128]{2,1,0:T(8,128)} %param.8) | copy-start | bytes 393220
  3.1 17.9 %copy-start.4 = (f32[64]{0:T(128)S(1)}, f32[64]{0:T(128)}, u32[]{:S(2)}) copy-start(f32[64]{0:T(128)} %param.11) | copy-start | bytes 772
  3.1 17.9 %copy-start.5 = (f32[64]{0:T(128)S(1)}, f32[64]{0:T(128)}, u32[]{:S(2)}) copy-start(f32[64]{0:T(128)} %param.13) | copy-start | bytes 772
  3.1 2.8 %collective-permute-start = (bf16[256,128]{1,0:T(8,128)(2,1)S(1)}, bf16[256,128]{1,0:T(8,128)(2,1)S(1)}, u32[]{:S(2)}, u32[]{:S(2)}) collective-permute-start(bf16[256,128]{1,0:T(8,128)(2,1)S(1)} %get-tuple-element.33.own_ref), channel_id=1, source_target_pairs={{0,32},{32,0},{64,96},{96,64},{128,160},{160,128},{192,224},{224,1... | collective-permute-start | bytes 196616 | tf_op jit(solution)/shard_map/ppermute | solution.py:406
  3.2 5.6 %collective-permute-start.1 = (bf16[256,128]{1,0:T(8,128)(2,1)S(1)}, bf16[256,128]{1,0:T(8,128)(2,1)S(1)}, u32[]{:S(2)}, u32[]{:S(2)}) collective-permute-start(bf16[256,128]{1,0:T(8,128)(2,1)S(1)} %get-tuple-element.33.own_ref), channel_id=1, source_target_pairs={{32,64},{64,32},{96,128},{128,96},{160,192},{192,160},{33,65},{65,... | collective-permute-start | bytes 196616 | tf_op jit(solution)/shard_map/ppermute | solution.py:405
  9.1 6.8 %collective-permute-start.2 = (bf16[6,2,8,128]{3,1,0,2:T(2,128)(2,1)S(1)}, bf16[6,2,8,128]{3,1,0,2:T(2,128)(2,1)S(1)}, u32[]{:S(2)}, u32[]{:S(2)}) collective-permute-start(bf16[6,2,8,128]{3,1,0,2:T(2,128)(2,1)S(1)} %pad_maximum_fusion.2), channel_id=1, source_target_pairs={{0,8},{8,0},{16,24},{24,16},{1,9},{9,1},{17,25},{25,17},{2,10},{10... | collective-permute-start | bytes 73736 | tf_op jit(solution)/shard_map/ppermute | solution.py:421
  9.8 6.1 %collective-permute-start.3 = (bf16[6,2,8,128]{3,1,0,2:T(2,128)(2,1)S(1)}, bf16[6,2,8,128]{3,1,0,2:T(2,128)(2,1)S(1)}, u32[]{:S(2)}, u32[]{:S(2)}) collective-permute-start(bf16[6,2,8,128]{3,1,0,2:T(2,128)(2,1)S(1)} %pad_maximum_fusion.3), channel_id=1, source_target_pairs={{8,16},{16,8},{9,17},{17,9},{10,18},{18,10},{11,19},{19,11},{12,20... | collective-permute-start | bytes 73736 | tf_op jit(solution)/shard_map/ppermute | solution.py:422
  16.0 8.9 %collective-permute-start.4 = (bf16[6,20,128]{2,1,0:T(8,128)(2,1)S(1)}, bf16[6,20,128]{2,1,0:T(8,128)(2,1)S(1)}, u32[]{:S(2)}, u32[]{:S(2)}) collective-permute-start(bf16[6,20,128]{2,1,0:T(8,128)(2,1)S(1)} %broadcast_select_fusion.1), channel_id=1, source_target_pairs={{1,2},{2,1},{3,4},{4,3},{5,6},{6,5},{9,10},{10,9},{11,12},{12,11},... | collective-permute-start | bytes 92168 | tf_op jit(solution)/shard_map/ppermute | solution.py:433
  16.7 8.2 %collective-permute-start.5 = (bf16[6,20,128]{2,1,0:T(8,128)(2,1)S(1)}, bf16[6,20,128]{2,1,0:T(8,128)(2,1)S(1)}, u32[]{:S(2)}, u32[]{:S(2)}) collective-permute-start(bf16[6,20,128]{2,1,0:T(8,128)(2,1)S(1)} %broadcast_select_fusion), channel_id=1, source_target_pairs={{0,1},{1,0},{2,3},{3,2},{4,5},{5,4},{6,7},{7,6},{8,9},{9,8},{10,11... | collective-permute-start | bytes 92168 | tf_op jit(solution)/shard_map/ppermute | solution.py:432

commit v6 on v5

--- a/solution.py
+++ b/solution.py
@@ -94,9 +94,30 @@
     return [jnp.concatenate([w[k + 1], w[k]], axis=1) for k in range(4)]
 
 
-def prepare_kernel(edge_ref, w1_ref, w2_ref, order_ref, w1a_ref, w1b_ref, w2a_ref):
+def bands_kernel(w1_ref, w2_ref, w1a_ref, w1b_ref, w2a_ref):
+    for tap in range(9):
+        bands = banded(tap, lambda t, k: w1_ref[3 * t + k])
+        w1a_ref[pl.ds(128 * tap, 128), :] = jnp.concatenate(bands, axis=0)
+        w1b_ref[pl.ds(128 * tap, 128), :] = jnp.concatenate(bands[2:] + bands[:2], axis=0)
+        bands = banded(tap, lambda t, k: w2_ref[3 * t + k].astype(F32).T.astype(BF))
+        w2a_ref[pl.ds(256 * tap, 256), :] = jnp.concatenate(bands, axis=0)
+
+
+def bands(w1, w2):
+    return pl.pallas_call(
+        bands_kernel,
+        in_specs=[pl.BlockSpec(memory_space=pltpu.VMEM)] * 2,
+        out_specs=[pl.BlockSpec(memory_space=pltpu.VMEM)] * 3,
+        out_shape=[pltpu.VMEM((1152, 128), BF), pltpu.VMEM((1152, 128), BF), pltpu.VMEM((2304, 128), BF)],
+        compiler_params=pltpu.CompilerParams(vmem_limit_bytes=16 << 20),
+        cost_estimate=pl.CostEstimate(flops=1_000_000, bytes_accessed=10_000, transcendentals=0),
+        name="bands",
+    )(w1, w2)
+
+
+def ordering(edge):
     i0, i1 = iota((128, 128), 0), iota((128, 128), 1)
-    label = jnp.broadcast_to(edge_ref[...], (128, 128))
+    label = jnp.broadcast_to(edge, (128, 128))
     owner = ((label >> 6) & 7).astype(F32)
     local = (label & 63).astype(F32)
     ahead = jnp.where((owner == owner.T) & (i0 < i1), 1.0, 0.0)
@@ -104,36 +125,19 @@
     chosen = place == i0.astype(F32)
     face = jnp.sum(jnp.where(chosen, i1.astype(F32), 0.0), axis=1, keepdims=True)
     edge = jnp.sum(jnp.where(chosen, local, 0.0), axis=1, keepdims=True)
-    order_ref[0] = jnp.broadcast_to(face, (128, 128))
-    order_ref[1] = jnp.broadcast_to(edge, (128, 128))
-    for tap in range(9):
-        bands = banded(tap, lambda t, k: w1_ref[3 * t + k])
-        w1a_ref[pl.ds(128 * tap, 128), :] = jnp.concatenate(bands, axis=0)
-        w1b_ref[pl.ds(128 * tap, 128), :] = jnp.concatenate(bands[2:] + bands[:2], axis=0)
-        bands = banded(tap, lambda t, k: w2_ref[3 * t + k].astype(F32).T.astype(BF))
-        w2a_ref[pl.ds(256 * tap, 256), :] = jnp.concatenate(bands, axis=0)
-
-
-def prepare(edge, w1, w2):
-    return pl.pallas_call(
-        prepare_kernel,
-        in_specs=[pl.BlockSpec(memory_space=pltpu.VMEM)] * 3,
-        out_specs=[pl.BlockSpec(memory_space=pltpu.VMEM)] * 4,
-        out_shape=[
-            pltpu.VMEM((2, 128, 128), F32),
-            pltpu.VMEM((1152, 128), BF),
-            pltpu.VMEM((1152, 128), BF),
-            pltpu.VMEM((2304, 128), BF),
-        ],
-        compiler_params=pltpu.CompilerParams(vmem_limit_bytes=16 << 20),
-        cost_estimate=pl.CostEstimate(flops=1_000_000, bytes_accessed=10_000, transcendentals=0),
-        name="prepare",
-    )(edge, w1, w2)
-
-
-def face_kernel(half, emb_ref, slot_ref, order_ref, before_ref, cnt_ref, after_ref, wide, cells):
+    return jnp.broadcast_to(face, (128, 128)), jnp.broadcast_to(edge, (128, 128))
+
+
+def face_kernel(half, emb_ref, slot_ref, given_ref, *refs):
+    cnt_ref, after_ref, wide, cells = refs
     wide[...] = emb_ref[:, pl.ds(128 * half, 128), :].astype(F32).reshape(4096, 128)
-    faces = order_ref[0].astype(jnp.int32)
+    if half == 0:
+        face, edge = ordering(given_ref[...])
+        after_ref[0:128] = face
+        after_ref[128:256] = edge
+    else:
+        face, edge = given_ref[0:128], given_ref[128:256]
+    faces = face.astype(jnp.int32)
     pool_x8 = jnp.concatenate([pool_x_matrix()] * 8, axis=1)
     sums = jnp.zeros((32, 128), F32)
     count = jnp.zeros((8, 128), F32)
@@ -153,26 +157,26 @@
     for x4 in range(4):
         cnt_ref[x4 // 2, 128 * (x4 % 2) : 128 * (x4 % 2) + 128, :] = cells[x4].T.astype(BF)
     if half == 0:
-        after_ref[0:32] = sums
-        after_ref[32:40] = count
+        after_ref[256:288] = sums
+        after_ref[288:296] = count
     else:
-        sums = sums + before_ref[0:32]
-        number = jnp.sum(count + before_ref[32:40], axis=0, keepdims=True)
+        sums = sums + given_ref[256:288]
+        number = jnp.sum(count + given_ref[288:296], axis=0, keepdims=True)
         stacked = jnp.concatenate([jnp.zeros((64, 128), F32), sums, jnp.broadcast_to(number, (32, 128))], axis=0)
-        after_ref[...] = jnp.where(iota((128, 128), 1) == 97, order_ref[1], stacked.T)
-
-
-def faces(half, emb, slot, order, before):
+        after_ref[...] = jnp.where(iota((128, 128), 1) == 97, edge, stacked.T)
+
+
+def faces(half, emb, slot, given):
     return pl.pallas_call(
         functools.partial(face_kernel, half),
-        in_specs=[pl.BlockSpec(memory_space=pltpu.VMEM)] * 4,
+        in_specs=[pl.BlockSpec(memory_space=pltpu.VMEM)] * 3,
         out_specs=[pl.BlockSpec(memory_space=pltpu.VMEM)] * 2,
-        out_shape=[pltpu.VMEM((2, 256, 128), BF), pltpu.VMEM((128 if half else 40, 128), F32)],
+        out_shape=[pltpu.VMEM((2, 256, 128), BF), pltpu.VMEM((128 if half else 296, 128), F32)],
         scratch_shapes=[pltpu.VMEM((4096, 128), F32), pltpu.VMEM((4, 128, 128), F32)],
         compiler_params=pltpu.CompilerParams(vmem_limit_bytes=16 << 20),
         cost_estimate=pl.CostEstimate(flops=1_000_000, bytes_accessed=10_000, transcendentals=0),
         name="faces",
-    )(keep(emb), slot, keep(order), keep(before))
+    )(keep(emb), slot, keep(given) if half else given)
 
 
 ROWS1 = 6 * 20 * 8
@@ -200,7 +204,7 @@
 
 
 def inner_kernel(own_ref, za_ref, zb_ref, ya_ref, yb_ref, w1a_ref, w1b_ref, b1_ref, w2_ref, b2_ref, cnt0_ref,
-                 cnt1_ref, fine_ref, sums_ref, ends_ref, near_ref, field, this, mixed, h0f, h1f, h0b, h0n, h1b):
+                 cnt1_ref, fine_ref, sums_ref, ends_ref, near_ref, rim_ref, field, this, mixed, h0f, h1f, h0b, h0n, h1b):
     gz, gy = lax.axis_index("gz"), lax.axis_index("gy")
     z_even, y_even = (gz & 1) == 0, (gy & 1) == 0
     z_low, z_high = ordered(z_even, za_ref[...].astype(F32), zb_ref[...].astype(F32))
@@ -269,18 +273,24 @@
             term = dot((cnt0_ref, cnt1_ref)[z][p], ctx)
             sums = term if sums is None else sums + term
     sums_ref[...] = sums
+    row, col = iota((512, 128), 0), iota((512, 128), 1)
+    cell = ((row >> 7) << 4) + ((row & 127) >> 3)
+    pick = jnp.where((cell == col) & ((row & 7) == 7 * (row >> 8)), 1.0, 0.0).astype(BF)
+    left = jnp.concatenate([cnt0_ref[0], cnt1_ref[0], cnt0_ref[1], cnt1_ref[1]], axis=1)
+    rim_ref[...] = dot(left, pick).astype(BF)
 
 
 def inner(*arrays):
     return pl.pallas_call(
         inner_kernel,
         in_specs=[pl.BlockSpec(memory_space=pltpu.VMEM)] * len(arrays),
-        out_specs=[pl.BlockSpec(memory_space=pltpu.VMEM)] * 4,
+        out_specs=[pl.BlockSpec(memory_space=pltpu.VMEM)] * 5,
         out_shape=[
             pltpu.VMEM((1024, 128), F32),
             pltpu.VMEM((256, 128), F32),
             pltpu.VMEM((2, 144, 128), F32),
             pltpu.VMEM((2, 96, 128), F32),
+            pltpu.VMEM((256, 128), BF),
         ],
         scratch_shapes=[
             pltpu.VMEM((HEAD + ROWS1 + 8, 128), F32),
@@ -298,14 +308,13 @@
     )(*arrays)
 
 
-def outer_kernel(xb_ref, xa_ref, ends_ref, near_ref, fine_ref, sums_ref, w1b_ref, b1_ref, w2_ref, b2_ref, cnt0_ref,
-                 cnt1_ref, face_ref, ctx_ref, send_ref, column, hidden, patch, sparse):
+def outer_kernel(xb_ref, xa_ref, ends_ref, near_ref, fine_ref, sums_ref, w1b_ref, b1_ref, w2_ref, b2_ref, rim_ref,
+                 face_ref, ctx_ref, send_ref, column, hidden, patch):
     gz, gy, gx = (lax.axis_index(a) for a in ("gz", "gy", "gx"))
     z_even, y_even, x_even = (gz & 1) == 0, (gy & 1) == 0, (gx & 1) == 0
     lane = iota((24, 128), 1)
     column[...] = jnp.zeros_like(column)
     patch[...] = fine_ref[...]
-    sparse[...] = jnp.zeros_like(sparse)
     for k, whole in enumerate(ordered(x_even, xa_ref[...].astype(F32), xb_ref[...].astype(F32))):
         low, high = ordered(z_even, whole[0:2], whole[4:6])
         for plane, rows in enumerate((low[0], low[1], whole[2], whole[3], high[0], high[1])):
@@ -335,14 +344,14 @@
         h = [jnp.concatenate(h[2 * k : 2 * k + 2], axis=1) for k in range(2)]
         lefts.append(jnp.concatenate(h, axis=0))
     ctx = (taps_dot(lefts, w2_ref, 256) + b2_ref[...]).astype(BF).astype(F32)
-    for k, (x, g) in enumerate(((0, 0), (30, 7))):
+    rows = []
+    for k, x in enumerate((0, 30)):
         for z in range(2):
             wide = ctx[40 * k + 24 * z : 40 * k + 24 * z + 16]
             patch[pl.ds(512 * z + x, 16, stride=32), :] = wide
             patch[pl.ds(512 * z + x + 1, 16, stride=32), :] = pltpu.roll(wide, 64, 1)
-            sparse[pl.ds(128 * (2 * k + z) + g, 16, stride=8), :] = wide
-    left = jnp.concatenate([cnt0_ref[0], cnt1_ref[0], cnt0_ref[1], cnt1_ref[1]], axis=1)
-    sums = sums_ref[...] + dot(left, sparse[...].astype(BF))
+            rows.append(wide)
+    sums = sums_ref[...] + dot(rim_ref[:, :64], jnp.concatenate(rows, axis=0).astype(BF))
     ctx_ref[...] = patch[...][:, :64].astype(BF)
     both = sums[:128] + pltpu.roll(sums[128:], 64, 1)
     send_ref[...] = jnp.where(iota((128, 128), 1) < 64, both, face_ref[...])
@@ -358,7 +367,6 @@
             pltpu.VMEM((2, 152, 128), F32),
             pltpu.VMEM((4, 96, 128), F32),
             pltpu.VMEM((1024, 128), F32),
-            pltpu.VMEM((512, 128), F32),
         ],
         compiler_params=pltpu.CompilerParams(vmem_limit_bytes=16 << 20),
         cost_estimate=pl.CostEstimate(flops=200_000_000, bytes_accessed=3_000_000, transcendentals=0),
@@ -404,12 +412,9 @@
     own, voxels = pool(emb)
     zb = lax.ppermute(own, "gz", pairs(1, 8))
     za = lax.ppermute(own, "gz", pairs(0, 8))
-    order, w1a, w1b, w2a = prepare(
-        face_edge.reshape(1, 128),
-        jnp.swapaxes(conv1_w, 3, 4).reshape(27, 32, 64),
-        conv2_w.reshape(27, 64, 64),
-    )
-    za, zb, order = lax.optimization_barrier((za, zb, order))
+    cnt0, half = faces(0, voxels, slot, face_edge.reshape(1, 128))
+    w1, w2 = jnp.swapaxes(conv1_w, 3, 4).reshape(27, 32, 64), conv2_w.reshape(27, 64, 64)
+    zb, za, half = lax.optimization_barrier((zb, za, half))
     planes = [a.reshape(2, 16, 8, 128) for a in (za, own, zb)]
     y_even, x_even = (gy & 1) == 0, (gx & 1) == 0
 
@@ -420,26 +425,26 @@
     to_a, to_b = lax.optimization_barrier((y_edge(y_even), y_edge(jnp.logical_not(y_even))))
     ya = lax.ppermute(to_a, "gy", pairs(0, 4))
     yb = lax.ppermute(to_b, "gy", pairs(1, 4))
-    cnt0, half = faces(0, voxels, slot, order, order[0, :40])
-    ya, yb, half = lax.optimization_barrier((ya, yb, half))
+    cnt1, face = faces(1, voxels, slot, half)
+    ya, yb, face = lax.optimization_barrier((ya, yb, face))
 
     def x_edge(g):
         mid = jnp.concatenate([a[:, :, g] for a in planes], axis=0)
         return jnp.concatenate([mid, ya[:, :, g], yb[:, :, g]], axis=1)
 
     low, high = x_edge(0), x_edge(7)
-    to_b, to_a, half = lax.optimization_barrier((jnp.where(x_even, low, high), jnp.where(x_even, high, low), half))
+    to_b, to_a, w1 = lax.optimization_barrier((jnp.where(x_even, low, high), jnp.where(x_even, high, low), w1))
+    w1a, w1b, w2a = bands(w1, w2)
     xa = lax.ppermute(to_a, "gx", pairs(0, 8))
     xb = lax.ppermute(to_b, "gx", pairs(1, 8))
-    cnt1, face = faces(1, voxels, slot, order, half)
     twice = lambda b: jnp.concatenate([b, b]).reshape(1, 128)
     b1, b2 = twice(conv1_b), twice(conv2_b)
     w1a, w1b, w2a, cnt0, cnt1 = (keep(a) for a in (w1a, w1b, w2a, cnt0, cnt1))
-    fine, sums, ends, near = inner(
+    fine, sums, ends, near, rim = inner(
         own, za, zb, ya.reshape(96, 128), yb.reshape(96, 128), w1a, w1b, b1, w2a, b2, cnt0, cnt1
     )
     context, send = outer(
-        xb, xa, keep(ends), keep(near), keep(fine), keep(sums), w1b, b1, w2a, b2, cnt0, cnt1, keep(face)
+        xb, xa, keep(ends), keep(near), keep(fine), keep(sums), w1b, b1, w2a, b2, keep(rim), keep(face)
     )
     rows = lax.all_to_all(send, "gx", 0, 0, tiled=True)
     edge_emb, edge_ctx, context = edges(rows, context)

time: 48.2 us -> 48 us (level)
  waiting for transfers between devices: 2.86 us -> 1.33 us
  blocking collectives: 20.6 us -> 21.8 us
    ppermute x1, waiting for transfers between devices: 2.84 us -> 1.22 us  [per_device(): zb = lax.ppermute(own, 'gz', pairs(1, 8))]
    all_to_all x1, blocking collectives: 20.6 us -> 21.8 us  [per_device(): rows = lax.all_to_all(send, 'gx', 0, 0, tiled=True)]
  transfers between devices with their start and end apart: 6 -> 6, of which waited for: 1 -> 2; matrix products, arithmetic and copies ran while one was open for 0% -> 0% of each run, Pallas kernels for 13% -> 13%
where the time goes in v6:
time: 48 us; the launch traced here: 47.4 us
  blocking collectives  21.8 us (45%)
  starting transfers between devices  11.9 us (25%)
  Pallas kernels  10.9 us (23%)
  waiting for transfers between devices  1.33 us (3%)
  between operations  0.97 us (2%)
    all_to_all x1, blocking collectives, per_device(): rows = lax.all_to_all(send, 'gx', 0, 0, tiled=True)  21.8 us
    ppermute x1, starting transfers between devices, per_device(): xa = lax.ppermute(to_a, 'gx', pairs(0, 8))  4.23 us
    pallas_call x2, Pallas kernels, faces(): pl.pallas_call(functools.partial(face_kernel, half), in_specs=[pl.BlockSp...  3.83 us
    ppermute x1, starting transfers between devices, per_device(): yb = lax.ppermute(to_b, 'gy', pairs(1, 4))  3.78 us
    pallas_call x1, Pallas kernels, pool(): pl.pallas_call(pool_kernel, in_specs=[pl.BlockSpec(memory_space=pl.ANY)],...  2.41 us
    pallas_call x1, Pallas kernels, inner(): pl.pallas_call(inner_kernel, in_specs=[pl.BlockSpec(memory_space=pltpu.VM...  2.13 us
    ppermute x1, starting transfers between devices, per_device(): zb = lax.ppermute(own, 'gz', pairs(1, 8))  2.11 us
    pallas_call x1, Pallas kernels, edges(): pl.pallas_call(edge_kernel, in_specs=[pl.BlockSpec(memory_space=pltpu.VME...  1.33 us
  transfers between devices with their start and end apart: 6, of which 2 were waited for; matrix products, arithmetic and copies ran while one was open for 0% of the time, Pallas kernels for 13%

profile of v6, /device:TPU:40, one launch (start us, length us, event | category | flops | bytes accessed | tf_op | source)
XLA Modules:
  0.0 47.4 jit_solution(16507836803246416493)
XLA Ops:
  0.6 0.0 copy-start.3
  0.6 0.0 copy-start
  0.7 2.4 %pool.1 = (bf16[256,128]{1,0:T(8,128)(2,1)S(1)}, bf16[32,256,128]{2,1,0:T(8,128)(2,1)S(1)}) custom-call(bf16[32,256,128]{2,1,0:T(8,128)(2,1)} %bitcast.56), custom_call_target="tpu_custom_call" | custom-call | flops 80000000 | bytes 2200000 | tf_op jit(solution)/shard_map/pool/pallas_call | solution.py:76
  3.1 0.1 collective-permute-start.1
  3.2 2.1 %collective-permute-start = (bf16[256,128]{1,0:T(8,128)(2,1)S(1)}, bf16[256,128]{1,0:T(8,128)(2,1)S(1)}, u32[]{:S(2)}, u32[]{:S(2)}) collective-permute-start(bf16[256,128]{1,0:T(8,128)(2,1)S(1)} %get-tuple-element.33.own_ref), channel_id=1, source_target_pairs={{32,64},{64,32},{96,128},{128,96},{160,192},{192,160},{33,65},{65,... | collective-permute-start | bytes 196616 | tf_op jit(solution)/shard_map/ppermute | solution.py:413
  5.4 0.0 copy-done.3
  5.4 0.0 copy-done
  5.4 2.1 %faces.2 = (bf16[2,256,128]{2,1,0:T(8,128)(2,1)S(1)}, f32[296,128]{1,0:T(8,128)S(1)}) custom-call(bf16[32,256,128]{2,1,0:T(8,128)(2,1)S(1)} %get-tuple-element.34.emb_ref, s32[256,128]{1,0:T(8,128)S(1)} %bitcast.41, s32[1,128]{1,0:T(1,128)S(1)} %bitcast.55), custom_call_target="tpu_custom_call" | custom-call | flops 1000000 | bytes 10000 | tf_op jit(solution)/shard_map/faces/pallas_call | solution.py:170
  7.5 0.0 copy-start.4
  7.5 0.0 copy-start.5
  7.5 0.0 copy-start.1
  7.5 0.0 copy-start.2
  7.5 0.0 collective-permute-done.1.za_ref
  7.5 1.2 %collective-permute-done.zb_ref = bf16[256,128]{1,0:T(8,128)(2,1)S(1)} collective-permute-done((bf16[256,128]{1,0:T(8,128)(2,1)S(1)}, bf16[256,128]{1,0:T(8,128)(2,1)S(1)}, u32[]{:S(2)}, u32[]{:S(2)}) %collective-permute-start) | collective-permute-done | bytes 65568 | tf_op jit(solution)/shard_map/ppermute | solution.py:413
  9.0 1.1 %collective-permute-start.2 = (bf16[6,2,8,128]{3,1,0,2:T(2,128)(2,1)S(1)}, bf16[6,2,8,128]{3,1,0,2:T(2,128)(2,1)S(1)}, u32[]{:S(2)}, u32[]{:S(2)}) collective-permute-start(bf16[6,2,8,128]{3,1,0,2:T(2,128)(2,1)S(1)} %pad_maximum_fusion.2), channel_id=1, source_target_pairs={{0,8},{8,0},{16,24},{24,16},{1,9},{9,1},{17,25},{25,17},{2,10},{10... | collective-permute-start | bytes 73736 | tf_op jit(solution)/shard_map/ppermute | solution.py:426
  10.1 3.8 %collective-permute-start.3 = (bf16[6,2,8,128]{3,1,0,2:T(2,128)(2,1)S(1)}, bf16[6,2,8,128]{3,1,0,2:T(2,128)(2,1)S(1)}, u32[]{:S(2)}, u32[]{:S(2)}) collective-permute-start(bf16[6,2,8,128]{3,1,0,2:T(2,128)(2,1)S(1)} %pad_maximum_fusion.3), channel_id=1, source_target_pairs={{8,16},{16,8},{9,17},{17,9},{10,18},{18,10},{11,19},{19,11},{12,20... | collective-permute-start | bytes 73736 | tf_op jit(solution)/shard_map/ppermute | solution.py:427
  13.9 1.8 %faces.3 = (bf16[2,256,128]{2,1,0:T(8,128)(2,1)S(1)}, f32[128,128]{1,0:T(8,128)S(1)}) custom-call(bf16[32,256,128]{2,1,0:T(8,128)(2,1)S(1)} %get-tuple-element.34.emb_ref, s32[256,128]{1,0:T(8,128)S(1)} %bitcast.42, f32[296,128]{1,0:T(8,128)S(1)} %get-tuple-element.40.given_ref), custom_call_target="tpu_custom_call" | custom-call | flops 1000000 | bytes 10000 | tf_op jit(solution)/shard_map/faces/pallas_call | solution.py:170
  15.7 0.0 collective-permute-done.2
  15.7 0.1 collective-permute-done.3
  15.9 0.7 %collective-permute-start.4 = (bf16[6,20,128]{2,1,0:T(8,128)(2,1)S(1)}, bf16[6,20,128]{2,1,0:T(8,128)(2,1)S(1)}, u32[]{:S(2)}, u32[]{:S(2)}) collective-permute-start(bf16[6,20,128]{2,1,0:T(8,128)(2,1)S(1)} %broadcast_select_fusion.1), channel_id=1, source_target_pairs={{1,2},{2,1},{3,4},{4,3},{5,6},{6,5},{9,10},{10,9},{11,12},{12,11},... | collective-permute-start | bytes 92168 | tf_op jit(solution)/shard_map/ppermute | solution.py:439
  16.5 4.2 %collective-permute-start.5 = (bf16[6,20,128]{2,1,0:T(8,128)(2,1)S(1)}, bf16[6,20,128]{2,1,0:T(8,128)(2,1)S(1)}, u32[]{:S(2)}, u32[]{:S(2)}) collective-permute-start(bf16[6,20,128]{2,1,0:T(8,128)(2,1)S(1)} %broadcast_select_fusion), channel_id=1, source_target_pairs={{0,1},{1,0},{2,3},{3,2},{4,5},{5,4},{6,7},{7,6},{8,9},{9,8},{10,11... | collective-permute-start | bytes 92168 | tf_op jit(solution)/shard_map/ppermute | solution.py:438
  20.8 0.0 copy-done.4
  20.8 0.0 copy-done.5
  20.8 0.1 maximum_bitcast_fusion
  20.9 0.0 copy-done.1
  20.9 0.0 copy-done.2
  20.9 0.4 bands.1
  21.3 2.1 %inner.1 = (f32[1024,128]{1,0:T(8,128)S(1)}, f32[256,128]{1,0:T(8,128)S(1)}, f32[2,144,128]{2,1,0:T(8,128)S(1)}, f32[2,96,128]{2,1,0:T(8,128)S(1)}, bf16[256,128]{1,0:T(8,128)(2,1)S(1)}) custom-call(bf16[256,128]{1,0:T(8,128)(2,1)S(1)} %get-tuple-element.33.own_ref, bf16[256,128]{1,0:T(8,128)(2,1)S(1)} %collective-permute-done.1.za_ref, ...), custom_call_target="tpu_custom_call" | custom-call | flops 1000000 | bytes 10000 | tf_op jit(solution)/shard_map/inner/pallas_call | solution.py:284
  23.4 0.0 collective-permute-done.4.xb_ref
  23.5 0.0 collective-permute-done.5.xa_ref
  23.5 0.8 %outer.1 = (bf16[1024,64]{1,0:T(8,128)(2,1)S(1)}, f32[128,128]{1,0:T(8,128)S(1)}) custom-call(bf16[6,20,128]{2,1,0:T(8,128)(2,1)S(1)} %collective-permute-done.4.xb_ref, bf16[6,20,128]{2,1,0:T(8,128)(2,1)S(1)} %collective-permute-done.5.xa_ref, f32[2,144,128]{2,1,0:T(8,128)S(1)} %get-tuple-element.52.ends_ref, f32[2,96,128]{2,1,0:T(8,128)S(1)} %get-tuple-element.53.near_ref, ...), custom_call_target="tpu_custom_call" | custom-call | flops 200000000 | bytes 3000000 | tf_op jit(solution)/shard_map/outer/pallas_call | solution.py:361
  24.3 21.8 %all_to_all.11 = f32[8,16,128]{2,1,0:T(8,128)S(1)} all-to-all(f32[8,16,128]{2,1,0:T(8,128)S(1)} %bitcast.54), channel_id=1, replica_groups=mesh['gz'=8,'gy'=4,'gx'=8] {'gx'}, dimensions={0} | all-to-all | bytes 131072 | tf_op jit(solution)/shard_map/all_to_all | solution.py:449
  46.1 1.3 %edges.1 = (f32[32,64]{1,0:T(8,128)}, f32[64,64]{1,0:T(8,128)}, bf16[1024,64]{1,0:T(8,128)(2,1)}) custom-call(f32[128,128]{1,0:T(8,128)S(1)} %bitcast.44, bf16[1024,64]{1,0:T(8,128)(2,1)S(1)} %get-tuple-element.59.ctx_ref), custom_call_target="tpu_custom_call" | custom-call | tf_op jit(solution)/shard_map/edges/pallas_call | solution.py:390
  (22 shorter events, 0.3 us)
Async XLA Ops:
  0.6 4.8 %copy-start.3 = (s32[128]{0:T(128)S(1)}, s32[128]{0:T(128)}, u32[]{:S(2)}) copy-start(s32[128]{0:T(128)} %param.9) | copy-start | bytes 1540
  0.6 4.8 %copy-start = (s32[4,64,128]{2,1,0:T(8,128)S(1)}, s32[4,64,128]{2,1,0:T(8,128)}, u32[]{:S(2)}) copy-start(s32[4,64,128]{2,1,0:T(8,128)} %param.8) | copy-start | bytes 393220
  3.1 4.5 %collective-permute-start.1 = (bf16[256,128]{1,0:T(8,128)(2,1)S(1)}, bf16[256,128]{1,0:T(8,128)(2,1)S(1)}, u32[]{:S(2)}, u32[]{:S(2)}) collective-permute-start(bf16[256,128]{1,0:T(8,128)(2,1)S(1)} %get-tuple-element.33.own_ref), channel_id=1, source_target_pairs={{0,32},{32,0},{64,96},{96,64},{128,160},{160,128},{192,224},{224,1... | collective-permute-start | bytes 196616 | tf_op jit(solution)/shard_map/ppermute | solution.py:414
  3.2 5.6 %collective-permute-start = (bf16[256,128]{1,0:T(8,128)(2,1)S(1)}, bf16[256,128]{1,0:T(8,128)(2,1)S(1)}, u32[]{:S(2)}, u32[]{:S(2)}) collective-permute-start(bf16[256,128]{1,0:T(8,128)(2,1)S(1)} %get-tuple-element.33.own_ref), channel_id=1, source_target_pairs={{32,64},{64,32},{96,128},{128,96},{160,192},{192,160},{33,65},{65,... | collective-permute-start | bytes 196616 | tf_op jit(solution)/shard_map/ppermute | solution.py:413
  7.5 13.3 %copy-start.4 = (f32[64]{0:T(128)S(1)}, f32[64]{0:T(128)}, u32[]{:S(2)}) copy-start(f32[64]{0:T(128)} %param.11) | copy-start | bytes 772
  7.5 13.3 %copy-start.5 = (f32[64]{0:T(128)S(1)}, f32[64]{0:T(128)}, u32[]{:S(2)}) copy-start(f32[64]{0:T(128)} %param.13) | copy-start | bytes 772
  7.5 13.4 %copy-start.1 = (bf16[3,3,3,64,64]{4,3,2,1,0:T(8,128)(2,1)S(1)}, bf16[3,3,3,64,64]{4,3,2,1,0:T(8,128)(2,1)}, u32[]{:S(2)}) copy-start(bf16[3,3,3,64,64]{4,3,2,1,0:T(8,128)(2,1)} %param.12) | copy-start | bytes 663556
  7.5 13.4 %copy-start.2 = (bf16[3,3,3,64,32]{3,4,2,1,0:T(8,128)(2,1)S(1)}, bf16[3,3,3,64,32]{3,4,2,1,0:T(8,128)(2,1)}, u32[]{:S(2)}) copy-start(bf16[3,3,3,64,32]{3,4,2,1,0:T(8,128)(2,1)} %param.10) | copy-start | bytes 331780
  9.0 6.7 %collective-permute-start.2 = (bf16[6,2,8,128]{3,1,0,2:T(2,128)(2,1)S(1)}, bf16[6,2,8,128]{3,1,0,2:T(2,128)(2,1)S(1)}, u32[]{:S(2)}, u32[]{:S(2)}) collective-permute-start(bf16[6,2,8,128]{3,1,0,2:T(2,128)(2,1)S(1)} %pad_maximum_fusion.2), channel_id=1, source_target_pairs={{0,8},{8,0},{16,24},{24,16},{1,9},{9,1},{17,25},{25,17},{2,10},{10... | collective-permute-start | bytes 73736 | tf_op jit(solution)/shard_map/ppermute | solution.py:426
  10.1 5.7 %collective-permute-start.3 = (bf16[6,2,8,128]{3,1,0,2:T(2,128)(2,1)S(1)}, bf16[6,2,8,128]{3,1,0,2:T(2,128)(2,1)S(1)}, u32[]{:S(2)}, u32[]{:S(2)}) collective-permute-start(bf16[6,2,8,128]{3,1,0,2:T(2,128)(2,1)S(1)} %pad_maximum_fusion.3), channel_id=1, source_target_pairs={{8,16},{16,8},{9,17},{17,9},{10,18},{18,10},{11,19},{19,11},{12,20... | collective-permute-start | bytes 73736 | tf_op jit(solution)/shard_map/ppermute | solution.py:427
  15.9 7.6 %collective-permute-start.4 = (bf16[6,20,128]{2,1,0:T(8,128)(2,1)S(1)}, bf16[6,20,128]{2,1,0:T(8,128)(2,1)S(1)}, u32[]{:S(2)}, u32[]{:S(2)}) collective-permute-start(bf16[6,20,128]{2,1,0:T(8,128)(2,1)S(1)} %broadcast_select_fusion.1), channel_id=1, source_target_pairs={{1,2},{2,1},{3,4},{4,3},{5,6},{6,5},{9,10},{10,9},{11,12},{12,11},... | collective-permute-start | bytes 92168 | tf_op jit(solution)/shard_map/ppermute | solution.py:439
  16.5 6.9 %collective-permute-start.5 = (bf16[6,20,128]{2,1,0:T(8,128)(2,1)S(1)}, bf16[6,20,128]{2,1,0:T(8,128)(2,1)S(1)}, u32[]{:S(2)}, u32[]{:S(2)}) collective-permute-start(bf16[6,20,128]{2,1,0:T(8,128)(2,1)S(1)} %broadcast_select_fusion), channel_id=1, source_target_pairs={{0,1},{1,0},{2,3},{3,2},{4,5},{5,4},{6,7},{7,6},{8,9},{9,8},{10,11... | collective-permute-start | bytes 92168 | tf_op jit(solution)/shard_map/ppermute | solution.py:438

commit v7 on v6

--- a/solution.py
+++ b/solution.py
@@ -129,7 +129,7 @@
 
 
 def face_kernel(half, emb_ref, slot_ref, given_ref, *refs):
-    cnt_ref, after_ref, wide, cells = refs
+    cnt_ref, after_ref, side_ref, wide, cells = refs
     wide[...] = emb_ref[:, pl.ds(128 * half, 128), :].astype(F32).reshape(4096, 128)
     if half == 0:
         face, edge = ordering(given_ref[...])
@@ -156,6 +156,8 @@
             count = count + part
     for x4 in range(4):
         cnt_ref[x4 // 2, 128 * (x4 % 2) : 128 * (x4 % 2) + 128, :] = cells[x4].T.astype(BF)
+    for x2 in range(2):
+        side_ref[pl.ds(16 * x2, 16), :] = cells[x2, pl.ds(0, 16, stride=8), :].astype(BF)
     if half == 0:
         after_ref[256:288] = sums
         after_ref[288:296] = count
@@ -163,15 +165,24 @@
         sums = sums + given_ref[256:288]
         number = jnp.sum(count + given_ref[288:296], axis=0, keepdims=True)
         stacked = jnp.concatenate([jnp.zeros((64, 128), F32), sums, jnp.broadcast_to(number, (32, 128))], axis=0)
-        after_ref[...] = jnp.where(iota((128, 128), 1) == 97, edge, stacked.T)
+        side_ref[pl.ds(32, 16), :] = edge.T[:16].astype(BF)
+        lane = iota((128, 128), 1)
+        rows = stacked.T
+        high = jnp.floor(rows * (1.0 / 256.0)) * 256.0
+        rows = jnp.where(lane == 96, high, jnp.where(lane == 98, rows - high, rows))
+        after_ref[...] = jnp.where(lane == 97, edge, rows)
 
 
 def faces(half, emb, slot, given):
     return pl.pallas_call(
         functools.partial(face_kernel, half),
         in_specs=[pl.BlockSpec(memory_space=pltpu.VMEM)] * 3,
-        out_specs=[pl.BlockSpec(memory_space=pltpu.VMEM)] * 2,
-        out_shape=[pltpu.VMEM((2, 256, 128), BF), pltpu.VMEM((128 if half else 296, 128), F32)],
+        out_specs=[pl.BlockSpec(memory_space=pltpu.VMEM)] * 3,
+        out_shape=[
+            pltpu.VMEM((2, 256, 128), BF),
+            pltpu.VMEM((128 if half else 296, 128), F32),
+            pltpu.VMEM((48 if half else 32, 128), BF),
+        ],
         scratch_shapes=[pltpu.VMEM((4096, 128), F32), pltpu.VMEM((4, 128, 128), F32)],
         compiler_params=pltpu.CompilerParams(vmem_limit_bytes=16 << 20),
         cost_estimate=pl.CostEstimate(flops=1_000_000, bytes_accessed=10_000, transcendentals=0),
@@ -308,21 +319,26 @@
     )(*arrays)
 
 
-def outer_kernel(xb_ref, xa_ref, ends_ref, near_ref, fine_ref, sums_ref, w1b_ref, b1_ref, w2_ref, b2_ref, rim_ref,
-                 face_ref, ctx_ref, send_ref, column, hidden, patch):
+def outer_kernel(xb_ref, xa_ref, ends_ref, near_ref, fine_ref, sums_ref, w1a_ref, w1b_ref, b1_ref, w2_ref, b2_ref, rim_ref,
+                 face_ref, patch, send_ref, column, hidden):
     gz, gy, gx = (lax.axis_index(a) for a in ("gz", "gy", "gx"))
     z_even, y_even, x_even = (gz & 1) == 0, (gy & 1) == 0, (gx & 1) == 0
     lane = iota((24, 128), 1)
     column[...] = jnp.zeros_like(column)
     patch[...] = fine_ref[...]
-    for k, whole in enumerate(ordered(x_even, xa_ref[...].astype(F32), xb_ref[...].astype(F32))):
-        low, high = ordered(z_even, whole[0:2], whole[4:6])
-        for plane, rows in enumerate((low[0], low[1], whole[2], whole[3], high[0], high[1])):
+    got = xb_ref[...].astype(F32)
+    for k, whole in enumerate(ordered(x_even, xa_ref[80:200].astype(F32), got[80:200])):
+        planes = [whole[20 * i : 20 * i + 20] for i in range(6)]
+        low0, high0 = ordered(z_even, planes[0], planes[4])
+        low1, high1 = ordered(z_even, planes[1], planes[5])
+        for plane, rows in enumerate((low0, low1, planes[2], planes[3], high0, high1)):
             first, last = ordered(y_even, rows[16:18], rows[18:20])
             halo = jnp.concatenate([first, rows[0:16], last, jnp.zeros((4, 128), F32)], axis=0)
             own = ends_ref[k, pl.ds(24 * plane, 24), :]
             left, right = (own, halo) if k == 0 else (halo, own)
             column[k, pl.ds(24 * plane, 24), :] = jnp.where(lane < 64, left, right)
+            if k == 1:
+                column[2, pl.ds(24 * plane, 24), :] = halo
 
     row, lane = iota((96, 128), 0), iota((96, 128), 1)
     z_of = jnp.where(row < 24, 0, jnp.where(row < 48, 1, jnp.where(row < 72, 2, 3)))
@@ -333,16 +349,18 @@
     at = [24 * (tap // 3) + tap % 3 for tap in range(9)]
     lefts = [jnp.concatenate([column[k, pl.ds(r, 96), :] for k in range(2)], axis=0).astype(BF) for r in at]
     total = jnp.maximum(taps_dot(lefts, w1b_ref, 128) + b1_ref[...], 0.0)
+    lefts = [column[2, pl.ds(r, 96), :].astype(BF) for r in at]
+    beyond = jnp.maximum(taps_dot(lefts, w1a_ref, 128) + b1_ref[...], 0.0)
     hidden[0, 0:96] = jnp.where(out0, 0.0, total[0:96])
     hidden[1, 0:96] = near_ref[0]
     hidden[2, 0:96] = near_ref[1]
     hidden[3, 0:96] = jnp.where(out1, 0.0, total[96:192])
+    hidden[4, 0:96] = jnp.where(gone, 0.0, beyond)
 
     lefts = []
     for r in at:
-        h = [hidden[k, pl.ds(r, 40), :].astype(BF) for k in range(4)]
-        h = [jnp.concatenate(h[2 * k : 2 * k + 2], axis=1) for k in range(2)]
-        lefts.append(jnp.concatenate(h, axis=0))
+        h = [hidden[k, pl.ds(r, 40), :].astype(BF) for k in range(5)]
+        lefts.append(jnp.concatenate([jnp.concatenate([h[k], h[k + 1]], axis=1) for k in (0, 2, 3)], axis=0))
     ctx = (taps_dot(lefts, w2_ref, 256) + b2_ref[...]).astype(BF).astype(F32)
     rows = []
     for k, x in enumerate((0, 30)):
@@ -350,11 +368,23 @@
             wide = ctx[40 * k + 24 * z : 40 * k + 24 * z + 16]
             patch[pl.ds(512 * z + x, 16, stride=32), :] = wide
             patch[pl.ds(512 * z + x + 1, 16, stride=32), :] = pltpu.roll(wide, 64, 1)
-            rows.append(wide)
+            rows.append(jnp.where(gx == 4, 0.0, wide) if k == 0 else wide)
     sums = sums_ref[...] + dot(rim_ref[:, :64], jnp.concatenate(rows, axis=0).astype(BF))
-    ctx_ref[...] = patch[...][:, :64].astype(BF)
     both = sums[:128] + pltpu.roll(sums[128:], 64, 1)
-    send_ref[...] = jnp.where(iota((128, 128), 1) < 64, both, face_ref[...])
+    lane = iota((128, 128), 1)
+    mine = jnp.where(lane < 64, both, face_ref[...]).astype(BF)
+
+    next_ctx = [ctx[80 + 24 * z : 96 + 24 * z] for z in range(2)]
+    right = jnp.concatenate([v for c in next_ctx for v in (c, pltpu.roll(c, 64, 1))], axis=0).astype(BF)
+    other = dot(got[0:64].T.astype(BF), right)
+    edge = jnp.broadcast_to(got[64:65], (128, 128)).T
+    other = jnp.where(lane < 64, other, jnp.where(lane == 97, edge, 0.0))
+    other = jnp.where(gx == 3, other, 0.0).astype(BF)
+    next_ctx = jnp.concatenate(next_ctx, axis=0).astype(BF)
+    for d in range(8):
+        send_ref[pl.ds(64 * d, 16), :] = mine[16 * d : 16 * d + 16]
+        send_ref[pl.ds(64 * d + 16, 16), :] = other[16 * d : 16 * d + 16]
+        send_ref[pl.ds(64 * d + 32, 32), :] = next_ctx
 
 
 def outer(*arrays):
@@ -362,25 +392,32 @@
         outer_kernel,
         in_specs=[pl.BlockSpec(memory_space=pltpu.VMEM)] * len(arrays),
         out_specs=[pl.BlockSpec(memory_space=pltpu.VMEM)] * 2,
-        out_shape=[pltpu.VMEM((1024, 64), BF), pltpu.VMEM((128, 128), F32)],
-        scratch_shapes=[
-            pltpu.VMEM((2, 152, 128), F32),
-            pltpu.VMEM((4, 96, 128), F32),
-            pltpu.VMEM((1024, 128), F32),
-        ],
+        out_shape=[pltpu.VMEM((1024, 128), F32), pltpu.VMEM((512, 128), BF)],
+        scratch_shapes=[pltpu.VMEM((3, 152, 128), F32), pltpu.VMEM((5, 96, 128), F32)],
         compiler_params=pltpu.CompilerParams(vmem_limit_bytes=16 << 20),
         cost_estimate=pl.CostEstimate(flops=200_000_000, bytes_accessed=3_000_000, transcendentals=0),
         name="outer",
     )(*arrays)
 
 
-def edge_kernel(rows_ref, ctx_ref, edge_emb_ref, edge_ctx_ref, out_ref, sent):
-    copy = pltpu.make_async_copy(ctx_ref, out_ref, sent)
+def edge_kernel(rows_ref, fine_ref, edge_emb_ref, edge_ctx_ref, out_ref, patch, final, sent):
+    patch[...] = fine_ref[...]
+
+    @pl.when(lax.axis_index("gx") == 4)
+    def _():
+        for z in range(2):
+            wide = rows_ref[pl.ds(64 * 3 + 32 + 16 * z, 16), :].astype(F32)
+            patch[pl.ds(512 * z, 16, stride=32), :] = wide
+            patch[pl.ds(512 * z + 1, 16, stride=32), :] = pltpu.roll(wide, 64, 1)
+
+    final[...] = patch[...][:, :64].astype(BF)
+    copy = pltpu.make_async_copy(final, out_ref, sent)
     copy.start()
-    rows = rows_ref[...]
-    hits = jnp.where(rows[:, 97:98] == iota((128, 64), 1).astype(F32), 1.0, 0.0).astype(BF)
-    sums = sum(dot(part, hits) for part in split3(rows.T))
-    scale = jnp.maximum(sums[96:97], 1.0)
+    rows = [rows_ref[pl.ds(64 * d + 16 * i, 16), :] for i in range(2) for d in range(8)]
+    rows = jnp.concatenate(rows, axis=0).astype(F32)
+    hits = jnp.where(rows[:, 97:98] == iota((256, 64), 1).astype(F32), 1.0, 0.0).astype(BF)
+    sums = dot(rows.T.astype(BF), hits)
+    scale = jnp.maximum(sums[96:97] + sums[98:99], 1.0)
     edge_ctx_ref[...] = sums[:64] / scale
     edge_emb_ref[...] = sums[64:96] / scale
     copy.wait()
@@ -396,7 +433,7 @@
             jax.ShapeDtypeStruct((64, 64), F32),
             jax.ShapeDtypeStruct((1024, 64), BF),
         ],
-        scratch_shapes=[pltpu.SemaphoreType.DMA],
+        scratch_shapes=[pltpu.VMEM((1024, 128), F32), pltpu.VMEM((1024, 64), BF), pltpu.SemaphoreType.DMA],
         name="edges",
     )(keep(rows), keep(context))
 
@@ -412,7 +449,7 @@
     own, voxels = pool(emb)
     zb = lax.ppermute(own, "gz", pairs(1, 8))
     za = lax.ppermute(own, "gz", pairs(0, 8))
-    cnt0, half = faces(0, voxels, slot, face_edge.reshape(1, 128))
+    cnt0, half, side0 = faces(0, voxels, slot, face_edge.reshape(1, 128))
     w1, w2 = jnp.swapaxes(conv1_w, 3, 4).reshape(27, 32, 64), conv2_w.reshape(27, 64, 64)
     zb, za, half = lax.optimization_barrier((zb, za, half))
     planes = [a.reshape(2, 16, 8, 128) for a in (za, own, zb)]
@@ -425,18 +462,20 @@
     to_a, to_b = lax.optimization_barrier((y_edge(y_even), y_edge(jnp.logical_not(y_even))))
     ya = lax.ppermute(to_a, "gy", pairs(0, 4))
     yb = lax.ppermute(to_b, "gy", pairs(1, 4))
-    cnt1, face = faces(1, voxels, slot, half)
+    cnt1, face, side1 = faces(1, voxels, slot, half)
     ya, yb, face = lax.optimization_barrier((ya, yb, face))
 
     def x_edge(g):
         mid = jnp.concatenate([a[:, :, g] for a in planes], axis=0)
-        return jnp.concatenate([mid, ya[:, :, g], yb[:, :, g]], axis=1)
+        return jnp.concatenate([mid, ya[:, :, g], yb[:, :, g]], axis=1).reshape(120, 128)
 
     low, high = x_edge(0), x_edge(7)
-    to_b, to_a, w1 = lax.optimization_barrier((jnp.where(x_even, low, high), jnp.where(x_even, high, low), w1))
+    to_b = jnp.concatenate([side0, side1, jnp.where(x_even, low, high)], axis=0)
+    to_a = jnp.concatenate([side0, side1, jnp.where(x_even, high, low)], axis=0)
+    to_b, to_a, w1 = lax.optimization_barrier((to_b, to_a, w1))
     w1a, w1b, w2a = bands(w1, w2)
     xa = lax.ppermute(to_a, "gx", pairs(0, 8))
-    xb = lax.ppermute(to_b, "gx", pairs(1, 8))
+    xb = lax.ppermute(to_b, "gx", [(1, 2), (2, 1), (5, 6), (6, 5), (4, 3)])
     twice = lambda b: jnp.concatenate([b, b]).reshape(1, 128)
     b1, b2 = twice(conv1_b), twice(conv2_b)
     w1a, w1b, w2a, cnt0, cnt1 = (keep(a) for a in (w1a, w1b, w2a, cnt0, cnt1))
@@ -444,7 +483,7 @@
         own, za, zb, ya.reshape(96, 128), yb.reshape(96, 128), w1a, w1b, b1, w2a, b2, cnt0, cnt1
     )
     context, send = outer(
-        xb, xa, keep(ends), keep(near), keep(fine), keep(sums), w1b, b1, w2a, b2, keep(rim), keep(face)
+        xb, xa, keep(ends), keep(near), keep(fine), keep(sums), w1a, w1b, b1, w2a, b2, keep(rim), keep(face)
     )
     rows = lax.all_to_all(send, "gx", 0, 0, tiled=True)
     edge_emb, edge_ctx, context = edges(rows, context)

time: 48 us -> 45.8 us (0.954)
  blocking collectives: 21.8 us -> 19.3 us
    all_to_all x1, blocking collectives: 21.8 us -> 19.3 us  [per_device(): rows = lax.all_to_all(send, 'gx', 0, 0, tiled=True)]
  transfers between devices with their start and end apart: 6 -> 6, of which waited for: 2 -> 2; matrix products, arithmetic and copies ran while one was open for 0% -> 0% of each run, Pallas kernels for 13% -> 14%
where the time goes in v7:
time: 45.8 us; the launch traced here: 45.3 us
  blocking collectives  19.3 us (42%)
  starting transfers between devices  12 us (26%)
  Pallas kernels  11.2 us (24%)
  waiting for transfers between devices  1.32 us (3%)
  between operations  0.99 us (2%)
    all_to_all x1, blocking collectives, per_device(): rows = lax.all_to_all(send, 'gx', 0, 0, tiled=True)  19.3 us
    ppermute x1, starting transfers between devices, per_device(): xa = lax.ppermute(to_a, 'gx', pairs(0, 8))  4.26 us
    pallas_call x2, Pallas kernels, faces(): pl.pallas_call(functools.partial(face_kernel, half), in_specs=[pl.BlockSp...  3.82 us
    ppermute x1, starting transfers between devices, per_device(): yb = lax.ppermute(to_b, 'gy', pairs(1, 4))  3.79 us
    pallas_call x1, Pallas kernels, pool(): pl.pallas_call(pool_kernel, in_specs=[pl.BlockSpec(memory_space=pl.ANY)],...  2.41 us
    pallas_call x1, Pallas kernels, inner(): pl.pallas_call(inner_kernel, in_specs=[pl.BlockSpec(memory_space=pltpu.VM...  2.12 us
    ppermute x1, starting transfers between devices, per_device(): zb = lax.ppermute(own, 'gz', pairs(1, 8))  2.11 us
    pallas_call x1, Pallas kernels, edges(): pl.pallas_call(edge_kernel, in_specs=[pl.BlockSpec(memory_space=pltpu.VME...  1.52 us
  transfers between devices with their start and end apart: 6, of which 2 were waited for; matrix products, arithmetic and copies ran while one was open for 0% of the time, Pallas kernels for 14%

profile of v7, /device:TPU:40, one launch (start us, length us, event | category | flops | bytes accessed | tf_op | source)
XLA Modules:
  0.0 45.3 jit_solution(2553367608103538411)
XLA Ops:
  0.6 0.0 copy-start.3
  0.6 0.0 copy-start
  0.7 2.4 %pool.1 = (bf16[256,128]{1,0:T(8,128)(2,1)S(1)}, bf16[32,256,128]{2,1,0:T(8,128)(2,1)S(1)}) custom-call(bf16[32,256,128]{2,1,0:T(8,128)(2,1)} %bitcast.56), custom_call_target="tpu_custom_call" | custom-call | flops 80000000 | bytes 2200000 | tf_op jit(solution)/shard_map/pool/pallas_call | solution.py:76
  3.1 0.1 collective-permute-start.1
  3.2 2.1 %collective-permute-start = (bf16[256,128]{1,0:T(8,128)(2,1)S(1)}, bf16[256,128]{1,0:T(8,128)(2,1)S(1)}, u32[]{:S(2)}, u32[]{:S(2)}) collective-permute-start(bf16[256,128]{1,0:T(8,128)(2,1)S(1)} %get-tuple-element.37.own_ref), channel_id=1, source_target_pairs={{32,64},{64,32},{96,128},{128,96},{160,192},{192,160},{33,65},{65,... | collective-permute-start | bytes 196616 | tf_op jit(solution)/shard_map/ppermute | solution.py:450
  5.4 0.0 copy-done.3
  5.4 0.0 copy-done
  5.4 2.0 %faces.2 = (bf16[2,256,128]{2,1,0:T(8,128)(2,1)S(1)}, f32[296,128]{1,0:T(8,128)S(1)}, bf16[32,128]{1,0:T(8,128)(2,1)S(1)}) custom-call(bf16[32,256,128]{2,1,0:T(8,128)(2,1)S(1)} %get-tuple-element.35.emb_ref, s32[256,128]{1,0:T(8,128)S(1)} %bitcast.41, s32[1,128]{1,0:T(1,128)S(1)} %bitcast.55), custom_call_target="tpu_custom_call" | custom-call | flops 1000000 | bytes 10000 | tf_op jit(solution)/shard_map/faces/pallas_call | solution.py:177
  7.5 0.0 copy-start.4
  7.5 0.0 copy-start.5
  7.5 0.0 copy-start.1
  7.5 0.0 copy-start.2
  7.5 0.0 collective-permute-done.1.za_ref
  7.5 1.2 %collective-permute-done.zb_ref = bf16[256,128]{1,0:T(8,128)(2,1)S(1)} collective-permute-done((bf16[256,128]{1,0:T(8,128)(2,1)S(1)}, bf16[256,128]{1,0:T(8,128)(2,1)S(1)}, u32[]{:S(2)}, u32[]{:S(2)}) %collective-permute-start) | collective-permute-done | bytes 65568 | tf_op jit(solution)/shard_map/ppermute | solution.py:450
  9.0 1.0 %collective-permute-start.2 = (bf16[6,2,8,128]{3,1,0,2:T(2,128)(2,1)S(1)}, bf16[6,2,8,128]{3,1,0,2:T(2,128)(2,1)S(1)}, u32[]{:S(2)}, u32[]{:S(2)}) collective-permute-start(bf16[6,2,8,128]{3,1,0,2:T(2,128)(2,1)S(1)} %pad_maximum_fusion.5), channel_id=1, source_target_pairs={{0,8},{8,0},{16,24},{24,16},{1,9},{9,1},{17,25},{25,17},{2,10},{10... | collective-permute-start | bytes 73736 | tf_op jit(solution)/shard_map/ppermute | solution.py:463
  10.0 3.8 %collective-permute-start.3 = (bf16[6,2,8,128]{3,1,0,2:T(2,128)(2,1)S(1)}, bf16[6,2,8,128]{3,1,0,2:T(2,128)(2,1)S(1)}, u32[]{:S(2)}, u32[]{:S(2)}) collective-permute-start(bf16[6,2,8,128]{3,1,0,2:T(2,128)(2,1)S(1)} %pad_maximum_fusion.6), channel_id=1, source_target_pairs={{8,16},{16,8},{9,17},{17,9},{10,18},{18,10},{11,19},{19,11},{12,20... | collective-permute-start | bytes 73736 | tf_op jit(solution)/shard_map/ppermute | solution.py:464
  13.9 1.8 %faces.3 = (bf16[2,256,128]{2,1,0:T(8,128)(2,1)S(1)}, f32[128,128]{1,0:T(8,128)S(1)}, bf16[48,128]{1,0:T(8,128)(2,1)S(1)}) custom-call(bf16[32,256,128]{2,1,0:T(8,128)(2,1)S(1)} %get-tuple-element.35.emb_ref, s32[256,128]{1,0:T(8,128)S(1)} %bitcast.42, f32[296,128]{1,0:T(8,128)S(1)} %get-tuple-element.39.given_ref), custom_call_target="tpu_custom_call" | custom-call | flops 1000000 | bytes 10000 | tf_op jit(solution)/shard_map/faces/pallas_call | solution.py:177
  15.7 0.0 collective-permute-done.2
  15.7 0.1 collective-permute-done.3
  15.9 0.7 %collective-permute-start.4 = (bf16[200,128]{1,0:T(8,128)(2,1)S(1)}, bf16[200,128]{1,0:T(8,128)(2,1)S(1)}, u32[]{:S(2)}, u32[]{:S(2)}) collective-permute-start(bf16[200,128]{1,0:T(8,128)(2,1)S(1)} %get-tuple-element.48), channel_id=1, source_target_pairs={{1,2},{2,1},{5,6},{6,5},{4,3},{9,10},{10,9},{13,14},{14,13},{12,11... | collective-permute-start | bytes 153608 | tf_op jit(solution)/shard_map/ppermute | solution.py:478
  16.6 4.3 %collective-permute-start.5 = (bf16[200,128]{1,0:T(8,128)(2,1)S(1)}, bf16[200,128]{1,0:T(8,128)(2,1)S(1)}, u32[]{:S(2)}, u32[]{:S(2)}) collective-permute-start(bf16[200,128]{1,0:T(8,128)(2,1)S(1)} %get-tuple-element.49), channel_id=1, source_target_pairs={{0,1},{1,0},{2,3},{3,2},{4,5},{5,4},{6,7},{7,6},{8,9},{9,8},{10,11... | collective-permute-start | bytes 153608 | tf_op jit(solution)/shard_map/ppermute | solution.py:477
  20.8 0.0 copy-done.4
  20.8 0.0 copy-done.5
  20.8 0.1 maximum_bitcast_fusion
  20.9 0.0 copy-done.1
  20.9 0.0 copy-done.2
  21.0 0.4 bands.1
  21.4 2.1 %inner.1 = (f32[1024,128]{1,0:T(8,128)S(1)}, f32[256,128]{1,0:T(8,128)S(1)}, f32[2,144,128]{2,1,0:T(8,128)S(1)}, f32[2,96,128]{2,1,0:T(8,128)S(1)}, bf16[256,128]{1,0:T(8,128)(2,1)S(1)}) custom-call(bf16[256,128]{1,0:T(8,128)(2,1)S(1)} %get-tuple-element.37.own_ref, bf16[256,128]{1,0:T(8,128)(2,1)S(1)} %collective-permute-done.1.za_ref, ...), custom_call_target="tpu_custom_call" | custom-call | flops 1000000 | bytes 10000 | tf_op jit(solution)/shard_map/inner/pallas_call | solution.py:295
  23.5 0.0 collective-permute-done.4.xb_ref
  23.5 0.0 collective-permute-done.5.xa_ref
  23.5 0.9 %outer.1 = (f32[1024,128]{1,0:T(8,128)S(1)}, bf16[512,128]{1,0:T(8,128)(2,1)S(1)}) custom-call(bf16[200,128]{1,0:T(8,128)(2,1)S(1)} %collective-permute-done.4.xb_ref, bf16[200,128]{1,0:T(8,128)(2,1)S(1)} %collective-permute-done.5.xa_ref, f32[2,144,128]{2,1,0:T(8,128)S(1)} %get-tuple-element.56.ends_ref, f32[2,96,128]{2,1,0:T(8,128)S(1)} %get-tuple-element.57.near_ref, ...), custom_call_target="tpu_custom_call" | custom-call | flops 200000000 | bytes 3000000 | tf_op jit(solution)/shard_map/outer/pallas_call | solution.py:391
  24.4 19.3 %all_to_all.11 = bf16[8,64,128]{2,1,0:T(8,128)(2,1)S(1)} all-to-all(bf16[8,64,128]{2,1,0:T(8,128)(2,1)S(1)} %bitcast.52), channel_id=1, replica_groups=mesh['gz'=8,'gy'=4,'gx'=8] {'gx'}, dimensions={0} | all-to-all | bytes 262144 | tf_op jit(solution)/shard_map/all_to_all | solution.py:488
  43.7 1.5 %edges.1 = (f32[32,64]{1,0:T(8,128)}, f32[64,64]{1,0:T(8,128)}, bf16[1024,64]{1,0:T(8,128)(2,1)}) custom-call(bf16[512,128]{1,0:T(8,128)(2,1)S(1)} %bitcast.43, f32[1024,128]{1,0:T(8,128)S(1)} %get-tuple-element.63.fine_ref), custom_call_target="tpu_custom_call" | custom-call | tf_op jit(solution)/shard_map/edges/pallas_call | solution.py:427
  (25 shorter events, 0.4 us)
Async XLA Ops:
  0.6 4.8 %copy-start.3 = (s32[128]{0:T(128)S(1)}, s32[128]{0:T(128)}, u32[]{:S(2)}) copy-start(s32[128]{0:T(128)} %param.9) | copy-start | bytes 1540
  0.6 4.8 %copy-start = (s32[4,64,128]{2,1,0:T(8,128)S(1)}, s32[4,64,128]{2,1,0:T(8,128)}, u32[]{:S(2)}) copy-start(s32[4,64,128]{2,1,0:T(8,128)} %param.8) | copy-start | bytes 393220
  3.1 4.4 %collective-permute-start.1 = (bf16[256,128]{1,0:T(8,128)(2,1)S(1)}, bf16[256,128]{1,0:T(8,128)(2,1)S(1)}, u32[]{:S(2)}, u32[]{:S(2)}) collective-permute-start(bf16[256,128]{1,0:T(8,128)(2,1)S(1)} %get-tuple-element.37.own_ref), channel_id=1, source_target_pairs={{0,32},{32,0},{64,96},{96,64},{128,160},{160,128},{192,224},{224,1... | collective-permute-start | bytes 196616 | tf_op jit(solution)/shard_map/ppermute | solution.py:451
  3.2 5.6 %collective-permute-start = (bf16[256,128]{1,0:T(8,128)(2,1)S(1)}, bf16[256,128]{1,0:T(8,128)(2,1)S(1)}, u32[]{:S(2)}, u32[]{:S(2)}) collective-permute-start(bf16[256,128]{1,0:T(8,128)(2,1)S(1)} %get-tuple-element.37.own_ref), channel_id=1, source_target_pairs={{32,64},{64,32},{96,128},{128,96},{160,192},{192,160},{33,65},{65,... | collective-permute-start | bytes 196616 | tf_op jit(solution)/shard_map/ppermute | solution.py:450
  7.5 13.4 %copy-start.4 = (f32[64]{0:T(128)S(1)}, f32[64]{0:T(128)}, u32[]{:S(2)}) copy-start(f32[64]{0:T(128)} %param.11) | copy-start | bytes 772
  7.5 13.4 %copy-start.5 = (f32[64]{0:T(128)S(1)}, f32[64]{0:T(128)}, u32[]{:S(2)}) copy-start(f32[64]{0:T(128)} %param.13) | copy-start | bytes 772
  7.5 13.5 %copy-start.1 = (bf16[3,3,3,64,64]{4,3,2,1,0:T(8,128)(2,1)S(1)}, bf16[3,3,3,64,64]{4,3,2,1,0:T(8,128)(2,1)}, u32[]{:S(2)}) copy-start(bf16[3,3,3,64,64]{4,3,2,1,0:T(8,128)(2,1)} %param.12) | copy-start | bytes 663556
  7.5 13.5 %copy-start.2 = (bf16[3,3,3,64,32]{3,4,2,1,0:T(8,128)(2,1)S(1)}, bf16[3,3,3,64,32]{3,4,2,1,0:T(8,128)(2,1)}, u32[]{:S(2)}) copy-start(bf16[3,3,3,64,32]{3,4,2,1,0:T(8,128)(2,1)} %param.10) | copy-start | bytes 331780
  9.0 6.7 %collective-permute-start.2 = (bf16[6,2,8,128]{3,1,0,2:T(2,128)(2,1)S(1)}, bf16[6,2,8,128]{3,1,0,2:T(2,128)(2,1)S(1)}, u32[]{:S(2)}, u32[]{:S(2)}) collective-permute-start(bf16[6,2,8,128]{3,1,0,2:T(2,128)(2,1)S(1)} %pad_maximum_fusion.5), channel_id=1, source_target_pairs={{0,8},{8,0},{16,24},{24,16},{1,9},{9,1},{17,25},{25,17},{2,10},{10... | collective-permute-start | bytes 73736 | tf_op jit(solution)/shard_map/ppermute | solution.py:463
  10.0 5.7 %collective-permute-start.3 = (bf16[6,2,8,128]{3,1,0,2:T(2,128)(2,1)S(1)}, bf16[6,2,8,128]{3,1,0,2:T(2,128)(2,1)S(1)}, u32[]{:S(2)}, u32[]{:S(2)}) collective-permute-start(bf16[6,2,8,128]{3,1,0,2:T(2,128)(2,1)S(1)} %pad_maximum_fusion.6), channel_id=1, source_target_pairs={{8,16},{16,8},{9,17},{17,9},{10,18},{18,10},{11,19},{19,11},{12,20... | collective-permute-start | bytes 73736 | tf_op jit(solution)/shard_map/ppermute | solution.py:464
  15.9 7.6 %collective-permute-start.4 = (bf16[200,128]{1,0:T(8,128)(2,1)S(1)}, bf16[200,128]{1,0:T(8,128)(2,1)S(1)}, u32[]{:S(2)}, u32[]{:S(2)}) collective-permute-start(bf16[200,128]{1,0:T(8,128)(2,1)S(1)} %get-tuple-element.48), channel_id=1, source_target_pairs={{1,2},{2,1},{5,6},{6,5},{4,3},{9,10},{10,9},{13,14},{14,13},{12,11... | collective-permute-start | bytes 153608 | tf_op jit(solution)/shard_map/ppermute | solution.py:478
  16.6 6.9 %collective-permute-start.5 = (bf16[200,128]{1,0:T(8,128)(2,1)S(1)}, bf16[200,128]{1,0:T(8,128)(2,1)S(1)}, u32[]{:S(2)}, u32[]{:S(2)}) collective-permute-start(bf16[200,128]{1,0:T(8,128)(2,1)S(1)} %get-tuple-element.49), channel_id=1, source_target_pairs={{0,1},{1,0},{2,3},{3,2},{4,5},{5,4},{6,7},{7,6},{8,9},{9,8},{10,11... | collective-permute-start | bytes 153608 | tf_op jit(solution)/shard_map/ppermute | solution.py:477

commit v8 on v7

--- a/solution.py
+++ b/solution.py
@@ -319,15 +319,14 @@
     )(*arrays)
 
 
-def outer_kernel(xb_ref, xa_ref, ends_ref, near_ref, fine_ref, sums_ref, w1a_ref, w1b_ref, b1_ref, w2_ref, b2_ref, rim_ref,
-                 face_ref, patch, send_ref, column, hidden):
+def outer_kernel(xb_ref, xa_ref, ends_ref, near_ref, sums_ref, w1a_ref, w1b_ref, b1_ref, w2_ref, b2_ref, rim_ref,
+                 face_ref, edge_ref, send_ref, column, hidden):
     gz, gy, gx = (lax.axis_index(a) for a in ("gz", "gy", "gx"))
     z_even, y_even, x_even = (gz & 1) == 0, (gy & 1) == 0, (gx & 1) == 0
     lane = iota((24, 128), 1)
     column[...] = jnp.zeros_like(column)
-    patch[...] = fine_ref[...]
     got = xb_ref[...].astype(F32)
-    for k, whole in enumerate(ordered(x_even, xa_ref[80:200].astype(F32), got[80:200])):
+    for k, whole in enumerate(ordered(x_even, xa_ref[80:208].astype(F32), got[80:208])):
         planes = [whole[20 * i : 20 * i + 20] for i in range(6)]
         low0, high0 = ordered(z_even, planes[0], planes[4])
         low1, high1 = ordered(z_even, planes[1], planes[5])
@@ -363,11 +362,10 @@
         lefts.append(jnp.concatenate([jnp.concatenate([h[k], h[k + 1]], axis=1) for k in (0, 2, 3)], axis=0))
     ctx = (taps_dot(lefts, w2_ref, 256) + b2_ref[...]).astype(BF).astype(F32)
     rows = []
-    for k, x in enumerate((0, 30)):
+    for k in range(2):
         for z in range(2):
             wide = ctx[40 * k + 24 * z : 40 * k + 24 * z + 16]
-            patch[pl.ds(512 * z + x, 16, stride=32), :] = wide
-            patch[pl.ds(512 * z + x + 1, 16, stride=32), :] = pltpu.roll(wide, 64, 1)
+            edge_ref[pl.ds(32 * k + 16 * z, 16), :] = wide
             rows.append(jnp.where(gx == 4, 0.0, wide) if k == 0 else wide)
     sums = sums_ref[...] + dot(rim_ref[:, :64], jnp.concatenate(rows, axis=0).astype(BF))
     both = sums[:128] + pltpu.roll(sums[128:], 64, 1)
@@ -392,7 +390,7 @@
         outer_kernel,
         in_specs=[pl.BlockSpec(memory_space=pltpu.VMEM)] * len(arrays),
         out_specs=[pl.BlockSpec(memory_space=pltpu.VMEM)] * 2,
-        out_shape=[pltpu.VMEM((1024, 128), F32), pltpu.VMEM((512, 128), BF)],
+        out_shape=[pltpu.VMEM((64, 128), F32), pltpu.VMEM((512, 128), BF)],
         scratch_shapes=[pltpu.VMEM((3, 152, 128), F32), pltpu.VMEM((5, 96, 128), F32)],
         compiler_params=pltpu.CompilerParams(vmem_limit_bytes=16 << 20),
         cost_estimate=pl.CostEstimate(flops=200_000_000, bytes_accessed=3_000_000, transcendentals=0),
@@ -400,16 +398,16 @@
     )(*arrays)
 
 
-def edge_kernel(rows_ref, fine_ref, edge_emb_ref, edge_ctx_ref, out_ref, patch, final, sent):
+def edge_kernel(rows_ref, fine_ref, rim_ref, edge_emb_ref, edge_ctx_ref, out_ref, patch, final, sent):
     patch[...] = fine_ref[...]
-
-    @pl.when(lax.axis_index("gx") == 4)
-    def _():
+    given = lax.axis_index("gx") == 4
+    for k, x in enumerate((0, 30)):
         for z in range(2):
-            wide = rows_ref[pl.ds(64 * 3 + 32 + 16 * z, 16), :].astype(F32)
-            patch[pl.ds(512 * z, 16, stride=32), :] = wide
-            patch[pl.ds(512 * z + 1, 16, stride=32), :] = pltpu.roll(wide, 64, 1)
-
+            wide = rim_ref[pl.ds(32 * k + 16 * z, 16), :]
+            if k == 0:
+                wide = jnp.where(given, rows_ref[pl.ds(64 * 3 + 32 + 16 * z, 16), :].astype(F32), wide)
+            patch[pl.ds(512 * z + x, 16, stride=32), :] = wide
+            patch[pl.ds(512 * z + x + 1, 16, stride=32), :] = pltpu.roll(wide, 64, 1)
     final[...] = patch[...][:, :64].astype(BF)
     copy = pltpu.make_async_copy(final, out_ref, sent)
     copy.start()
@@ -423,10 +421,10 @@
     copy.wait()
 
 
-def edges(rows, context):
+def edges(rows, fine, rim):
     return pl.pallas_call(
         edge_kernel,
-        in_specs=[pl.BlockSpec(memory_space=pltpu.VMEM)] * 2,
+        in_specs=[pl.BlockSpec(memory_space=pltpu.VMEM)] * 3,
         out_specs=[pl.BlockSpec(memory_space=pltpu.VMEM)] * 2 + [pl.BlockSpec(memory_space=pl.ANY)],
         out_shape=[
             jax.ShapeDtypeStruct((32, 64), F32),
@@ -435,7 +433,7 @@
         ],
         scratch_shapes=[pltpu.VMEM((1024, 128), F32), pltpu.VMEM((1024, 64), BF), pltpu.SemaphoreType.DMA],
         name="edges",
-    )(keep(rows), keep(context))
+    )(keep(rows), keep(fine), keep(rim))
 
 
 def pairs(first, count):
@@ -470,8 +468,9 @@
         return jnp.concatenate([mid, ya[:, :, g], yb[:, :, g]], axis=1).reshape(120, 128)
 
     low, high = x_edge(0), x_edge(7)
-    to_b = jnp.concatenate([side0, side1, jnp.where(x_even, low, high)], axis=0)
-    to_a = jnp.concatenate([side0, side1, jnp.where(x_even, high, low)], axis=0)
+    rest = jnp.zeros((8, 128), BF)
+    to_b = jnp.concatenate([side0, side1, jnp.where(x_even, low, high), rest], axis=0)
+    to_a = jnp.concatenate([side0, side1, jnp.where(x_even, high, low), rest], axis=0)
     to_b, to_a, w1 = lax.optimization_barrier((to_b, to_a, w1))
     w1a, w1b, w2a = bands(w1, w2)
     xa = lax.ppermute(to_a, "gx", pairs(0, 8))
@@ -482,11 +481,11 @@
     fine, sums, ends, near, rim = inner(
         own, za, zb, ya.reshape(96, 128), yb.reshape(96, 128), w1a, w1b, b1, w2a, b2, cnt0, cnt1
     )
-    context, send = outer(
-        xb, xa, keep(ends), keep(near), keep(fine), keep(sums), w1a, w1b, b1, w2a, b2, keep(rim), keep(face)
+    rim_ctx, send = outer(
+        xb, xa, keep(ends), keep(near), keep(sums), w1a, w1b, b1, w2a, b2, keep(rim), keep(face)
     )
     rows = lax.all_to_all(send, "gx", 0, 0, tiled=True)
-    edge_emb, edge_ctx, context = edges(rows, context)
+    edge_emb, edge_ctx, context = edges(rows, fine, rim_ctx)
     context = jnp.transpose(context.reshape(2, 16, 32, 64), (3, 0, 1, 2))
     return (context, edge_emb, edge_ctx)
 

time: 45.8 us -> 46 us (level)
  transfers between devices with their start and end apart: 6 -> 6, of which waited for: 2 -> 2; matrix products, arithmetic and copies ran while one was open for 0% -> 1% of each run, Pallas kernels for 14% -> 14%
where the time goes in v8:
time: 46 us; the launch traced here: 45.4 us
  blocking collectives  19.3 us (42%)
  starting transfers between devices  11.9 us (26%)
  Pallas kernels  11.3 us (25%)
  waiting for transfers between devices  1.32 us (3%)
  between operations  0.99 us (2%)
    all_to_all x1, blocking collectives, per_device(): rows = lax.all_to_all(send, 'gx', 0, 0, tiled=True)  19.3 us
    ppermute x1, starting transfers between devices, per_device(): xa = lax.ppermute(to_a, 'gx', pairs(0, 8))  4.19 us
    pallas_call x2, Pallas kernels, faces(): pl.pallas_call(functools.partial(face_kernel, half), in_specs=[pl.BlockSp...  3.82 us
    ppermute x1, starting transfers between devices, per_device(): yb = lax.ppermute(to_b, 'gy', pairs(1, 4))  3.73 us
    pallas_call x1, Pallas kernels, pool(): pl.pallas_call(pool_kernel, in_specs=[pl.BlockSpec(memory_space=pl.ANY)],...  2.41 us
    pallas_call x1, Pallas kernels, inner(): pl.pallas_call(inner_kernel, in_specs=[pl.BlockSpec(memory_space=pltpu.VM...  2.14 us
    ppermute x1, starting transfers between devices, per_device(): zb = lax.ppermute(own, 'gz', pairs(1, 8))  2.11 us
    pallas_call x1, Pallas kernels, edges(): pl.pallas_call(edge_kernel, in_specs=[pl.BlockSpec(memory_space=pltpu.VME...  1.58 us
  transfers between devices with their start and end apart: 6, of which 2 were waited for; matrix products, arithmetic and copies ran while one was open for 1% of the time, Pallas kernels for 14%

profile of v8, /device:TPU:40, one launch (start us, length us, event | category | flops | bytes accessed | tf_op | source)
XLA Modules:
  0.0 45.4 jit_solution(8840893904778804924)
XLA Ops:
  0.6 0.0 copy-start.3
  0.6 0.0 copy-start
  0.7 2.4 %pool.1 = (bf16[256,128]{1,0:T(8,128)(2,1)S(1)}, bf16[32,256,128]{2,1,0:T(8,128)(2,1)S(1)}) custom-call(bf16[32,256,128]{2,1,0:T(8,128)(2,1)} %bitcast.56), custom_call_target="tpu_custom_call" | custom-call | flops 80000000 | bytes 2200000 | tf_op jit(solution)/shard_map/pool/pallas_call | solution.py:76
  3.1 0.1 collective-permute-start.1
  3.2 2.1 %collective-permute-start = (bf16[256,128]{1,0:T(8,128)(2,1)S(1)}, bf16[256,128]{1,0:T(8,128)(2,1)S(1)}, u32[]{:S(2)}, u32[]{:S(2)}) collective-permute-start(bf16[256,128]{1,0:T(8,128)(2,1)S(1)} %get-tuple-element.37.own_ref), channel_id=1, source_target_pairs={{32,64},{64,32},{96,128},{128,96},{160,192},{192,160},{33,65},{65,... | collective-permute-start | bytes 196616 | tf_op jit(solution)/shard_map/ppermute | solution.py:448
  5.4 0.1 pad.11.clone
  5.5 0.0 copy-done.3
  5.5 0.0 copy-done
  5.5 2.0 %faces.2 = (bf16[2,256,128]{2,1,0:T(8,128)(2,1)S(1)}, f32[296,128]{1,0:T(8,128)S(1)}, bf16[32,128]{1,0:T(8,128)(2,1)S(1)}) custom-call(bf16[32,256,128]{2,1,0:T(8,128)(2,1)S(1)} %get-tuple-element.35.emb_ref, s32[256,128]{1,0:T(8,128)S(1)} %bitcast.41, s32[1,128]{1,0:T(1,128)S(1)} %bitcast.55), custom_call_target="tpu_custom_call" | custom-call | flops 1000000 | bytes 10000 | tf_op jit(solution)/shard_map/faces/pallas_call | solution.py:177
  7.5 0.0 copy-start.4
  7.5 0.0 copy-start.5
  7.5 0.0 copy-start.1
  7.6 0.0 copy-start.2
  7.6 0.0 collective-permute-done.1.za_ref
  7.6 1.2 %collective-permute-done.zb_ref = bf16[256,128]{1,0:T(8,128)(2,1)S(1)} collective-permute-done((bf16[256,128]{1,0:T(8,128)(2,1)S(1)}, bf16[256,128]{1,0:T(8,128)(2,1)S(1)}, u32[]{:S(2)}, u32[]{:S(2)}) %collective-permute-start) | collective-permute-done | bytes 65568 | tf_op jit(solution)/shard_map/ppermute | solution.py:448
  9.0 1.1 %collective-permute-start.2 = (bf16[6,2,8,128]{3,1,0,2:T(2,128)(2,1)S(1)}, bf16[6,2,8,128]{3,1,0,2:T(2,128)(2,1)S(1)}, u32[]{:S(2)}, u32[]{:S(2)}) collective-permute-start(bf16[6,2,8,128]{3,1,0,2:T(2,128)(2,1)S(1)} %pad_maximum_fusion.3), channel_id=1, source_target_pairs={{0,8},{8,0},{16,24},{24,16},{1,9},{9,1},{17,25},{25,17},{2,10},{10... | collective-permute-start | bytes 73736 | tf_op jit(solution)/shard_map/ppermute | solution.py:461
  10.1 3.7 %collective-permute-start.3 = (bf16[6,2,8,128]{3,1,0,2:T(2,128)(2,1)S(1)}, bf16[6,2,8,128]{3,1,0,2:T(2,128)(2,1)S(1)}, u32[]{:S(2)}, u32[]{:S(2)}) collective-permute-start(bf16[6,2,8,128]{3,1,0,2:T(2,128)(2,1)S(1)} %pad_maximum_fusion.4), channel_id=1, source_target_pairs={{8,16},{16,8},{9,17},{17,9},{10,18},{18,10},{11,19},{19,11},{12,20... | collective-permute-start | bytes 73736 | tf_op jit(solution)/shard_map/ppermute | solution.py:462
  13.9 1.8 %faces.3 = (bf16[2,256,128]{2,1,0:T(8,128)(2,1)S(1)}, f32[128,128]{1,0:T(8,128)S(1)}, bf16[48,128]{1,0:T(8,128)(2,1)S(1)}) custom-call(bf16[32,256,128]{2,1,0:T(8,128)(2,1)S(1)} %get-tuple-element.35.emb_ref, s32[256,128]{1,0:T(8,128)S(1)} %bitcast.42, f32[296,128]{1,0:T(8,128)S(1)} %get-tuple-element.39.given_ref), custom_call_target="tpu_custom_call" | custom-call | flops 1000000 | bytes 10000 | tf_op jit(solution)/shard_map/faces/pallas_call | solution.py:177
  15.7 0.0 collective-permute-done.2
  15.7 0.1 collective-permute-done.3
  15.9 0.1 maximum_maximum_fusion.1
  16.1 0.7 %collective-permute-start.4 = (bf16[208,128]{1,0:T(8,128)(2,1)S(1)}, bf16[208,128]{1,0:T(8,128)(2,1)S(1)}, u32[]{:S(2)}, u32[]{:S(2)}) collective-permute-start(bf16[208,128]{1,0:T(8,128)(2,1)S(1)} %get-tuple-element.48), channel_id=1, source_target_pairs={{1,2},{2,1},{5,6},{6,5},{4,3},{9,10},{10,9},{13,14},{14,13},{12,11... | collective-permute-start | bytes 159752 | tf_op jit(solution)/shard_map/ppermute | solution.py:477
  16.7 4.2 %collective-permute-start.5 = (bf16[208,128]{1,0:T(8,128)(2,1)S(1)}, bf16[208,128]{1,0:T(8,128)(2,1)S(1)}, u32[]{:S(2)}, u32[]{:S(2)}) collective-permute-start(bf16[208,128]{1,0:T(8,128)(2,1)S(1)} %get-tuple-element.49), channel_id=1, source_target_pairs={{0,1},{1,0},{2,3},{3,2},{4,5},{5,4},{6,7},{7,6},{8,9},{9,8},{10,11... | collective-permute-start | bytes 159752 | tf_op jit(solution)/shard_map/ppermute | solution.py:476
  20.9 0.0 copy-done.4
  20.9 0.0 copy-done.5
  20.9 0.1 maximum_bitcast_fusion
  21.0 0.0 copy-done.1
  21.0 0.0 copy-done.2
  21.0 0.4 bands.1
  21.5 2.1 %inner.1 = (f32[1024,128]{1,0:T(8,128)S(1)}, f32[256,128]{1,0:T(8,128)S(1)}, f32[2,144,128]{2,1,0:T(8,128)S(1)}, f32[2,96,128]{2,1,0:T(8,128)S(1)}, bf16[256,128]{1,0:T(8,128)(2,1)S(1)}) custom-call(bf16[256,128]{1,0:T(8,128)(2,1)S(1)} %get-tuple-element.37.own_ref, bf16[256,128]{1,0:T(8,128)(2,1)S(1)} %collective-permute-done.1.za_ref, ...), custom_call_target="tpu_custom_call" | custom-call | flops 1000000 | bytes 10000 | tf_op jit(solution)/shard_map/inner/pallas_call | solution.py:295
  23.6 0.0 collective-permute-done.4.xb_ref
  23.6 0.0 collective-permute-done.5.xa_ref
  23.6 0.9 %outer.1 = (f32[64,128]{1,0:T(8,128)S(1)}, bf16[512,128]{1,0:T(8,128)(2,1)S(1)}) custom-call(bf16[208,128]{1,0:T(8,128)(2,1)S(1)} %collective-permute-done.4.xb_ref, bf16[208,128]{1,0:T(8,128)(2,1)S(1)} %collective-permute-done.5.xa_ref, f32[2,144,128]{2,1,0:T(8,128)S(1)} %get-tuple-element.56.ends_ref, f32[2,96,128]{2,1,0:T(8,128)S(1)} %get-tuple-element.57.near_ref, ...), custom_call_target="tpu_custom_call" | custom-call | flops 200000000 | bytes 3000000 | tf_op jit(solution)/shard_map/outer/pallas_call | solution.py:389
  24.6 19.3 %all_to_all.11 = bf16[8,64,128]{2,1,0:T(8,128)(2,1)S(1)} all-to-all(bf16[8,64,128]{2,1,0:T(8,128)(2,1)S(1)} %bitcast.52), channel_id=1, replica_groups=mesh['gz'=8,'gy'=4,'gx'=8] {'gx'}, dimensions={0} | all-to-all | bytes 262144 | tf_op jit(solution)/shard_map/all_to_all | solution.py:487
  43.8 1.6 %edges.1 = (f32[32,64]{1,0:T(8,128)}, f32[64,64]{1,0:T(8,128)}, bf16[1024,64]{1,0:T(8,128)(2,1)}) custom-call(bf16[512,128]{1,0:T(8,128)(2,1)S(1)} %bitcast.43, f32[1024,128]{1,0:T(8,128)S(1)} %get-tuple-element.62.fine_ref, f32[64,128]{1,0:T(8,128)S(1)} %get-tuple-element.63.rim_ref), custom_call_target="tpu_custom_call" | custom-call | tf_op jit(solution)/shard_map/edges/pallas_call | solution.py:425
  (25 shorter events, 0.4 us)
Async XLA Ops:
  0.6 4.9 %copy-start.3 = (s32[128]{0:T(128)S(1)}, s32[128]{0:T(128)}, u32[]{:S(2)}) copy-start(s32[128]{0:T(128)} %param.9) | copy-start | bytes 1540
  0.6 4.8 %copy-start = (s32[4,64,128]{2,1,0:T(8,128)S(1)}, s32[4,64,128]{2,1,0:T(8,128)}, u32[]{:S(2)}) copy-start(s32[4,64,128]{2,1,0:T(8,128)} %param.8) | copy-start | bytes 393220
  3.1 4.5 %collective-permute-start.1 = (bf16[256,128]{1,0:T(8,128)(2,1)S(1)}, bf16[256,128]{1,0:T(8,128)(2,1)S(1)}, u32[]{:S(2)}, u32[]{:S(2)}) collective-permute-start(bf16[256,128]{1,0:T(8,128)(2,1)S(1)} %get-tuple-element.37.own_ref), channel_id=1, source_target_pairs={{0,32},{32,0},{64,96},{96,64},{128,160},{160,128},{192,224},{224,1... | collective-permute-start | bytes 196616 | tf_op jit(solution)/shard_map/ppermute | solution.py:449
  3.2 5.6 %collective-permute-start = (bf16[256,128]{1,0:T(8,128)(2,1)S(1)}, bf16[256,128]{1,0:T(8,128)(2,1)S(1)}, u32[]{:S(2)}, u32[]{:S(2)}) collective-permute-start(bf16[256,128]{1,0:T(8,128)(2,1)S(1)} %get-tuple-element.37.own_ref), channel_id=1, source_target_pairs={{32,64},{64,32},{96,128},{128,96},{160,192},{192,160},{33,65},{65,... | collective-permute-start | bytes 196616 | tf_op jit(solution)/shard_map/ppermute | solution.py:448
  7.5 13.4 %copy-start.4 = (f32[64]{0:T(128)S(1)}, f32[64]{0:T(128)}, u32[]{:S(2)}) copy-start(f32[64]{0:T(128)} %param.11) | copy-start | bytes 772
  7.5 13.4 %copy-start.5 = (f32[64]{0:T(128)S(1)}, f32[64]{0:T(128)}, u32[]{:S(2)}) copy-start(f32[64]{0:T(128)} %param.13) | copy-start | bytes 772
  7.5 13.5 %copy-start.1 = (bf16[3,3,3,64,64]{4,3,2,1,0:T(8,128)(2,1)S(1)}, bf16[3,3,3,64,64]{4,3,2,1,0:T(8,128)(2,1)}, u32[]{:S(2)}) copy-start(bf16[3,3,3,64,64]{4,3,2,1,0:T(8,128)(2,1)} %param.12) | copy-start | bytes 663556
  7.6 13.5 %copy-start.2 = (bf16[3,3,3,64,32]{3,4,2,1,0:T(8,128)(2,1)S(1)}, bf16[3,3,3,64,32]{3,4,2,1,0:T(8,128)(2,1)}, u32[]{:S(2)}) copy-start(bf16[3,3,3,64,32]{3,4,2,1,0:T(8,128)(2,1)} %param.10) | copy-start | bytes 331780
  9.0 6.7 %collective-permute-start.2 = (bf16[6,2,8,128]{3,1,0,2:T(2,128)(2,1)S(1)}, bf16[6,2,8,128]{3,1,0,2:T(2,128)(2,1)S(1)}, u32[]{:S(2)}, u32[]{:S(2)}) collective-permute-start(bf16[6,2,8,128]{3,1,0,2:T(2,128)(2,1)S(1)} %pad_maximum_fusion.3), channel_id=1, source_target_pairs={{0,8},{8,0},{16,24},{24,16},{1,9},{9,1},{17,25},{25,17},{2,10},{10... | collective-permute-start | bytes 73736 | tf_op jit(solution)/shard_map/ppermute | solution.py:461
  10.1 5.7 %collective-permute-start.3 = (bf16[6,2,8,128]{3,1,0,2:T(2,128)(2,1)S(1)}, bf16[6,2,8,128]{3,1,0,2:T(2,128)(2,1)S(1)}, u32[]{:S(2)}, u32[]{:S(2)}) collective-permute-start(bf16[6,2,8,128]{3,1,0,2:T(2,128)(2,1)S(1)} %pad_maximum_fusion.4), channel_id=1, source_target_pairs={{8,16},{16,8},{9,17},{17,9},{10,18},{18,10},{11,19},{19,11},{12,20... | collective-permute-start | bytes 73736 | tf_op jit(solution)/shard_map/ppermute | solution.py:462
  16.1 7.6 %collective-permute-start.4 = (bf16[208,128]{1,0:T(8,128)(2,1)S(1)}, bf16[208,128]{1,0:T(8,128)(2,1)S(1)}, u32[]{:S(2)}, u32[]{:S(2)}) collective-permute-start(bf16[208,128]{1,0:T(8,128)(2,1)S(1)} %get-tuple-element.48), channel_id=1, source_target_pairs={{1,2},{2,1},{5,6},{6,5},{4,3},{9,10},{10,9},{13,14},{14,13},{12,11... | collective-permute-start | bytes 159752 | tf_op jit(solution)/shard_map/ppermute | solution.py:477
  16.7 6.9 %collective-permute-start.5 = (bf16[208,128]{1,0:T(8,128)(2,1)S(1)}, bf16[208,128]{1,0:T(8,128)(2,1)S(1)}, u32[]{:S(2)}, u32[]{:S(2)}) collective-permute-start(bf16[208,128]{1,0:T(8,128)(2,1)S(1)} %get-tuple-element.49), channel_id=1, source_target_pairs={{0,1},{1,0},{2,3},{3,2},{4,5},{5,4},{6,7},{7,6},{8,9},{9,8},{10,11... | collective-permute-start | bytes 159752 | tf_op jit(solution)/shard_map/ppermute | solution.py:476

commit v9 on v8

--- a/solution.py
+++ b/solution.py
@@ -398,19 +398,21 @@
     )(*arrays)
 
 
-def edge_kernel(rows_ref, fine_ref, rim_ref, edge_emb_ref, edge_ctx_ref, out_ref, patch, final, sent):
-    patch[...] = fine_ref[...]
+def edge_kernel(rows_ref, fine_ref, rim_ref, edge_emb_ref, edge_ctx_ref, out_ref, field, final, sent):
     given = lax.axis_index("gx") == 4
-    for k, x in enumerate((0, 30)):
-        for z in range(2):
+    copies = []
+    for z in range(2):
+        half = pl.ds(512 * z, 512)
+        field[half, :] = fine_ref[half, :]
+        for k, x in enumerate((0, 30)):
             wide = rim_ref[pl.ds(32 * k + 16 * z, 16), :]
             if k == 0:
                 wide = jnp.where(given, rows_ref[pl.ds(64 * 3 + 32 + 16 * z, 16), :].astype(F32), wide)
-            patch[pl.ds(512 * z + x, 16, stride=32), :] = wide
-            patch[pl.ds(512 * z + x + 1, 16, stride=32), :] = pltpu.roll(wide, 64, 1)
-    final[...] = patch[...][:, :64].astype(BF)
-    copy = pltpu.make_async_copy(final, out_ref, sent)
-    copy.start()
+            field[pl.ds(512 * z + x, 16, stride=32), :] = wide
+            field[pl.ds(512 * z + x + 1, 16, stride=32), :] = pltpu.roll(wide, 64, 1)
+        final[half, :] = field[half, :][:, :64].astype(BF)
+        copies.append(pltpu.make_async_copy(final.at[half], out_ref.at[half], sent.at[z]))
+        copies[z].start()
     rows = [rows_ref[pl.ds(64 * d + 16 * i, 16), :] for i in range(2) for d in range(8)]
     rows = jnp.concatenate(rows, axis=0).astype(F32)
     hits = jnp.where(rows[:, 97:98] == iota((256, 64), 1).astype(F32), 1.0, 0.0).astype(BF)
@@ -418,7 +420,8 @@
     scale = jnp.maximum(sums[96:97] + sums[98:99], 1.0)
     edge_ctx_ref[...] = sums[:64] / scale
     edge_emb_ref[...] = sums[64:96] / scale
-    copy.wait()
+    for copy in copies:
+        copy.wait()
 
 
 def edges(rows, fine, rim):
@@ -431,7 +434,7 @@
             jax.ShapeDtypeStruct((64, 64), F32),
             jax.ShapeDtypeStruct((1024, 64), BF),
         ],
-        scratch_shapes=[pltpu.VMEM((1024, 128), F32), pltpu.VMEM((1024, 64), BF), pltpu.SemaphoreType.DMA],
+        scratch_shapes=[pltpu.VMEM((1024, 128), F32), pltpu.VMEM((1024, 64), BF), pltpu.SemaphoreType.DMA((2,))],
         name="edges",
     )(keep(rows), keep(fine), keep(rim))
 
@@ -471,7 +474,7 @@
     rest = jnp.zeros((8, 128), BF)
     to_b = jnp.concatenate([side0, side1, jnp.where(x_even, low, high), rest], axis=0)
     to_a = jnp.concatenate([side0, side1, jnp.where(x_even, high, low), rest], axis=0)
-    to_b, to_a, w1 = lax.optimization_barrier((to_b, to_a, w1))
+    to_b, w1 = lax.optimization_barrier((to_b, w1))
     w1a, w1b, w2a = bands(w1, w2)
     xa = lax.ppermute(to_a, "gx", pairs(0, 8))
     xb = lax.ppermute(to_b, "gx", [(1, 2), (2, 1), (5, 6), (6, 5), (4, 3)])

time: 46 us -> 46 us (level)
  no operation moved by 1% of the time
where the time goes in v9:
time: 46 us; the launch traced here: 45.4 us
  blocking collectives  19.3 us (42%)
  starting transfers between devices  11.9 us (26%)
  Pallas kernels  11.2 us (24%)
  waiting for transfers between devices  1.32 us (3%)
  between operations  0.99 us (2%)
    all_to_all x1, blocking collectives, per_device(): rows = lax.all_to_all(send, 'gx', 0, 0, tiled=True)  19.3 us
    ppermute x1, starting transfers between devices, per_device(): xa = lax.ppermute(to_a, 'gx', pairs(0, 8))  4.19 us
    pallas_call x2, Pallas kernels, faces(): pl.pallas_call(functools.partial(face_kernel, half), in_specs=[pl.BlockSp...  3.82 us
    ppermute x1, starting transfers between devices, per_device(): yb = lax.ppermute(to_b, 'gy', pairs(1, 4))  3.73 us
    pallas_call x1, Pallas kernels, pool(): pl.pallas_call(pool_kernel, in_specs=[pl.BlockSpec(memory_space=pl.ANY)],...  2.41 us
    pallas_call x1, Pallas kernels, inner(): pl.pallas_call(inner_kernel, in_specs=[pl.BlockSpec(memory_space=pltpu.VM...  2.14 us
    ppermute x1, starting transfers between devices, per_device(): zb = lax.ppermute(own, 'gz', pairs(1, 8))  2.11 us
    pallas_call x1, Pallas kernels, edges(): pl.pallas_call(edge_kernel, in_specs=[pl.BlockSpec(memory_space=pltpu.VME...  1.54 us
  transfers between devices with their start and end apart: 6, of which 2 were waited for; matrix products, arithmetic and copies ran while one was open for 1% of the time, Pallas kernels for 14%

profile of v9, /device:TPU:40, one launch (start us, length us, event | category | flops | bytes accessed | tf_op | source)
XLA Modules:
  0.0 45.4 jit_solution(4464870415478677172)
XLA Ops:
  0.6 0.0 copy-start.3
  0.6 0.0 copy-start
  0.7 2.4 %pool.1 = (bf16[256,128]{1,0:T(8,128)(2,1)S(1)}, bf16[32,256,128]{2,1,0:T(8,128)(2,1)S(1)}) custom-call(bf16[32,256,128]{2,1,0:T(8,128)(2,1)} %bitcast.56), custom_call_target="tpu_custom_call" | custom-call | flops 80000000 | bytes 2200000 | tf_op jit(solution)/shard_map/pool/pallas_call | solution.py:76
  3.1 0.1 collective-permute-start.1
  3.2 2.1 %collective-permute-start = (bf16[256,128]{1,0:T(8,128)(2,1)S(1)}, bf16[256,128]{1,0:T(8,128)(2,1)S(1)}, u32[]{:S(2)}, u32[]{:S(2)}) collective-permute-start(bf16[256,128]{1,0:T(8,128)(2,1)S(1)} %get-tuple-element.36.own_ref), channel_id=1, source_target_pairs={{32,64},{64,32},{96,128},{128,96},{160,192},{192,160},{33,65},{65,... | collective-permute-start | bytes 196616 | tf_op jit(solution)/shard_map/ppermute | solution.py:451
  5.4 0.1 pad.11.clone
  5.5 0.0 copy-done.3
  5.5 0.0 copy-done
  5.5 2.0 %faces.2 = (bf16[2,256,128]{2,1,0:T(8,128)(2,1)S(1)}, f32[296,128]{1,0:T(8,128)S(1)}, bf16[32,128]{1,0:T(8,128)(2,1)S(1)}) custom-call(bf16[32,256,128]{2,1,0:T(8,128)(2,1)S(1)} %get-tuple-element.34.emb_ref, s32[256,128]{1,0:T(8,128)S(1)} %bitcast.41, s32[1,128]{1,0:T(1,128)S(1)} %bitcast.55), custom_call_target="tpu_custom_call" | custom-call | flops 1000000 | bytes 10000 | tf_op jit(solution)/shard_map/faces/pallas_call | solution.py:177
  7.5 0.0 copy-start.4
  7.5 0.0 copy-start.5
  7.5 0.0 copy-start.1
  7.6 0.0 copy-start.2
  7.6 0.0 collective-permute-done.1.za_ref
  7.6 1.2 %collective-permute-done.zb_ref = bf16[256,128]{1,0:T(8,128)(2,1)S(1)} collective-permute-done((bf16[256,128]{1,0:T(8,128)(2,1)S(1)}, bf16[256,128]{1,0:T(8,128)(2,1)S(1)}, u32[]{:S(2)}, u32[]{:S(2)}) %collective-permute-start) | collective-permute-done | bytes 65568 | tf_op jit(solution)/shard_map/ppermute | solution.py:451
  9.0 1.1 %collective-permute-start.2 = (bf16[6,2,8,128]{3,1,0,2:T(2,128)(2,1)S(1)}, bf16[6,2,8,128]{3,1,0,2:T(2,128)(2,1)S(1)}, u32[]{:S(2)}, u32[]{:S(2)}) collective-permute-start(bf16[6,2,8,128]{3,1,0,2:T(2,128)(2,1)S(1)} %pad_maximum_fusion.3), channel_id=1, source_target_pairs={{0,8},{8,0},{16,24},{24,16},{1,9},{9,1},{17,25},{25,17},{2,10},{10... | collective-permute-start | bytes 73736 | tf_op jit(solution)/shard_map/ppermute | solution.py:464
  10.1 3.7 %collective-permute-start.3 = (bf16[6,2,8,128]{3,1,0,2:T(2,128)(2,1)S(1)}, bf16[6,2,8,128]{3,1,0,2:T(2,128)(2,1)S(1)}, u32[]{:S(2)}, u32[]{:S(2)}) collective-permute-start(bf16[6,2,8,128]{3,1,0,2:T(2,128)(2,1)S(1)} %pad_maximum_fusion.4), channel_id=1, source_target_pairs={{8,16},{16,8},{9,17},{17,9},{10,18},{18,10},{11,19},{19,11},{12,20... | collective-permute-start | bytes 73736 | tf_op jit(solution)/shard_map/ppermute | solution.py:465
  13.9 1.8 %faces.3 = (bf16[2,256,128]{2,1,0:T(8,128)(2,1)S(1)}, f32[128,128]{1,0:T(8,128)S(1)}, bf16[48,128]{1,0:T(8,128)(2,1)S(1)}) custom-call(bf16[32,256,128]{2,1,0:T(8,128)(2,1)S(1)} %get-tuple-element.34.emb_ref, s32[256,128]{1,0:T(8,128)S(1)} %bitcast.42, f32[296,128]{1,0:T(8,128)S(1)} %get-tuple-element.38.given_ref), custom_call_target="tpu_custom_call" | custom-call | flops 1000000 | bytes 10000 | tf_op jit(solution)/shard_map/faces/pallas_call | solution.py:177
  15.7 0.0 collective-permute-done.2
  15.7 0.1 collective-permute-done.3
  15.9 0.1 maximum_maximum_fusion.1
  16.1 0.7 %collective-permute-start.4 = (bf16[208,128]{1,0:T(8,128)(2,1)S(1)}, bf16[208,128]{1,0:T(8,128)(2,1)S(1)}, u32[]{:S(2)}, u32[]{:S(2)}) collective-permute-start(bf16[208,128]{1,0:T(8,128)(2,1)S(1)} %get-tuple-element.47), channel_id=1, source_target_pairs={{1,2},{2,1},{5,6},{6,5},{4,3},{9,10},{10,9},{13,14},{14,13},{12,11... | collective-permute-start | bytes 159752 | tf_op jit(solution)/shard_map/ppermute | solution.py:480
  16.7 4.2 %collective-permute-start.5 = (bf16[208,128]{1,0:T(8,128)(2,1)S(1)}, bf16[208,128]{1,0:T(8,128)(2,1)S(1)}, u32[]{:S(2)}, u32[]{:S(2)}) collective-permute-start(bf16[208,128]{1,0:T(8,128)(2,1)S(1)} %get-tuple-element.81), channel_id=1, source_target_pairs={{0,1},{1,0},{2,3},{3,2},{4,5},{5,4},{6,7},{7,6},{8,9},{9,8},{10,11... | collective-permute-start | bytes 159752 | tf_op jit(solution)/shard_map/ppermute | solution.py:479
  20.9 0.0 copy-done.4
  20.9 0.0 copy-done.5
  20.9 0.1 maximum_bitcast_fusion
  21.0 0.0 copy-done.1
  21.0 0.0 copy-done.2
  21.0 0.4 bands.1
  21.5 2.1 %inner.1 = (f32[1024,128]{1,0:T(8,128)S(1)}, f32[256,128]{1,0:T(8,128)S(1)}, f32[2,144,128]{2,1,0:T(8,128)S(1)}, f32[2,96,128]{2,1,0:T(8,128)S(1)}, bf16[256,128]{1,0:T(8,128)(2,1)S(1)}) custom-call(bf16[256,128]{1,0:T(8,128)(2,1)S(1)} %get-tuple-element.36.own_ref, bf16[256,128]{1,0:T(8,128)(2,1)S(1)} %collective-permute-done.1.za_ref, ...), custom_call_target="tpu_custom_call" | custom-call | flops 1000000 | bytes 10000 | tf_op jit(solution)/shard_map/inner/pallas_call | solution.py:295
  23.6 0.0 collective-permute-done.4.xb_ref
  23.6 0.0 collective-permute-done.5.xa_ref
  23.6 0.9 %outer.1 = (f32[64,128]{1,0:T(8,128)S(1)}, bf16[512,128]{1,0:T(8,128)(2,1)S(1)}) custom-call(bf16[208,128]{1,0:T(8,128)(2,1)S(1)} %collective-permute-done.4.xb_ref, bf16[208,128]{1,0:T(8,128)(2,1)S(1)} %collective-permute-done.5.xa_ref, f32[2,144,128]{2,1,0:T(8,128)S(1)} %get-tuple-element.54.ends_ref, f32[2,96,128]{2,1,0:T(8,128)S(1)} %get-tuple-element.55.near_ref, ...), custom_call_target="tpu_custom_call" | custom-call | flops 200000000 | bytes 3000000 | tf_op jit(solution)/shard_map/outer/pallas_call | solution.py:389
  24.6 19.3 %all_to_all.11 = bf16[8,64,128]{2,1,0:T(8,128)(2,1)S(1)} all-to-all(bf16[8,64,128]{2,1,0:T(8,128)(2,1)S(1)} %bitcast.52), channel_id=1, replica_groups=mesh['gz'=8,'gy'=4,'gx'=8] {'gx'}, dimensions={0} | all-to-all | bytes 262144 | tf_op jit(solution)/shard_map/all_to_all | solution.py:490
  43.8 1.5 %edges.1 = (f32[32,64]{1,0:T(8,128)}, f32[64,64]{1,0:T(8,128)}, bf16[1024,64]{1,0:T(8,128)(2,1)}) custom-call(bf16[512,128]{1,0:T(8,128)(2,1)S(1)} %bitcast.43, f32[1024,128]{1,0:T(8,128)S(1)} %get-tuple-element.60.fine_ref, f32[64,128]{1,0:T(8,128)S(1)} %get-tuple-element.61.rim_ref), custom_call_target="tpu_custom_call" | custom-call | tf_op jit(solution)/shard_map/edges/pallas_call | solution.py:428
  (25 shorter events, 0.4 us)
Async XLA Ops:
  0.6 4.9 %copy-start.3 = (s32[128]{0:T(128)S(1)}, s32[128]{0:T(128)}, u32[]{:S(2)}) copy-start(s32[128]{0:T(128)} %param.9) | copy-start | bytes 1540
  0.6 4.8 %copy-start = (s32[4,64,128]{2,1,0:T(8,128)S(1)}, s32[4,64,128]{2,1,0:T(8,128)}, u32[]{:S(2)}) copy-start(s32[4,64,128]{2,1,0:T(8,128)} %param.8) | copy-start | bytes 393220
  3.1 4.5 %collective-permute-start.1 = (bf16[256,128]{1,0:T(8,128)(2,1)S(1)}, bf16[256,128]{1,0:T(8,128)(2,1)S(1)}, u32[]{:S(2)}, u32[]{:S(2)}) collective-permute-start(bf16[256,128]{1,0:T(8,128)(2,1)S(1)} %get-tuple-element.36.own_ref), channel_id=1, source_target_pairs={{0,32},{32,0},{64,96},{96,64},{128,160},{160,128},{192,224},{224,1... | collective-permute-start | bytes 196616 | tf_op jit(solution)/shard_map/ppermute | solution.py:452
  3.2 5.6 %collective-permute-start = (bf16[256,128]{1,0:T(8,128)(2,1)S(1)}, bf16[256,128]{1,0:T(8,128)(2,1)S(1)}, u32[]{:S(2)}, u32[]{:S(2)}) collective-permute-start(bf16[256,128]{1,0:T(8,128)(2,1)S(1)} %get-tuple-element.36.own_ref), channel_id=1, source_target_pairs={{32,64},{64,32},{96,128},{128,96},{160,192},{192,160},{33,65},{65,... | collective-permute-start | bytes 196616 | tf_op jit(solution)/shard_map/ppermute | solution.py:451
  7.5 13.4 %copy-start.4 = (f32[64]{0:T(128)S(1)}, f32[64]{0:T(128)}, u32[]{:S(2)}) copy-start(f32[64]{0:T(128)} %param.11) | copy-start | bytes 772
  7.5 13.4 %copy-start.5 = (f32[64]{0:T(128)S(1)}, f32[64]{0:T(128)}, u32[]{:S(2)}) copy-start(f32[64]{0:T(128)} %param.13) | copy-start | bytes 772
  7.5 13.5 %copy-start.1 = (bf16[3,3,3,64,64]{4,3,2,1,0:T(8,128)(2,1)S(1)}, bf16[3,3,3,64,64]{4,3,2,1,0:T(8,128)(2,1)}, u32[]{:S(2)}) copy-start(bf16[3,3,3,64,64]{4,3,2,1,0:T(8,128)(2,1)} %param.12) | copy-start | bytes 663556
  7.6 13.5 %copy-start.2 = (bf16[3,3,3,64,32]{3,4,2,1,0:T(8,128)(2,1)S(1)}, bf16[3,3,3,64,32]{3,4,2,1,0:T(8,128)(2,1)}, u32[]{:S(2)}) copy-start(bf16[3,3,3,64,32]{3,4,2,1,0:T(8,128)(2,1)} %param.10) | copy-start | bytes 331780
  9.0 6.7 %collective-permute-start.2 = (bf16[6,2,8,128]{3,1,0,2:T(2,128)(2,1)S(1)}, bf16[6,2,8,128]{3,1,0,2:T(2,128)(2,1)S(1)}, u32[]{:S(2)}, u32[]{:S(2)}) collective-permute-start(bf16[6,2,8,128]{3,1,0,2:T(2,128)(2,1)S(1)} %pad_maximum_fusion.3), channel_id=1, source_target_pairs={{0,8},{8,0},{16,24},{24,16},{1,9},{9,1},{17,25},{25,17},{2,10},{10... | collective-permute-start | bytes 73736 | tf_op jit(solution)/shard_map/ppermute | solution.py:464
  10.1 5.7 %collective-permute-start.3 = (bf16[6,2,8,128]{3,1,0,2:T(2,128)(2,1)S(1)}, bf16[6,2,8,128]{3,1,0,2:T(2,128)(2,1)S(1)}, u32[]{:S(2)}, u32[]{:S(2)}) collective-permute-start(bf16[6,2,8,128]{3,1,0,2:T(2,128)(2,1)S(1)} %pad_maximum_fusion.4), channel_id=1, source_target_pairs={{8,16},{16,8},{9,17},{17,9},{10,18},{18,10},{11,19},{19,11},{12,20... | collective-permute-start | bytes 73736 | tf_op jit(solution)/shard_map/ppermute | solution.py:465
  16.1 7.6 %collective-permute-start.4 = (bf16[208,128]{1,0:T(8,128)(2,1)S(1)}, bf16[208,128]{1,0:T(8,128)(2,1)S(1)}, u32[]{:S(2)}, u32[]{:S(2)}) collective-permute-start(bf16[208,128]{1,0:T(8,128)(2,1)S(1)} %get-tuple-element.47), channel_id=1, source_target_pairs={{1,2},{2,1},{5,6},{6,5},{4,3},{9,10},{10,9},{13,14},{14,13},{12,11... | collective-permute-start | bytes 159752 | tf_op jit(solution)/shard_map/ppermute | solution.py:480
  16.7 6.9 %collective-permute-start.5 = (bf16[208,128]{1,0:T(8,128)(2,1)S(1)}, bf16[208,128]{1,0:T(8,128)(2,1)S(1)}, u32[]{:S(2)}, u32[]{:S(2)}) collective-permute-start(bf16[208,128]{1,0:T(8,128)(2,1)S(1)} %get-tuple-element.81), channel_id=1, source_target_pairs={{0,1},{1,0},{2,3},{3,2},{4,5},{5,4},{6,7},{7,6},{8,9},{9,8},{10,11... | collective-permute-start | bytes 159752 | tf_op jit(solution)/shard_map/ppermute | solution.py:479

commit v10 on v8

--- a/solution.py
+++ b/solution.py
@@ -449,7 +449,7 @@
     za = lax.ppermute(own, "gz", pairs(0, 8))
     cnt0, half, side0 = faces(0, voxels, slot, face_edge.reshape(1, 128))
     w1, w2 = jnp.swapaxes(conv1_w, 3, 4).reshape(27, 32, 64), conv2_w.reshape(27, 64, 64)
-    zb, za, half = lax.optimization_barrier((zb, za, half))
+    zb, za, half, w1 = lax.optimization_barrier((zb, za, half, w1))
     planes = [a.reshape(2, 16, 8, 128) for a in (za, own, zb)]
     y_even, x_even = (gy & 1) == 0, (gx & 1) == 0
 
@@ -461,7 +461,8 @@
     ya = lax.ppermute(to_a, "gy", pairs(0, 4))
     yb = lax.ppermute(to_b, "gy", pairs(1, 4))
     cnt1, face, side1 = faces(1, voxels, slot, half)
-    ya, yb, face = lax.optimization_barrier((ya, yb, face))
+    w1a, w1b, w2a = bands(w1, w2)
+    ya, yb, face, w1a = lax.optimization_barrier((ya, yb, face, w1a))
 
     def x_edge(g):
         mid = jnp.concatenate([a[:, :, g] for a in planes], axis=0)
@@ -471,8 +472,7 @@
     rest = jnp.zeros((8, 128), BF)
     to_b = jnp.concatenate([side0, side1, jnp.where(x_even, low, high), rest], axis=0)
     to_a = jnp.concatenate([side0, side1, jnp.where(x_even, high, low), rest], axis=0)
-    to_b, to_a, w1 = lax.optimization_barrier((to_b, to_a, w1))
-    w1a, w1b, w2a = bands(w1, w2)
+    to_b, to_a = lax.optimization_barrier((to_b, to_a))
     xa = lax.ppermute(to_a, "gx", pairs(0, 8))
     xb = lax.ppermute(to_b, "gx", [(1, 2), (2, 1), (5, 6), (6, 5), (4, 3)])
     twice = lambda b: jnp.concatenate([b, b]).reshape(1, 128)

time: 46 us -> 46.1 us (level)
  blocking collectives: 19.3 us -> 19.8 us
    all_to_all x1, blocking collectives: 19.3 us -> 19.8 us  [per_device(): rows = lax.all_to_all(send, 'gx', 0, 0, tiled=True)]
  transfers between devices with their start and end apart: 6 -> 6, of which waited for: 2 -> 1; matrix products, arithmetic and copies ran while one was open for 1% -> 1% of each run, Pallas kernels for 14% -> 14%
where the time goes in v10:
time: 46.1 us; the launch traced here: 45.8 us
  blocking collectives  19.8 us (43%)
  starting transfers between devices  12 us (26%)
  Pallas kernels  11.2 us (24%)
  waiting for transfers between devices  1.19 us (3%)
  between operations  1 us (2%)
    all_to_all x1, blocking collectives, per_device(): rows = lax.all_to_all(send, 'gx', 0, 0, tiled=True)  19.8 us
    ppermute x1, starting transfers between devices, per_device(): xa = lax.ppermute(to_a, 'gx', pairs(0, 8))  4.31 us
    pallas_call x2, Pallas kernels, faces(): pl.pallas_call(functools.partial(face_kernel, half), in_specs=[pl.BlockSp...  3.82 us
    ppermute x1, starting transfers between devices, per_device(): yb = lax.ppermute(to_b, 'gy', pairs(1, 4))  3.76 us
    pallas_call x1, Pallas kernels, pool(): pl.pallas_call(pool_kernel, in_specs=[pl.BlockSpec(memory_space=pl.ANY)],...  2.41 us
    ppermute x1, starting transfers between devices, per_device(): zb = lax.ppermute(own, 'gz', pairs(1, 8))  2.11 us
    pallas_call x1, Pallas kernels, inner(): pl.pallas_call(inner_kernel, in_specs=[pl.BlockSpec(memory_space=pltpu.VM...  2.1 us
    pallas_call x1, Pallas kernels, edges(): pl.pallas_call(edge_kernel, in_specs=[pl.BlockSpec(memory_space=pltpu.VME...  1.58 us
  transfers between devices with their start and end apart: 6, of which 1 were waited for; matrix products, arithmetic and copies ran while one was open for 1% of the time, Pallas kernels for 14%

profile of v10, /device:TPU:40, one launch (start us, length us, event | category | flops | bytes accessed | tf_op | source)
XLA Modules:
  0.0 45.8 jit_solution(15861889291935079552)
XLA Ops:
  0.6 0.0 copy-start.3
  0.6 0.0 copy-start
  0.7 2.4 %pool.1 = (bf16[256,128]{1,0:T(8,128)(2,1)S(1)}, bf16[32,256,128]{2,1,0:T(8,128)(2,1)S(1)}) custom-call(bf16[32,256,128]{2,1,0:T(8,128)(2,1)} %bitcast.56), custom_call_target="tpu_custom_call" | custom-call | flops 80000000 | bytes 2200000 | tf_op jit(solution)/shard_map/pool/pallas_call | solution.py:76
  3.1 0.1 collective-permute-start.1
  3.2 2.1 %collective-permute-start = (bf16[256,128]{1,0:T(8,128)(2,1)S(1)}, bf16[256,128]{1,0:T(8,128)(2,1)S(1)}, u32[]{:S(2)}, u32[]{:S(2)}) collective-permute-start(bf16[256,128]{1,0:T(8,128)(2,1)S(1)} %get-tuple-element.38.own_ref), channel_id=1, source_target_pairs={{32,64},{64,32},{96,128},{128,96},{160,192},{192,160},{33,65},{65,... | collective-permute-start | bytes 196616 | tf_op jit(solution)/shard_map/ppermute | solution.py:448
  5.4 0.1 pad.11.clone
  5.5 0.0 copy-done.3
  5.5 0.0 copy-done
  5.5 0.0 copy-start.1
  5.5 0.0 copy-start.2
  5.5 2.0 %faces.2 = (bf16[2,256,128]{2,1,0:T(8,128)(2,1)S(1)}, f32[296,128]{1,0:T(8,128)S(1)}, bf16[32,128]{1,0:T(8,128)(2,1)S(1)}) custom-call(bf16[32,256,128]{2,1,0:T(8,128)(2,1)S(1)} %get-tuple-element.36.emb_ref, s32[256,128]{1,0:T(8,128)S(1)} %bitcast.41, s32[1,128]{1,0:T(1,128)S(1)} %bitcast.55), custom_call_target="tpu_custom_call" | custom-call | flops 1000000 | bytes 10000 | tf_op jit(solution)/shard_map/faces/pallas_call | solution.py:177
  7.5 0.0 copy-start.4
  7.5 0.0 copy-start.5
  7.6 0.0 collective-permute-done.1.za_ref
  7.6 1.2 %collective-permute-done.zb_ref = bf16[256,128]{1,0:T(8,128)(2,1)S(1)} collective-permute-done((bf16[256,128]{1,0:T(8,128)(2,1)S(1)}, bf16[256,128]{1,0:T(8,128)(2,1)S(1)}, u32[]{:S(2)}, u32[]{:S(2)}) %collective-permute-start) | collective-permute-done | bytes 65568 | tf_op jit(solution)/shard_map/ppermute | solution.py:448
  9.0 1.1 %collective-permute-start.2 = (bf16[6,2,8,128]{3,1,0,2:T(2,128)(2,1)S(1)}, bf16[6,2,8,128]{3,1,0,2:T(2,128)(2,1)S(1)}, u32[]{:S(2)}, u32[]{:S(2)}) collective-permute-start(bf16[6,2,8,128]{3,1,0,2:T(2,128)(2,1)S(1)} %pad_maximum_fusion.3), channel_id=1, source_target_pairs={{0,8},{8,0},{16,24},{24,16},{1,9},{9,1},{17,25},{25,17},{2,10},{10... | collective-permute-start | bytes 73736 | tf_op jit(solution)/shard_map/ppermute | solution.py:461
  10.1 3.8 %collective-permute-start.3 = (bf16[6,2,8,128]{3,1,0,2:T(2,128)(2,1)S(1)}, bf16[6,2,8,128]{3,1,0,2:T(2,128)(2,1)S(1)}, u32[]{:S(2)}, u32[]{:S(2)}) collective-permute-start(bf16[6,2,8,128]{3,1,0,2:T(2,128)(2,1)S(1)} %pad_maximum_fusion.4), channel_id=1, source_target_pairs={{8,16},{16,8},{9,17},{17,9},{10,18},{18,10},{11,19},{19,11},{12,20... | collective-permute-start | bytes 73736 | tf_op jit(solution)/shard_map/ppermute | solution.py:462
  13.9 1.8 %faces.3 = (bf16[2,256,128]{2,1,0:T(8,128)(2,1)S(1)}, f32[128,128]{1,0:T(8,128)S(1)}, bf16[48,128]{1,0:T(8,128)(2,1)S(1)}) custom-call(bf16[32,256,128]{2,1,0:T(8,128)(2,1)S(1)} %get-tuple-element.36.emb_ref, s32[256,128]{1,0:T(8,128)S(1)} %bitcast.42, f32[296,128]{1,0:T(8,128)S(1)} %get-tuple-element.40.given_ref), custom_call_target="tpu_custom_call" | custom-call | flops 1000000 | bytes 10000 | tf_op jit(solution)/shard_map/faces/pallas_call | solution.py:177
  15.7 0.0 copy-done.1
  15.7 0.0 copy-done.2
  15.7 0.4 bands.1
  16.1 0.0 collective-permute-done.2
  16.1 0.0 collective-permute-done.3
  16.3 0.1 maximum_maximum_fusion.1
  16.4 0.7 %collective-permute-start.4 = (bf16[208,128]{1,0:T(8,128)(2,1)S(1)}, bf16[208,128]{1,0:T(8,128)(2,1)S(1)}, u32[]{:S(2)}, u32[]{:S(2)}) collective-permute-start(bf16[208,128]{1,0:T(8,128)(2,1)S(1)} %get-tuple-element.51), channel_id=1, source_target_pairs={{1,2},{2,1},{5,6},{6,5},{4,3},{9,10},{10,9},{13,14},{14,13},{12,11... | collective-permute-start | bytes 159752 | tf_op jit(solution)/shard_map/ppermute | solution.py:477
  17.1 4.3 %collective-permute-start.5 = (bf16[208,128]{1,0:T(8,128)(2,1)S(1)}, bf16[208,128]{1,0:T(8,128)(2,1)S(1)}, u32[]{:S(2)}, u32[]{:S(2)}) collective-permute-start(bf16[208,128]{1,0:T(8,128)(2,1)S(1)} %get-tuple-element.52), channel_id=1, source_target_pairs={{0,1},{1,0},{2,3},{3,2},{4,5},{5,4},{6,7},{7,6},{8,9},{9,8},{10,11... | collective-permute-start | bytes 159752 | tf_op jit(solution)/shard_map/ppermute | solution.py:476
  21.4 0.0 copy-done.4
  21.4 0.0 copy-done.5
  21.4 0.1 maximum_bitcast_fusion
  21.5 2.1 %inner.1 = (f32[1024,128]{1,0:T(8,128)S(1)}, f32[256,128]{1,0:T(8,128)S(1)}, f32[2,144,128]{2,1,0:T(8,128)S(1)}, f32[2,96,128]{2,1,0:T(8,128)S(1)}, bf16[256,128]{1,0:T(8,128)(2,1)S(1)}) custom-call(bf16[256,128]{1,0:T(8,128)(2,1)S(1)} %get-tuple-element.38.own_ref, bf16[256,128]{1,0:T(8,128)(2,1)S(1)} %collective-permute-done.1.za_ref, ...), custom_call_target="tpu_custom_call" | custom-call | flops 1000000 | bytes 10000 | tf_op jit(solution)/shard_map/inner/pallas_call | solution.py:295
  23.6 0.0 collective-permute-done.4.xb_ref
  23.6 0.0 collective-permute-done.5.xa_ref
  23.6 0.9 %outer.1 = (f32[64,128]{1,0:T(8,128)S(1)}, bf16[512,128]{1,0:T(8,128)(2,1)S(1)}) custom-call(bf16[208,128]{1,0:T(8,128)(2,1)S(1)} %collective-permute-done.4.xb_ref, bf16[208,128]{1,0:T(8,128)(2,1)S(1)} %collective-permute-done.5.xa_ref, f32[2,144,128]{2,1,0:T(8,128)S(1)} %get-tuple-element.58.ends_ref, f32[2,96,128]{2,1,0:T(8,128)S(1)} %get-tuple-element.59.near_ref, ...), custom_call_target="tpu_custom_call" | custom-call | flops 200000000 | bytes 3000000 | tf_op jit(solution)/shard_map/outer/pallas_call | solution.py:389
  24.5 19.8 %all_to_all.11 = bf16[8,64,128]{2,1,0:T(8,128)(2,1)S(1)} all-to-all(bf16[8,64,128]{2,1,0:T(8,128)(2,1)S(1)} %bitcast.52), channel_id=1, replica_groups=mesh['gz'=8,'gy'=4,'gx'=8] {'gx'}, dimensions={0} | all-to-all | bytes 262144 | tf_op jit(solution)/shard_map/all_to_all | solution.py:487
  44.3 1.6 %edges.1 = (f32[32,64]{1,0:T(8,128)}, f32[64,64]{1,0:T(8,128)}, bf16[1024,64]{1,0:T(8,128)(2,1)}) custom-call(bf16[512,128]{1,0:T(8,128)(2,1)S(1)} %bitcast.43, f32[1024,128]{1,0:T(8,128)S(1)} %get-tuple-element.64.fine_ref, f32[64,128]{1,0:T(8,128)S(1)} %get-tuple-element.65.rim_ref), custom_call_target="tpu_custom_call" | custom-call | tf_op jit(solution)/shard_map/edges/pallas_call | solution.py:425
  (25 shorter events, 0.4 us)
Async XLA Ops:
  0.6 4.9 %copy-start.3 = (s32[128]{0:T(128)S(1)}, s32[128]{0:T(128)}, u32[]{:S(2)}) copy-start(s32[128]{0:T(128)} %param.9) | copy-start | bytes 1540
  0.6 4.8 %copy-start = (s32[4,64,128]{2,1,0:T(8,128)S(1)}, s32[4,64,128]{2,1,0:T(8,128)}, u32[]{:S(2)}) copy-start(s32[4,64,128]{2,1,0:T(8,128)} %param.8) | copy-start | bytes 393220
  3.1 4.5 %collective-permute-start.1 = (bf16[256,128]{1,0:T(8,128)(2,1)S(1)}, bf16[256,128]{1,0:T(8,128)(2,1)S(1)}, u32[]{:S(2)}, u32[]{:S(2)}) collective-permute-start(bf16[256,128]{1,0:T(8,128)(2,1)S(1)} %get-tuple-element.38.own_ref), channel_id=1, source_target_pairs={{0,32},{32,0},{64,96},{96,64},{128,160},{160,128},{192,224},{224,1... | collective-permute-start | bytes 196616 | tf_op jit(solution)/shard_map/ppermute | solution.py:449
  3.2 5.6 %collective-permute-start = (bf16[256,128]{1,0:T(8,128)(2,1)S(1)}, bf16[256,128]{1,0:T(8,128)(2,1)S(1)}, u32[]{:S(2)}, u32[]{:S(2)}) collective-permute-start(bf16[256,128]{1,0:T(8,128)(2,1)S(1)} %get-tuple-element.38.own_ref), channel_id=1, source_target_pairs={{32,64},{64,32},{96,128},{128,96},{160,192},{192,160},{33,65},{65,... | collective-permute-start | bytes 196616 | tf_op jit(solution)/shard_map/ppermute | solution.py:448
  5.5 10.2 %copy-start.1 = (bf16[3,3,3,64,64]{4,3,2,1,0:T(8,128)(2,1)S(1)}, bf16[3,3,3,64,64]{4,3,2,1,0:T(8,128)(2,1)}, u32[]{:S(2)}) copy-start(bf16[3,3,3,64,64]{4,3,2,1,0:T(8,128)(2,1)} %param.12) | copy-start | bytes 663556
  5.5 10.2 %copy-start.2 = (bf16[3,3,3,64,32]{3,4,2,1,0:T(8,128)(2,1)S(1)}, bf16[3,3,3,64,32]{3,4,2,1,0:T(8,128)(2,1)}, u32[]{:S(2)}) copy-start(bf16[3,3,3,64,32]{3,4,2,1,0:T(8,128)(2,1)} %param.10) | copy-start | bytes 331780
  7.5 13.9 %copy-start.4 = (f32[64]{0:T(128)S(1)}, f32[64]{0:T(128)}, u32[]{:S(2)}) copy-start(f32[64]{0:T(128)} %param.11) | copy-start | bytes 772
  7.5 13.8 %copy-start.5 = (f32[64]{0:T(128)S(1)}, f32[64]{0:T(128)}, u32[]{:S(2)}) copy-start(f32[64]{0:T(128)} %param.13) | copy-start | bytes 772
  9.0 7.1 %collective-permute-start.2 = (bf16[6,2,8,128]{3,1,0,2:T(2,128)(2,1)S(1)}, bf16[6,2,8,128]{3,1,0,2:T(2,128)(2,1)S(1)}, u32[]{:S(2)}, u32[]{:S(2)}) collective-permute-start(bf16[6,2,8,128]{3,1,0,2:T(2,128)(2,1)S(1)} %pad_maximum_fusion.3), channel_id=1, source_target_pairs={{0,8},{8,0},{16,24},{24,16},{1,9},{9,1},{17,25},{25,17},{2,10},{10... | collective-permute-start | bytes 73736 | tf_op jit(solution)/shard_map/ppermute | solution.py:461
  10.1 6.1 %collective-permute-start.3 = (bf16[6,2,8,128]{3,1,0,2:T(2,128)(2,1)S(1)}, bf16[6,2,8,128]{3,1,0,2:T(2,128)(2,1)S(1)}, u32[]{:S(2)}, u32[]{:S(2)}) collective-permute-start(bf16[6,2,8,128]{3,1,0,2:T(2,128)(2,1)S(1)} %pad_maximum_fusion.4), channel_id=1, source_target_pairs={{8,16},{16,8},{9,17},{17,9},{10,18},{18,10},{11,19},{19,11},{12,20... | collective-permute-start | bytes 73736 | tf_op jit(solution)/shard_map/ppermute | solution.py:462
  16.4 7.2 %collective-permute-start.4 = (bf16[208,128]{1,0:T(8,128)(2,1)S(1)}, bf16[208,128]{1,0:T(8,128)(2,1)S(1)}, u32[]{:S(2)}, u32[]{:S(2)}) collective-permute-start(bf16[208,128]{1,0:T(8,128)(2,1)S(1)} %get-tuple-element.51), channel_id=1, source_target_pairs={{1,2},{2,1},{5,6},{6,5},{4,3},{9,10},{10,9},{13,14},{14,13},{12,11... | collective-permute-start | bytes 159752 | tf_op jit(solution)/shard_map/ppermute | solution.py:477
  17.1 6.5 %collective-permute-start.5 = (bf16[208,128]{1,0:T(8,128)(2,1)S(1)}, bf16[208,128]{1,0:T(8,128)(2,1)S(1)}, u32[]{:S(2)}, u32[]{:S(2)}) collective-permute-start(bf16[208,128]{1,0:T(8,128)(2,1)S(1)} %get-tuple-element.52), channel_id=1, source_target_pairs={{0,1},{1,0},{2,3},{3,2},{4,5},{5,4},{6,7},{7,6},{8,9},{9,8},{10,11... | collective-permute-start | bytes 159752 | tf_op jit(solution)/shard_map/ppermute | solution.py:476
